TPU v7x, 32 devices: a whole 2x2x4 slice. The times are simulated.
32 devices in a mesh: code: 8 (over z, y), dp: 4 (over x, core).
Axes of the slice: x: 2, y: 2, z: 4, core: 2. Of those that a mesh axis runs over, the one named last changes fastest.
Arguments:
- codebook: bfloat16 [32768, 768], P(('code', 'dp')), may hold values from -6 to 6
- weight_in: bfloat16 [768, 1024], replicated, may hold values from -0.21875 to 0.21875
- bias_in: float32 [1024], replicated, may hold values from -3 to 3
- weight_out: bfloat16 [1024, 256], replicated, may hold values from -0.1875 to 0.1875
- bias_out: float32 [256], replicated, may hold values from -3 to 3
- latents: float32 [32768, 256], P(('code', 'dp')), may hold values from -6 to 6
- cotangent: float32 [32768, 256], P(('code', 'dp')), may hold values from -6 to 6
- code_owner: int32 [32768, 1], P(('code', 'dp')), may hold values from 0 to 31; in each aligned block of 1024 rows (0 to 1023, 1024 to 2047, ...) at most 64 rows name the same one
- code_row: int32 [32768], P(('code', 'dp')), may hold values from 0 to 1023
Outputs:
- latent_grad: float32 [32768, 256], P(('code', 'dp'))
- grad_weight_in: float32 [768, 1024], replicated
- grad_bias_in: float32 [1024], replicated
- grad_weight_out: float32 [1024, 256], replicated
- grad_bias_out: float32 [256], replicated
Inputs may be any that keep to these rules, and one draw needn't show every extreme that they name: In the rows of one device no owner is named by more than 64 rows, a bound that some block reaches; a latent's code is code_owner * 1024 + code_row.
All inputs are finite; a program needn't handle non-finite values.
Results may differ from a plain program's by a relative error of at most 0.0023.
Values sent between devices are 32-bit elements; how exact they have to be, the bound alone decides.
No kernel may reach another device: no remote copies, remote signals or barrier semaphores. Data moves between devices by JAX's collectives and lax.ppermute only.
A program may use at most 128 MiB of HBM per device.

v0:
```python
import functools

import jax
import jax.numpy as jnp
from jax import lax
from jax.experimental import pallas as pl
from jax.experimental.pallas import tpu as pltpu
from jax.sharding import Mesh, PartitionSpec as P

scale_gelu = 0.7978845608028654
cubic_term = 0.044715
LANES = 128
EXTRA = 8
AXES = ("outer", "inner", "chip", "core")


def gelu_parts(x):
    tangent = jnp.tanh(scale_gelu * (x + cubic_term * x * x * x))
    value = 0.5 * x * (1.0 + tangent)
    slope = 0.5 * (1.0 + tangent) + 0.5 * x * (1.0 - tangent * tangent) * scale_gelu * (
        1.0 + 3.0 * cubic_term * x * x
    )
    return value, slope


def split_two(x):
    high = lax.reduce_precision(x, 8, 7)
    low = (x - high).astype(jnp.bfloat16)
    return jnp.concatenate([high.astype(jnp.bfloat16), low], axis=1)


def pick(chooser, rows):
    width = rows.shape[1]
    both = jnp.dot(chooser, split_two(rows), preferred_element_type=jnp.float32)
    return both[:, :width] + both[:, width:]


def dot(a, b):
    return jnp.dot(a, b, preferred_element_type=jnp.float32)


def route_kernel(devices, capacity, owner_hbm, row_hbm, latents_hbm, cotangent_hbm,
                 out_ref, slot_ref, owner_ref, row_ref, latents_ref, cotangent_ref, parts_ref, sems):
    count, width = latents_ref.shape
    step = pl.program_id(0)
    tile = out_ref.shape[0] * capacity

    @pl.when(step == 0)
    def _():
        loads = [
            pltpu.make_async_copy(a, b, sems.at[k])
            for k, (a, b) in enumerate((
                (owner_hbm, owner_ref), (row_hbm, row_ref),
                (latents_hbm, latents_ref), (cotangent_hbm, cotangent_ref),
            ))
        ]
        for load in loads:
            load.start()
        before = (
            lax.broadcasted_iota(jnp.int32, (LANES, LANES), 0)
            < lax.broadcasted_iota(jnp.int32, (LANES, LANES), 1)
        ).astype(jnp.bfloat16)
        owner_ids = lax.broadcasted_iota(jnp.int32, (devices, LANES), 0)
        lane = lax.broadcasted_iota(jnp.int32, (LANES, LANES), 1)
        seen = jnp.zeros((devices, 1), jnp.float32)
        loads[0].wait()
        loads[1].wait()
        for start in range(0, count, LANES):
            part = pl.ds(start, LANES)
            owners = owner_ref[:, part]
            mine = (owner_ids == owners).astype(jnp.float32)
            ranks = dot(mine.astype(jnp.bfloat16), before) + seen
            rank = jnp.sum(mine * ranks, axis=0, keepdims=True)
            seen = seen + jnp.sum(mine, axis=1, keepdims=True)
            slot_ref[:, part] = owners * capacity + rank.astype(jnp.int32)
            rows = jnp.transpose(
                jnp.broadcast_to(row_ref[:, part].astype(jnp.float32), (LANES, LANES))
            )
            tall = jnp.floor(rows * (1.0 / 32.0))
            extra = jnp.where(lane == 0, tall, jnp.where(lane == 1, rows - 32.0 * tall, 0.0))
            extra = jnp.where(lane == 2, 1.0, extra)
            parts_ref[part, 2 * width :] = extra.astype(jnp.bfloat16)
        loads[2].wait()
        loads[3].wait()
        for start in range(0, count, LANES):
            part = pl.ds(start, LANES)
            value = cotangent_ref[part, :] - latents_ref[part, :]
            high = value.astype(jnp.bfloat16)
            parts_ref[part, :width] = high
            parts_ref[part, width : 2 * width] = (value - high.astype(jnp.float32)).astype(
                jnp.bfloat16
            )

    ids = lax.broadcasted_iota(jnp.int32, (tile, count), 0) + step * tile
    chooser = (ids == slot_ref[...]).astype(jnp.float32).astype(jnp.bfloat16)
    both = dot(chooser, parts_ref[...])
    value = both[:, :width] + both[:, width : 2 * width]
    turned = jnp.transpose(both[:, 2 * width :])
    wanted = 32.0 * turned[0:1] + turned[1:2] + turned[2:3] - 1.0
    lane = lax.broadcasted_iota(jnp.int32, (EXTRA, LANES), 1)
    for k in range(out_ref.shape[0]):
        own = slice(k * capacity, (k + 1) * capacity)
        for j in range(width // LANES):
            out_ref[k, j * capacity : (j + 1) * capacity, :] = value[own, j * LANES : (j + 1) * LANES]
        at = k * capacity // LANES * LANES
        row = jnp.broadcast_to(wanted[:, at : at + LANES], (EXTRA, LANES))
        shift = k * capacity - at
        if shift:
            row = pltpu.roll(row, LANES - shift, 1)
        out_ref[k, width // LANES * capacity :, :] = jnp.where(lane < capacity, row, -1.0)


def route(devices, capacity, code_owner, code_row, latents, cotangent):
    count, width = latents.shape
    per_step = max(1, 256 // capacity)
    block = width // LANES * capacity + EXTRA
    whole = lambda *shape: pl.BlockSpec(shape, lambda i: (0,) * len(shape))
    return pl.pallas_call(
        functools.partial(route_kernel, devices, capacity),
        grid=(devices // per_step,),
        in_specs=[pl.BlockSpec(memory_space=pl.ANY)] * 4,
        out_specs=[
            pl.BlockSpec((per_step, block, LANES), lambda i: (i, 0, 0)),
            whole(1, count),
        ],
        out_shape=[
            jax.ShapeDtypeStruct((devices, block, LANES), jnp.float32),
            jax.ShapeDtypeStruct((1, count), jnp.int32),
        ],
        scratch_shapes=[
            pltpu.VMEM((1, count), jnp.int32),
            pltpu.VMEM((1, count), jnp.int32),
            pltpu.VMEM((count, width), jnp.float32),
            pltpu.VMEM((count, width), jnp.float32),
            pltpu.VMEM((count, 2 * width + LANES), jnp.bfloat16),
            pltpu.SemaphoreType.DMA((4,)),
        ],
        compiler_params=pltpu.CompilerParams(vmem_limit_bytes=60 * 2**20),
        name="route",
    )(code_owner.reshape(1, count), code_row.reshape(1, count), latents, cotangent)


def place(sizes, k, j):
    _, inner, chip, _ = sizes
    if k % 2:
        return j
    return j % inner * chip + j // inner


def backward_kernel(sizes, capacity, incoming_hbm, hidden_hbm, slope_hbm, projected_hbm,
                    codebook_hbm, weight_hbm, *refs):
    outer, inner, chip, core = sizes
    devices = outer * inner * chip * core
    mine_hbm, theirs_hbm, refs = refs[:outer], refs[outer : 2 * outer], refs[2 * outer :]
    (incoming, hidden, slope, projected, codebook, weight, parts, wanted, low, grad, flat,
     in_sem, out_sem) = refs
    width = projected.shape[1]
    dim_in, rows = codebook.shape
    hidden_size = hidden.shape[0]
    length = flat.shape[2] - EXTRA
    pairs = list(zip(
        (incoming_hbm, projected_hbm, weight_hbm, slope_hbm, hidden_hbm, codebook_hbm),
        (incoming, projected, weight, slope, hidden, codebook),
    ))
    loads = [pltpu.make_async_copy(a, b, in_sem.at[k]) for k, (a, b) in enumerate(pairs)]
    loads[0].start()
    loads[0].wait()
    for load in loads[1:]:
        load.start()

    blocks = width // LANES
    for s in range(devices):
        own = pl.ds(s * capacity, capacity)
        for j in range(blocks):
            value = incoming[s, j * capacity : (j + 1) * capacity, :]
            high = value.astype(jnp.bfloat16)
            parts[own, j * LANES : (j + 1) * LANES] = high
            parts[own, width + j * LANES : width + (j + 1) * LANES] = (
                value - high.astype(jnp.float32)
            ).astype(jnp.bfloat16)
    per_row = LANES // capacity
    for t in range(devices * capacity // LANES):
        row = None
        for k in range(per_row):
            one = incoming[t * per_row + k, blocks * capacity :, :]
            if k:
                one = pltpu.roll(one, k * capacity, 1)
            row = one if row is None else jnp.maximum(row, one)
        wanted[:, t * LANES : (t + 1) * LANES] = row.astype(jnp.int32)

    loads[1].wait()
    loads[2].wait()
    loads[3].wait()
    tile = min(256, rows)
    bias_in = jnp.zeros((1, hidden_size), jnp.float32)
    bias_out = jnp.zeros((1, width), jnp.float32)
    for start in range(0, rows, tile):
        part = pl.ds(start, tile)
        ids = lax.broadcasted_iota(jnp.int32, (tile, wanted.shape[1]), 0) + start
        chooser = (ids == wanted[0:1, :]).astype(jnp.float32)
        times = jnp.sum(chooser, axis=1, keepdims=True)
        both = dot(chooser.astype(jnp.bfloat16), parts[...])
        code_grad = both[:, :width] + both[:, width:] + times * projected[part, :]
        bias_out += jnp.sum(code_grad, axis=0, keepdims=True)
        code_low = code_grad.astype(jnp.bfloat16)
        low[part, :] = code_low
        preact_grad = (dot(code_low, weight[...]) * slope[part, :]).astype(jnp.bfloat16)
        grad[part, :] = preact_grad
        bias_in += jnp.sum(preact_grad.astype(jnp.float32), axis=0, keepdims=True)


    first = lax.axis_index("outer")
    plane = lax.axis_index("inner") * chip + lax.axis_index("chip")
    me = lax.axis_index("core")
    band = hidden_size // outer
    pieces = inner * chip
    home = lax.rem(outer - first, outer)
    for k in range(outer):
        for e in range(pieces * core):
            flat[k, e, length:, :] = jnp.zeros((EXTRA, LANES), jnp.float32)
    biases = [bias_in[:, k : k + LANES] for k in range(0, hidden_size, LANES)]
    biases += [bias_out[:, k : k + LANES] for k in range(0, width, LANES)]
    for j, bias in enumerate(biases):
        flat[home, j // EXTRA, length + j % EXTRA : length + j % EXTRA + 1, :] = bias

    loads[4].wait()
    loads[5].wait()
    stores = []
    for k in range(outer - 1, -1, -1):
        o = lax.rem(first + k, outer)
        here = pl.ds(pl.multiple_of(o * band, band), band)

        def keep(row, value):
            for r in range(0, value.shape[0], length):
                flat[k, (row + r) // length, :length, :] = value[r : r + length, :]

        out = dot(codebook[...], grad[:, here])
        for j in range(band // LANES):
            keep(j * dim_in, out[:, j * LANES : (j + 1) * LANES])
        out = dot(hidden[here, :], low[...])
        for j in range(blocks):
            keep(band // LANES * dim_in + j * band, out[:, j * LANES : (j + 1) * LANES])
        for target, c in ((theirs_hbm, 1 - me), (mine_hbm, me)):
            for j in range(pieces):
                e = lax.bitwise_xor(plane, place(sizes, k, j)) * core + c
                copy = pltpu.make_async_copy(
                    flat.at[k, e], target[k].at[j], out_sem.at[len(stores)]
                )
                copy.start()
                stores.append(copy)
    for copy in stores:
        copy.wait()


def backward(sizes, capacity, incoming, hidden_t, slope, projected, codebook_t, weight_t):
    devices = incoming.shape[0]
    rows, width = projected.shape
    dim_in, hidden_size = codebook_t.shape[0], hidden_t.shape[0]
    length = (dim_in + width) * hidden_size // LANES // devices
    outer, inner, chip, _ = sizes
    piece = jax.ShapeDtypeStruct((inner * chip, length + EXTRA, LANES), jnp.float32)
    operands = (incoming, hidden_t, slope, projected, codebook_t, weight_t)
    vmem = lambda shape, dtype: pltpu.VMEM(shape, dtype)
    slots = devices * capacity
    return pl.pallas_call(
        functools.partial(backward_kernel, sizes, capacity),
        in_specs=[pl.BlockSpec(memory_space=pl.ANY)] * 6,
        out_specs=[pl.BlockSpec(memory_space=pl.ANY)] * (2 * outer),
        out_shape=[piece] * (2 * outer),
        scratch_shapes=[vmem(a.shape, a.dtype) for a in operands]
        + [
            vmem((slots, 2 * width), jnp.bfloat16),
            vmem((EXTRA, slots), jnp.int32),
            vmem((rows, width), jnp.bfloat16),
            vmem((rows, hidden_size), jnp.bfloat16),
            vmem((outer, inner * chip * 2, length + EXTRA, LANES), jnp.float32),
            pltpu.SemaphoreType.DMA((6,)),
            pltpu.SemaphoreType.DMA((devices,)),
        ],
        compiler_params=pltpu.CompilerParams(vmem_limit_bytes=56 * 2**20),
        name="backward",
    )(*operands)


def assemble_kernel(sizes, *refs):
    outer, inner, chip, core = sizes
    devices = outer * inner * chip * core
    pieces, (weight_in, weight_out, biases, sems, bias_sem) = refs[:devices], refs[devices:]
    length = pieces[0].shape[0] - EXTRA
    dim_in, hidden_size = weight_in.shape
    band = hidden_size // outer
    base = band // LANES * dim_in
    first = lax.axis_index("outer")
    plane = lax.axis_index("inner") * chip + lax.axis_index("chip")
    me = lax.axis_index("core")
    copies = []
    for n, piece in enumerate(pieces):
        c, n = divmod(n, devices // core)
        k, j = divmod(n, inner * chip)
        n += c * (devices // core)
        o = lax.rem(first + outer - k, outer)
        e = lax.bitwise_xor(plane, place(sizes, k, j)) * core + lax.bitwise_xor(me, c)
        at = e * length
        source = piece.at[pl.ds(0, length)]

        def copy_to(target, row, column):
            rows = pl.ds(pl.multiple_of(row, length), length)
            lanes = pl.ds(pl.multiple_of(column * LANES, LANES), LANES)
            return pltpu.make_async_copy(source, target.at[rows, lanes], sems.at[n])

        @pl.when(at < base)
        def _():
            column = o * (band // LANES) + lax.div(at, dim_in)
            copy_to(weight_in, lax.rem(at, dim_in), column).start()

        @pl.when(at >= base)
        def _():
            copy_to(weight_out, o * band + lax.rem(at - base, band), lax.div(at - base, band)).start()

        @pl.when((o == 0) & (e < 2))
        def _():
            copy = pltpu.make_async_copy(
                piece.at[pl.ds(length, EXTRA)], biases.at[jnp.minimum(e, 1)], bias_sem
            )
            copy.start()
            copy.wait()

        copies.append(copy_to(weight_in, 0, 0))
    for copy in copies:
        copy.wait()


def assemble(sizes, pieces, dim_in, hidden_size, width):
    hbm = pl.BlockSpec(memory_space=pl.ANY)
    return pl.pallas_call(
        functools.partial(assemble_kernel, sizes),
        in_specs=[hbm] * len(pieces),
        out_specs=[hbm] * 3,
        out_shape=[
            jax.ShapeDtypeStruct((dim_in, hidden_size), jnp.float32),
            jax.ShapeDtypeStruct((hidden_size, width), jnp.float32),
            jax.ShapeDtypeStruct((2, EXTRA, LANES), jnp.float32),
        ],
        scratch_shapes=[
            pltpu.SemaphoreType.DMA((len(pieces),)),
            pltpu.SemaphoreType.DMA,
        ],
        compiler_params=pltpu.CompilerParams(vmem_limit_bytes=4 * 2**20),
        name="assemble",
    )(*pieces)


def along(sizes, x, k):
    outer = sizes[0]
    return lax.ppermute(x, "outer", [(o, (o + k) % outer) for o in range(outer)])


def across(sizes, axis, x, j):
    size = sizes[AXES.index(axis)]
    return lax.ppermute(x, axis, [(p, p ^ j) for p in range(size)])


def sum_chunks(sizes, mine, theirs):
    outer, inner, chip, _ = sizes
    total = None
    for k in range(outer - 1, -1, -1):
        slow, fast = ("inner", "chip") if k % 2 else ("chip", "inner")
        low = sizes[AXES.index(fast)]
        arrived = across(sizes, "core", theirs[k], 1)
        part = mine[k][:low] + arrived[:low]
        for j in range(1, sizes[AXES.index(slow)]):
            here = slice(j * low, (j + 1) * low)
            part = part + across(sizes, slow, mine[k][here] + arrived[here], j)
        chunk = part[0]
        for j in range(1, low):
            chunk = chunk + across(sizes, fast, part[j], j)
        if k:
            chunk = along(sizes, chunk, k)
        total = chunk if total is None else total + chunk
    return total


def spread_chunks(sizes, total):
    outer, inner, chip, _ = sizes
    near = []
    for k in range(outer):
        slow, fast = ("inner", "chip") if k % 2 else ("chip", "inner")
        x = along(sizes, total, k) if k else total
        row = [across(sizes, fast, x, j) if j else x for j in range(sizes[AXES.index(fast)])]
        for j in range(sizes[AXES.index(slow)]):
            near += [across(sizes, slow, x, j) if j else x for x in row]
    return near


def per_device(
    sizes, codebook, weight_in, bias_in, weight_out, bias_out, latents, cotangent, code_owner, code_row
):
    outer, inner, chip, core = sizes
    devices = outer * inner * chip * core
    rows, dim_in = codebook.shape
    hidden_size = weight_in.shape[1]
    count, width = latents.shape
    capacity = max(2, 2 * count // devices)

    outgoing, slots = route(devices, capacity, code_owner, code_row, latents, cotangent)
    outgoing, bias_in = lax.optimization_barrier((outgoing, bias_in))
    incoming = lax.all_to_all(outgoing, AXES, split_axis=0, concat_axis=0, tiled=True)

    preact = dot(codebook, weight_in) + bias_in
    hidden, slope = gelu_parts(preact)
    hidden = hidden.astype(jnp.bfloat16)
    projected = dot(hidden, weight_out) + bias_out

    wanted = incoming[:, -EXTRA, :capacity].reshape(-1)
    asked = wanted[:, None] == jnp.arange(rows, dtype=jnp.float32)[None, :]
    picked = pick(asked.astype(jnp.bfloat16), projected)
    incoming, picked = lax.optimization_barrier((incoming, picked))
    answers = lax.all_to_all(
        picked.reshape(devices, capacity, width), AXES, split_axis=0, concat_axis=0, tiled=True
    ).reshape(-1, width)

    pieces = backward(
        sizes, capacity, incoming, hidden.T, slope, projected, codebook.T, weight_out.T
    )
    total = sum_chunks(sizes, list(pieces[:outer]), list(pieces[outer:]))
    near = spread_chunks(sizes, total)

    slot_ids = jnp.arange(devices * capacity, dtype=jnp.int32)
    from_slot = slots.reshape(-1, 1) == slot_ids[None, :]
    chosen = pick(from_slot.astype(jnp.bfloat16), answers)
    latent_grad = cotangent - 0.25 * (chosen - latents)
    late = len(near) - inner * chip
    near[late], latent_grad = lax.optimization_barrier((near[late], latent_grad))

    chunks = near + [across(sizes, "core", x, 1) for x in near]
    gw_in, gw_out, biases = assemble(sizes, chunks, dim_in, hidden_size, width)
    biases = biases.reshape(-1)
    gb_in, gb_out = biases[:hidden_size], biases[hidden_size : hidden_size + width]
    return (latent_grad, gw_in, gb_in, gw_out, gb_out)


def solution(mesh):
    code, data = mesh.shape["code"], mesh.shape["dp"]
    core = 2
    outer = 1
    while outer * outer < code:
        outer *= 2
    sizes = (outer, code // outer, data // core, core)
    fine = Mesh(mesh.devices.reshape(sizes), AXES)
    rows = P(AXES, None)
    return jax.shard_map(
        functools.partial(per_device, sizes),
        mesh=fine,
        in_specs=(rows, P(), P(), P(), P(), rows, rows, rows, P(AXES)),
        out_specs=(rows, P(), P(), P(), P()),
        check_vma=False,
    )
```

profile of v0, /device:TPU:0, one launch (start us, length us, event | category | flops | bytes accessed | tf_op | source)
XLA Modules:
  0.0 204.7 jit_solution(10625251454225682274)
XLA Ops:
  0.7 8.2 %route.1 = (f32[32,136,128]{2,1,0:T(8,128)}, s32[1,1024]{1,0:T(1,128)}) custom-call(s32[1,1024]{1,0:T(1,128)} %bitcast.48, s32[1,1024]{1,0:T(1,128)} %bitcast.49, f32[1024,256]{1,0:T(8,128)} %latents_hbm.1, f32[1024,256]{1,0:T(8,128)} %cotangent_hbm.1), custom_call_target="tpu_custom_call" | custom-call | tf_op jit(solution)/shard_map/route/pallas_call | solution.py:118
  8.9 7.4 %all-to-all-start = ((f32[32,136,128]{2,1,0:T(8,128)}), f32[32,136,128]{2,1,0:T(8,128)}, u32[]{:S(2)}, u32[]{:S(2)}) async-start(f32[32,136,128]{2,1,0:T(8,128)} %get-tuple-element.25), calls=%async_computation | async-start | bytes 4456448 | tf_op jit(solution)/shard_map/all_to_all | solution.py:407
  17.3 2.7 %copy.24 = bf16[1024,768]{0,1:T(8,128)(2,1)} copy(bf16[1024,768]{1,0:T(8,128)(2,1)} %param.9) | data formatting | bytes 3145728 | tf_op args[0]
  20.0 6.8 %multiply_add_fusion = (f32[1024,1024]{0,1:T(8,128)}, f32[1024,1024]{1,0:T(8,128)}) fusion(f32[1024]{0:T(1024)S(1)} %copy-done.19, bf16[1024,768]{1,0:T(8,128)(2,1)} %param.9, bf16[768,1024]{1,0:T(8,128)(2,1)S(1)} %copy-done), kind=kOutput, calls=%fused_computation.5 | convolution fusion | flops 1615855616 | bytes 11538432 | tf_op jit(solution)/shard_map/dot_general | solution.py:39
  26.8 5.4 %copy.22 = f32[1024,1024]{1,0:T(8,128)} copy(f32[1024,1024]{0,1:T(8,128)} %get-tuple-element.50) | data formatting | bytes 8388608 | tf_op jit(solution)/shard_map/add | solution.py:18
  32.2 5.3 %copy.17 = f32[1024,1024]{0,1:T(8,128)} copy(f32[1024,1024]{1,0:T(8,128)} %get-tuple-element.51) | data formatting | bytes 8388608 | tf_op jit(solution)/shard_map/add | solution.py:409
  37.5 5.4 %copy.21 = f32[1024,1024]{1,0:T(8,128)} copy(f32[1024,1024]{0,1:T(8,128)} %bitcast.44) | data formatting | bytes 8388608 | tf_op jit(solution)/shard_map/add | solution.py:409
  42.9 7.1 %fusion.37 = (f32[1024,1024]{0,1:T(8,128)}, f32[1024,1024]{0,1:T(8,128)}) fusion(f32[1024,1024]{0,1:T(8,128)} %copy.17), kind=kLoop, calls=%fused_computation.69 | loop fusion | flops 6291456 | bytes 12582912 | tf_op jit(solution)/shard_map/mul | solution.py:20
  50.0 5.3 %copy.23 = f32[1024,1024]{1,0:T(8,128)} copy(f32[1024,1024]{0,1:T(8,128)} %get-tuple-element.43) | data formatting | bytes 8388608 | tf_op jit(solution)/shard_map/mul | solution.py:20
  55.4 5.3 %copy.19 = f32[1024,1024]{1,0:T(8,128)} copy(f32[1024,1024]{0,1:T(8,128)} %get-tuple-element.44) | data formatting | bytes 8388608 | tf_op jit(solution)/shard_map/tanh | solution.py:18
  60.7 6.1 %multiply_convert_fusion.hidden_hbm = bf16[1024,1024]{1,0:T(8,128)(2,1)} fusion(f32[1024,1024]{1,0:T(8,128)} %copy.22, f32[1024,1024]{1,0:T(8,128)} %copy.21), kind=kLoop, calls=%fused_computation.13 | loop fusion | flops 5242880 | bytes 10485760 | tf_op jit(solution)/shard_map/convert_element_type | solution.py:411
  67.0 1.9 reduce-precision_convert_fusion.1
  69.5 3.6 %fusion.6.slope_hbm = f32[1024,1024]{1,0:T(8,128)} fusion(f32[1024,1024]{1,0:T(8,128)S(1)} %copy-done.8, f32[1024,1024]{1,0:T(8,128)S(1)} %copy-done.10, f32[1024,1024]{1,0:T(8,128)S(1)} %copy-done.9), kind=kLoop, calls=%fused_computation.11 | loop fusion | flops 11534336 | bytes 16777216 | tf_op jit(solution)/shard_map/add | solution.py:20
  74.1 2.4 %fusion = f32[2048,512]{1,0:T(8,128)S(1)} fusion(f32[2048]{0:T(1024)S(1)} %eq.30, bf16[1024,256]{1,0:T(8,128)(2,1)S(1)} %get-tuple-element.48, bf16[1024,256]{1,0:T(8,128)(2,1)S(1)} %get-tuple-element.47), kind=kOutput, calls=%fused_computation.2 | convolution fusion | flops 2151677952 | bytes 5251072 | tf_op jit(solution)/shard_map/dot_general | solution.py:34
  78.1 14.2 %backward.1 = (f32[4,264,128]{2,1,0:T(8,128)}, f32[4,264,128]{2,1,0:T(8,128)}, f32[4,264,128]{2,1,0:T(8,128)}, f32[4,264,128]{2,1,0:T(8,128)}, f32[4,264,128]{2,...) custom-call(f32[32,136,128]{2,1,0:T(8,128)} %all-to-all-done.incoming_hbm, ...), custom_call_target="tpu_custom_call" | custom-call | tf_op jit(solution)/shard_map/backward/pallas_call | solution.py:265
  93.1 5.9 %all-to-all-start.1 = ((f32[32,64,256]{2,1,0:T(8,128)}), f32[32,64,256]{2,1,0:T(8,128)}, u32[]{:S(2)}, u32[]{:S(2)}) async-start(f32[32,64,256]{2,1,0:T(8,128)} %bitcast.45), calls=%async_computation.1 | async-start | bytes 4194304 | tf_op jit(solution)/shard_map/all_to_all | solution.py:418
  100.2 1.7 collective-permute-start.1
  105.6 17.5 %collective-permute-done.1 = f32[2,264,128]{2,1,0:T(8,128)S(1)} collective-permute-done((f32[2,264,128]{2,1,0:T(8,128)S(1)}, f32[2,264,128]{2,1,0:T(8,128)S(1)}, u32[]{:S(2)}, u32[]{:S(2)}) %collective-permute-start.1) | collective-permute-done | bytes 270368 | tf_op jit(solution)/shard_map/ppermute | solution.py:360
  124.2 2.6 %collective-permute-start.2 = (f32[264,128]{1,0:T(8,128)S(1)}, f32[264,128]{1,0:T(8,128)S(1)}, u32[]{:S(2)}, u32[]{:S(2)}) collective-permute-start(f32[264,128]{1,0:T(8,128)S(1)} %slice_bitcast_fusion.6), channel_id=1, source_target_pairs={{0,2},{2,0},{1,3},{3,1},{4,6},{6,4},{5,7},{7,5},{8,10},{10,8},{9,1... | collective-permute-start | bytes 405512 | tf_op jit(solution)/shard_map/ppermute | solution.py:360
  129.2 3.5 %collective-permute-done.9 = f32[2,264,128]{2,1,0:T(8,128)S(1)} collective-permute-done((f32[2,264,128]{2,1,0:T(8,128)S(1)}, f32[2,264,128]{2,1,0:T(8,128)S(1)}, u32[]{:S(2)}, u32[]{:S(2)}) %collective-permute-start.9) | collective-permute-done | bytes 270368 | tf_op jit(solution)/shard_map/ppermute | solution.py:360
  132.8 1.8 collective-permute-start.10
  136.0 3.2 %collective-permute-start.3 = (f32[264,128]{1,0:T(8,128)S(1)}, f32[264,128]{1,0:T(8,128)S(1)}, u32[]{:S(2)}, u32[]{:S(2)}) collective-permute-start(f32[264,128]{1,0:T(8,128)S(1)} %fusion.32), channel_id=1, source_target_pairs={{0,24},{8,0},{16,8},{24,16},{1,25},{9,1},{17,9},{25,17},{2,26},{10... | collective-permute-start | bytes 405512 | tf_op jit(solution)/shard_map/ppermute | solution.py:355
  139.6 2.1 %collective-permute-start.11 = (f32[264,128]{1,0:T(8,128)S(1)}, f32[264,128]{1,0:T(8,128)S(1)}, u32[]{:S(2)}, u32[]{:S(2)}) collective-permute-start(f32[264,128]{1,0:T(8,128)S(1)} %fusion.30), channel_id=1, source_target_pairs={{0,8},{8,16},{16,24},{24,0},{1,9},{9,17},{17,25},{25,1},{2,10},{10... | collective-permute-start | bytes 405512 | tf_op jit(solution)/shard_map/ppermute | solution.py:355
  143.2 16.2 %collective-permute-done.7 = f32[264,128]{1,0:T(8,128)S(1)} collective-permute-done((f32[264,128]{1,0:T(8,128)S(1)}, f32[264,128]{1,0:T(8,128)S(1)}, u32[]{:S(2)}, u32[]{:S(2)}) %collective-permute-start.7) | collective-permute-done | bytes 135200 | tf_op jit(solution)/shard_map/ppermute | solution.py:355
  161.5 2.0 collective-permute-start.16
  163.4 3.8 %collective-permute-start.15 = (f32[264,128]{1,0:T(8,128)S(1)}, f32[264,128]{1,0:T(8,128)S(1)}, u32[]{:S(2)}, u32[]{:S(2)}) collective-permute-start(f32[264,128]{1,0:T(8,128)S(1)} %fusion.29.refs_0_), channel_id=1, source_target_pairs={{0,24},{8,0},{16,8},{24,16},{1,25},{9,1},{17,9},{25,17},{2,26},{10... | collective-permute-start | bytes 405512 | tf_op jit(solution)/shard_map/ppermute | solution.py:355
  167.2 3.5 %collective-permute-done.23.refs_8_ = f32[264,128]{1,0:T(8,128)S(1)} collective-permute-done((f32[264,128]{1,0:T(8,128)S(1)}, f32[264,128]{1,0:T(8,128)S(1)}, u32[]{:S(2)}, u32[]{:S(2)}) %collective-permute-start.23) | collective-permute-done | bytes 135200 | tf_op jit(solution)/shard_map/ppermute | solution.py:355
  171.7 2.0 collective-permute-start.24
  182.3 1.9 reduce-precision_convert_fusion
  188.3 2.4 %fusion.1 = f32[1024,512]{1,0:T(8,128)S(1)} fusion(s32[1024]{0:T(1024)S(1)} %bitcast.50, bf16[2048,256]{1,0:T(8,128)(2,1)S(1)} %get-tuple-element.46, bf16[2048,256]{1,0:T(8,128)(2,1)S(1)} %get-tuple-element.45), kind=kOutput, calls=%fused_computation.3 | convolution fusion | flops 2153775104 | bytes 4198400 | tf_op jit(solution)/shard_map/dot_general | solution.py:34
  194.8 2.6 %collective-permute-done.22.refs_7_ = f32[264,128]{1,0:T(8,128)S(1)} collective-permute-done((f32[264,128]{1,0:T(8,128)S(1)}, f32[264,128]{1,0:T(8,128)S(1)}, u32[]{:S(2)}, u32[]{:S(2)}) %collective-permute-start.22) | collective-permute-done | bytes 135200 | tf_op jit(solution)/shard_map/ppermute | solution.py:360
  201.3 2.3 %assemble.1 = (f32[768,1024]{1,0:T(8,128)}, f32[1024,256]{1,0:T(8,128)}, f32[2,8,128]{2,1,0:T(8,128)S(1)}) custom-call(f32[264,128]{1,0:T(8,128)S(1)} %fusion.29.refs_0_, f32[264,128]{1,0:T(8,128)S(1)} %collective-permute-done.16.refs_1_, f32[264,128]{1,0:T(8,128)S(1)} %collective-permute-done.17.refs_2_, f32[264,128]{1,0:T(8,128)S(1)} %copy-done.3, ...), custom_call_target="tpu_custom_call" | custom-call | tf_op jit(solution)/shard_map/assemble/pallas_call | solution.py:335
  (146 shorter events, 41.7 us)
Async XLA Ops:
  8.9 64.2 %all-to-all-start = ((f32[32,136,128]{2,1,0:T(8,128)}), f32[32,136,128]{2,1,0:T(8,128)}, u32[]{:S(2)}, u32[]{:S(2)}) async-start(f32[32,136,128]{2,1,0:T(8,128)} %get-tuple-element.25), calls=%async_computation | async-start | bytes 4456448 | tf_op jit(solution)/shard_map/all_to_all | solution.py:407
  92.3 6.9 %collective-permute-start = (f32[4,264,128]{2,1,0:T(8,128)}, f32[4,264,128]{2,1,0:T(8,128)}, u32[]{:S(2)}, u32[]{:S(2)}) collective-permute-start(f32[4,264,128]{2,1,0:T(8,128)} %get-tuple-element.29), channel_id=1, source_target_pairs={{0,1},{1,0},{2,3},{3,2},{4,5},{5,4},{6,7},{7,6},{8,9},{9,8},{10,11... | collective-permute-start | bytes 1622024 | tf_op jit(solution)/shard_map/ppermute | solution.py:360
  92.6 9.4 %collective-permute-start.4 = (f32[4,264,128]{2,1,0:T(8,128)}, f32[4,264,128]{2,1,0:T(8,128)}, u32[]{:S(2)}, u32[]{:S(2)}) collective-permute-start(f32[4,264,128]{2,1,0:T(8,128)} %get-tuple-element.31), channel_id=1, source_target_pairs={{0,1},{1,0},{2,3},{3,2},{4,5},{5,4},{6,7},{7,6},{8,9},{9,8},{10,11... | collective-permute-start | bytes 1622024 | tf_op jit(solution)/shard_map/ppermute | solution.py:360
  92.9 11.6 %collective-permute-start.8 = (f32[4,264,128]{2,1,0:T(8,128)}, f32[4,264,128]{2,1,0:T(8,128)S(1)}, u32[]{:S(2)}, u32[]{:S(2)}) collective-permute-start(f32[4,264,128]{2,1,0:T(8,128)} %get-tuple-element.33), channel_id=1, source_target_pairs={{0,1},{1,0},{2,3},{3,2},{4,5},{5,4},{6,7},{7,6},{8,9},{9,8},{10,11... | collective-permute-start | bytes 1622024 | tf_op jit(solution)/shard_map/ppermute | solution.py:360
  93.1 89.2 %all-to-all-start.1 = ((f32[32,64,256]{2,1,0:T(8,128)}), f32[32,64,256]{2,1,0:T(8,128)}, u32[]{:S(2)}, u32[]{:S(2)}) async-start(f32[32,64,256]{2,1,0:T(8,128)} %bitcast.45), calls=%async_computation.1 | async-start | bytes 4194304 | tf_op jit(solution)/shard_map/all_to_all | solution.py:418
  100.2 22.9 %collective-permute-start.1 = (f32[2,264,128]{2,1,0:T(8,128)S(1)}, f32[2,264,128]{2,1,0:T(8,128)S(1)}, u32[]{:S(2)}, u32[]{:S(2)}) collective-permute-start(f32[2,264,128]{2,1,0:T(8,128)S(1)} %slice_add_fusion.8), channel_id=1, source_target_pairs={{0,4},{4,0},{1,5},{5,1},{2,6},{6,2},{3,7},{7,3},{8,12},{12,8},{9,1... | collective-permute-start | bytes 811016 | tf_op jit(solution)/shard_map/ppermute | solution.py:360
  102.9 23.9 %collective-permute-start.5 = (f32[2,264,128]{2,1,0:T(8,128)S(1)}, f32[2,264,128]{2,1,0:T(8,128)S(1)}, u32[]{:S(2)}, u32[]{:S(2)}) collective-permute-start(f32[2,264,128]{2,1,0:T(8,128)S(1)} %slice_add_fusion.6), channel_id=1, source_target_pairs={{0,2},{2,0},{1,3},{3,1},{4,6},{6,4},{5,7},{7,5},{8,10},{10,8},{9,1... | collective-permute-start | bytes 811016 | tf_op jit(solution)/shard_map/ppermute | solution.py:360
  104.5 28.2 %collective-permute-start.9 = (f32[2,264,128]{2,1,0:T(8,128)S(1)}, f32[2,264,128]{2,1,0:T(8,128)S(1)}, u32[]{:S(2)}, u32[]{:S(2)}) collective-permute-start(f32[2,264,128]{2,1,0:T(8,128)S(1)} %slice_add_fusion.4), channel_id=1, source_target_pairs={{0,4},{4,0},{1,5},{5,1},{2,6},{6,2},{3,7},{7,3},{8,12},{12,8},{9,1... | collective-permute-start | bytes 811016 | tf_op jit(solution)/shard_map/ppermute | solution.py:360
  105.2 29.4 %collective-permute-start.13 = (f32[2,264,128]{2,1,0:T(8,128)S(1)}, f32[2,264,128]{2,1,0:T(8,128)S(1)}, u32[]{:S(2)}, u32[]{:S(2)}) collective-permute-start(f32[2,264,128]{2,1,0:T(8,128)S(1)} %slice_add_fusion.2), channel_id=1, source_target_pairs={{0,2},{2,0},{1,3},{3,1},{4,6},{6,4},{5,7},{7,5},{8,10},{10,8},{9,1... | collective-permute-start | bytes 811016 | tf_op jit(solution)/shard_map/ppermute | solution.py:360
  124.2 11.8 %collective-permute-start.2 = (f32[264,128]{1,0:T(8,128)S(1)}, f32[264,128]{1,0:T(8,128)S(1)}, u32[]{:S(2)}, u32[]{:S(2)}) collective-permute-start(f32[264,128]{1,0:T(8,128)S(1)} %slice_bitcast_fusion.6), channel_id=1, source_target_pairs={{0,2},{2,0},{1,3},{3,1},{4,6},{6,4},{5,7},{7,5},{8,10},{10,8},{9,1... | collective-permute-start | bytes 405512 | tf_op jit(solution)/shard_map/ppermute | solution.py:360
  127.9 11.4 %collective-permute-start.6 = (f32[264,128]{1,0:T(8,128)S(1)}, f32[264,128]{1,0:T(8,128)S(1)}, u32[]{:S(2)}, u32[]{:S(2)}) collective-permute-start(f32[264,128]{1,0:T(8,128)S(1)} %slice_bitcast_fusion.4), channel_id=1, source_target_pairs={{0,4},{4,0},{1,5},{5,1},{2,6},{6,2},{3,7},{7,3},{8,12},{12,8},{9,1... | collective-permute-start | bytes 405512 | tf_op jit(solution)/shard_map/ppermute | solution.py:360
  132.8 6.8 %collective-permute-start.10 = (f32[264,128]{1,0:T(8,128)S(1)}, f32[264,128]{1,0:T(8,128)S(1)}, u32[]{:S(2)}, u32[]{:S(2)}) collective-permute-start(f32[264,128]{1,0:T(8,128)S(1)} %slice_bitcast_fusion.2), channel_id=1, source_target_pairs={{0,2},{2,0},{1,3},{3,1},{4,6},{6,4},{5,7},{7,5},{8,10},{10,8},{9,1... | collective-permute-start | bytes 405512 | tf_op jit(solution)/shard_map/ppermute | solution.py:360
  134.7 7.0 %collective-permute-start.14 = (f32[264,128]{1,0:T(8,128)S(1)}, f32[264,128]{1,0:T(8,128)S(1)}, u32[]{:S(2)}, u32[]{:S(2)}) collective-permute-start(f32[264,128]{1,0:T(8,128)S(1)} %slice_bitcast_fusion), channel_id=1, source_target_pairs={{0,4},{4,0},{1,5},{5,1},{2,6},{6,2},{3,7},{7,3},{8,12},{12,8},{9,1... | collective-permute-start | bytes 405512 | tf_op jit(solution)/shard_map/ppermute | solution.py:360
  136.0 7.2 %collective-permute-start.3 = (f32[264,128]{1,0:T(8,128)S(1)}, f32[264,128]{1,0:T(8,128)S(1)}, u32[]{:S(2)}, u32[]{:S(2)}) collective-permute-start(f32[264,128]{1,0:T(8,128)S(1)} %fusion.32), channel_id=1, source_target_pairs={{0,24},{8,0},{16,8},{24,16},{1,25},{9,1},{17,9},{25,17},{2,26},{10... | collective-permute-start | bytes 405512 | tf_op jit(solution)/shard_map/ppermute | solution.py:355
  139.3 20.2 %collective-permute-start.7 = (f32[264,128]{1,0:T(8,128)S(1)}, f32[264,128]{1,0:T(8,128)S(1)}, u32[]{:S(2)}, u32[]{:S(2)}) collective-permute-start(f32[264,128]{1,0:T(8,128)S(1)} %fusion.31), channel_id=1, source_target_pairs={{0,16},{8,24},{16,0},{24,8},{1,17},{9,25},{17,1},{25,9},{2,18},{10... | collective-permute-start | bytes 405512 | tf_op jit(solution)/shard_map/ppermute | solution.py:355
  139.6 19.9 %collective-permute-start.11 = (f32[264,128]{1,0:T(8,128)S(1)}, f32[264,128]{1,0:T(8,128)S(1)}, u32[]{:S(2)}, u32[]{:S(2)}) collective-permute-start(f32[264,128]{1,0:T(8,128)S(1)} %fusion.30), channel_id=1, source_target_pairs={{0,8},{8,16},{16,24},{24,0},{1,9},{9,17},{17,25},{25,1},{2,10},{10... | collective-permute-start | bytes 405512 | tf_op jit(solution)/shard_map/ppermute | solution.py:355
  159.6 11.1 %collective-permute-start.23 = (f32[264,128]{1,0:T(8,128)S(1)}, f32[264,128]{1,0:T(8,128)S(1)}, u32[]{:S(2)}, u32[]{:S(2)}) collective-permute-start(f32[264,128]{1,0:T(8,128)S(1)} %fusion.29.refs_0_), channel_id=1, source_target_pairs={{0,16},{8,24},{16,0},{24,8},{1,17},{9,25},{17,1},{25,9},{2,18},{10... | collective-permute-start | bytes 405512 | tf_op jit(solution)/shard_map/ppermute | solution.py:355
  160.5 10.3 %collective-permute-start.19 = (f32[264,128]{1,0:T(8,128)S(1)}, f32[264,128]{1,0:T(8,128)S(1)}, u32[]{:S(2)}, u32[]{:S(2)}) collective-permute-start(f32[264,128]{1,0:T(8,128)S(1)} %fusion.29.refs_0_), channel_id=1, source_target_pairs={{0,8},{8,16},{16,24},{24,0},{1,9},{9,17},{17,25},{25,1},{2,10},{10... | collective-permute-start | bytes 405512 | tf_op jit(solution)/shard_map/ppermute | solution.py:355
  160.5 11.3 %collective-permute-start.17 = (f32[264,128]{1,0:T(8,128)S(1)}, f32[264,128]{1,0:T(8,128)S(1)}, u32[]{:S(2)}, u32[]{:S(2)}) collective-permute-start(f32[264,128]{1,0:T(8,128)S(1)} %fusion.29.refs_0_), channel_id=1, source_target_pairs={{0,2},{2,0},{1,3},{3,1},{4,6},{6,4},{5,7},{7,5},{8,10},{10,8},{9,1... | collective-permute-start | bytes 405512 | tf_op jit(solution)/shard_map/ppermute | solution.py:360
  161.5 12.2 %collective-permute-start.16 = (f32[264,128]{1,0:T(8,128)S(1)}, f32[264,128]{1,0:T(8,128)S(1)}, u32[]{:S(2)}, u32[]{:S(2)}) collective-permute-start(f32[264,128]{1,0:T(8,128)S(1)} %fusion.29.refs_0_), channel_id=1, source_target_pairs={{0,4},{4,0},{1,5},{5,1},{2,6},{6,2},{3,7},{7,3},{8,12},{12,8},{9,1... | collective-permute-start | bytes 405512 | tf_op jit(solution)/shard_map/ppermute | solution.py:360
  163.4 10.3 %collective-permute-start.15 = (f32[264,128]{1,0:T(8,128)S(1)}, f32[264,128]{1,0:T(8,128)S(1)}, u32[]{:S(2)}, u32[]{:S(2)}) collective-permute-start(f32[264,128]{1,0:T(8,128)S(1)} %fusion.29.refs_0_), channel_id=1, source_target_pairs={{0,24},{8,0},{16,8},{24,16},{1,25},{9,1},{17,9},{25,17},{2,26},{10... | collective-permute-start | bytes 405512 | tf_op jit(solution)/shard_map/ppermute | solution.py:355
  171.7 6.4 %collective-permute-start.24 = (f32[264,128]{1,0:T(8,128)S(1)}, f32[264,128]{1,0:T(8,128)S(1)}, u32[]{:S(2)}, u32[]{:S(2)}) collective-permute-start(f32[264,128]{1,0:T(8,128)S(1)} %collective-permute-done.23.refs_8_), channel_id=1, source_target_pairs={{0,4},{4,0},{1,5},{5,1},{2,6},{6,2},{3,7},{7,3},{8,12},{12,8},{9,1... | collective-permute-start | bytes 405512 | tf_op jit(solution)/shard_map/ppermute | solution.py:360
  173.7 6.9 %collective-permute-start.21 = (f32[264,128]{1,0:T(8,128)S(1)}, f32[264,128]{1,0:T(8,128)S(1)}, u32[]{:S(2)}, u32[]{:S(2)}) collective-permute-start(f32[264,128]{1,0:T(8,128)S(1)} %collective-permute-done.19.refs_4_), channel_id=1, source_target_pairs={{0,4},{4,0},{1,5},{5,1},{2,6},{6,2},{3,7},{7,3},{8,12},{12,8},{9,1... | collective-permute-start | bytes 405512 | tf_op jit(solution)/shard_map/ppermute | solution.py:360
  174.4 9.8 %collective-permute-start.20 = (f32[264,128]{1,0:T(8,128)S(1)}, f32[264,128]{1,0:T(8,128)S(1)}, u32[]{:S(2)}, u32[]{:S(2)}) collective-permute-start(f32[264,128]{1,0:T(8,128)S(1)} %collective-permute-done.19.refs_4_), channel_id=1, source_target_pairs={{0,2},{2,0},{1,3},{3,1},{4,6},{6,4},{5,7},{7,5},{8,10},{10,8},{9,1... | collective-permute-start | bytes 405512 | tf_op jit(solution)/shard_map/ppermute | solution.py:360
  176.7 8.6 %collective-permute-start.31 = (f32[264,128]{1,0:T(8,128)S(1)}, f32[264,128]{1,0:T(8,128)S(1)}, u32[]{:S(2)}, u32[]{:S(2)}) collective-permute-start(f32[264,128]{1,0:T(8,128)S(1)} %collective-permute-done.16.refs_1_), channel_id=1, source_target_pairs={{0,1},{1,0},{2,3},{3,2},{4,5},{5,4},{6,7},{7,6},{8,9},{9,8},{10,11... | collective-permute-start | bytes 405512 | tf_op jit(solution)/shard_map/ppermute | solution.py:360
  178.1 8.9 %collective-permute-start.18 = (f32[264,128]{1,0:T(8,128)S(1)}, f32[264,128]{1,0:T(8,128)S(1)}, u32[]{:S(2)}, u32[]{:S(2)}) collective-permute-start(f32[264,128]{1,0:T(8,128)S(1)} %collective-permute-done.16.refs_1_), channel_id=1, source_target_pairs={{0,2},{2,0},{1,3},{3,1},{4,6},{6,4},{5,7},{7,5},{8,10},{10,8},{9,1... | collective-permute-start | bytes 405512 | tf_op jit(solution)/shard_map/ppermute | solution.py:360
  180.6 6.7 %collective-permute-start.28 = (f32[264,128]{1,0:T(8,128)S(1)}, f32[264,128]{1,0:T(8,128)S(1)}, u32[]{:S(2)}, u32[]{:S(2)}) collective-permute-start(f32[264,128]{1,0:T(8,128)S(1)} %collective-permute-done.15.refs_12_), channel_id=1, source_target_pairs={{0,4},{4,0},{1,5},{5,1},{2,6},{6,2},{3,7},{7,3},{8,12},{12,8},{9,1... | collective-permute-start | bytes 405512 | tf_op jit(solution)/shard_map/ppermute | solution.py:360
  184.2 6.5 %collective-permute-start.27 = (f32[264,128]{1,0:T(8,128)S(1)}, f32[264,128]{1,0:T(8,128)S(1)}, u32[]{:S(2)}, u32[]{:S(2)}) collective-permute-start(f32[264,128]{1,0:T(8,128)S(1)} %collective-permute-done.15.refs_12_), channel_id=1, source_target_pairs={{0,2},{2,0},{1,3},{3,1},{4,6},{6,4},{5,7},{7,5},{8,10},{10,8},{9,1... | collective-permute-start | bytes 405512 | tf_op jit(solution)/shard_map/ppermute | solution.py:360
  185.3 6.9 %collective-permute-start.26 = (f32[264,128]{1,0:T(8,128)S(1)}, f32[264,128]{1,0:T(8,128)S(1)}, u32[]{:S(2)}, u32[]{:S(2)}) collective-permute-start(f32[264,128]{1,0:T(8,128)S(1)} %collective-permute-done.24.refs_9_), channel_id=1, source_target_pairs={{0,2},{2,0},{1,3},{3,1},{4,6},{6,4},{5,7},{7,5},{8,10},{10,8},{9,1... | collective-permute-start | bytes 405512 | tf_op jit(solution)/shard_map/ppermute | solution.py:360
  191.0 6.4 %collective-permute-start.22 = (f32[264,128]{1,0:T(8,128)S(1)}, f32[264,128]{1,0:T(8,128)S(1)}, u32[]{:S(2)}, u32[]{:S(2)}) collective-permute-start(f32[264,128]{1,0:T(8,128)S(1)} %collective-permute-done.20.refs_5_), channel_id=1, source_target_pairs={{0,4},{4,0},{1,5},{5,1},{2,6},{6,2},{3,7},{7,3},{8,12},{12,8},{9,1... | collective-permute-start | bytes 405512 | tf_op jit(solution)/shard_map/ppermute | solution.py:360
  192.2 7.5 %collective-permute-start.44 = (f32[264,128]{1,0:T(8,128)S(1)}, f32[264,128]{1,0:T(8,128)S(1)}, u32[]{:S(2)}, u32[]{:S(2)}) collective-permute-start(f32[264,128]{1,0:T(8,128)S(1)} %copy-done.7), channel_id=1, source_target_pairs={{0,1},{1,0},{2,3},{3,2},{4,5},{5,4},{6,7},{7,6},{8,9},{9,8},{10,11... | collective-permute-start | bytes 405512 | tf_op jit(solution)/shard_map/ppermute | solution.py:360
  192.2 7.5 %collective-permute-start.29 = (f32[264,128]{1,0:T(8,128)S(1)}, f32[264,128]{1,0:T(8,128)S(1)}, u32[]{:S(2)}, u32[]{:S(2)}) collective-permute-start(f32[264,128]{1,0:T(8,128)S(1)} %collective-permute-done.27.refs_13_), channel_id=1, source_target_pairs={{0,4},{4,0},{1,5},{5,1},{2,6},{6,2},{3,7},{7,3},{8,12},{12,8},{9,1... | collective-permute-start | bytes 405512 | tf_op jit(solution)/shard_map/ppermute | solution.py:360
  (37 other events, 280.1 us)
where the time goes:
time: 206 us; the launch traced here: 205 us
  waiting for transfers between devices  53.3 us (26%)
  starting transfers between devices  51.3 us (25%)
  local copies, waits for them, and re-layouts  35.1 us (17%)
  other arithmetic  25.9 us (13%)
  Pallas kernels  24.7 us (12%)
  matrix products  13.4 us (7%)
    ppermute x40, waiting for transfers between devices, across(): return lax.ppermute(x, axis, [(p, p ^ j) for p in range(size)])  32 us
    ppermute x40, starting transfers between devices, across(): return lax.ppermute(x, axis, [(p, p ^ j) for p in range(size)])  27.8 us
    ppermute x6, waiting for transfers between devices, along(): lax.ppermute(x, 'outer', [(o, (o + k) % outer) for o in range(outer)])  21.3 us
    pallas_call x1, Pallas kernels, backward(): pl.pallas_call(functools.partial(backward_kernel, sizes, capacity), in_sp...  14.2 us
    add x2, local copies, waits for them, and re-layouts, per_device(): preact = dot(codebook, weight_in) + bias_in  10.8 us
    ppermute x6, starting transfers between devices, along(): lax.ppermute(x, 'outer', [(o, (o + k) % outer) for o in range(outer)])  10.2 us
    dot_general x2, matrix products, dot(): return jnp.dot(a, b, preferred_element_type=jnp.float32)  8.63 us
    pallas_call x1, Pallas kernels, route(): pl.pallas_call(functools.partial(route_kernel, devices, capacity), grid=(...  8.21 us
  transfers between devices with their start and end apart: 48, of which 14 were waited for; matrix products, arithmetic and copies ran while one was open for 32% of the time, Pallas kernels for 0%

commit v1 on v0

--- a/solution.py
+++ b/solution.py
@@ -37,6 +37,132 @@
 
 def dot(a, b):
     return jnp.dot(a, b, preferred_element_type=jnp.float32)
+
+
+def forward_kernel(codebook_ref, weight_in_ref, bias_in_ref, weight_out_ref, bias_out_ref,
+                   hidden_ref, codebook_t_ref, slope_ref, projected_ref, parts_ref):
+    width = projected_ref.shape[1]
+    codebook = codebook_ref[...]
+    codebook_t_ref[...] = jnp.transpose(codebook.astype(jnp.float32)).astype(jnp.bfloat16)
+    hidden, slope = gelu_parts(dot(codebook, weight_in_ref[...]) + bias_in_ref[...])
+    slope_ref[...] = slope
+    hidden_ref[...] = jnp.transpose(hidden).astype(jnp.bfloat16)
+    projected = dot(hidden.astype(jnp.bfloat16), weight_out_ref[...]) + bias_out_ref[...]
+    projected_ref[...] = projected
+    high = projected.astype(jnp.bfloat16)
+    parts_ref[:, :width] = high
+    parts_ref[:, width:] = (projected - high.astype(jnp.float32)).astype(jnp.bfloat16)
+
+
+def forward(codebook, weight_in, bias_in, weight_out, bias_out):
+    rows, dim_in = codebook.shape
+    hidden_size, width = weight_out.shape
+    tile = min(256, rows)
+    whole = lambda *shape: pl.BlockSpec(shape, lambda i: (0, 0))
+    return pl.pallas_call(
+        forward_kernel,
+        grid=(rows // tile,),
+        in_specs=[
+            pl.BlockSpec((tile, dim_in), lambda i: (i, 0)),
+            whole(dim_in, hidden_size),
+            whole(1, hidden_size),
+            whole(hidden_size, width),
+            whole(1, width),
+        ],
+        out_specs=[
+            pl.BlockSpec((hidden_size, tile), lambda i: (0, i)),
+            pl.BlockSpec((dim_in, tile), lambda i: (0, i)),
+            pl.BlockSpec((tile, hidden_size), lambda i: (i, 0)),
+            pl.BlockSpec((tile, width), lambda i: (i, 0)),
+            pl.BlockSpec((tile, 2 * width), lambda i: (i, 0)),
+        ],
+        out_shape=[
+            jax.ShapeDtypeStruct((hidden_size, rows), jnp.bfloat16),
+            jax.ShapeDtypeStruct((dim_in, rows), jnp.bfloat16),
+            jax.ShapeDtypeStruct((rows, hidden_size), jnp.float32),
+            jax.ShapeDtypeStruct((rows, width), jnp.float32),
+            jax.ShapeDtypeStruct((rows, 2 * width), jnp.bfloat16),
+        ],
+        cost_estimate=pl.CostEstimate(
+            flops=2 * rows * hidden_size * (dim_in + width),
+            bytes_accessed=14 * rows * hidden_size,
+            transcendentals=rows * hidden_size,
+        ),
+        compiler_params=pltpu.CompilerParams(vmem_limit_bytes=60 * 2**20),
+        name="forward",
+    )(codebook, weight_in, bias_in.reshape(1, -1), weight_out, bias_out.reshape(1, -1))
+
+
+def pick_kernel(capacity, incoming_hbm, parts_ref, out_ref, wanted_ref, asked_ref, sem):
+    devices = asked_ref.shape[0]
+    rows, both = parts_ref.shape
+    width = both // 2
+    step = pl.program_id(0)
+    per_row = LANES // capacity
+
+    @pl.when(step == 0)
+    def _():
+        payload = incoming_hbm.shape[1] - EXTRA
+        load = pltpu.make_async_copy(
+            incoming_hbm.at[pl.ds(0, devices), pl.ds(payload, EXTRA)], asked_ref, sem
+        )
+        load.start()
+        load.wait()
+        for t in range(devices // per_row):
+            row = asked_ref[t * per_row]
+            for k in range(1, per_row):
+                row = jnp.maximum(row, pltpu.roll(asked_ref[t * per_row + k], k * capacity, 1))
+            wanted_ref[:, t * LANES : (t + 1) * LANES] = row
+
+    tile = out_ref.shape[0] * capacity
+    lane = lax.broadcasted_iota(jnp.int32, (LANES, LANES), 1).astype(jnp.float32)
+    for start in range(0, tile, LANES):
+        at = pl.ds(pl.multiple_of(step * tile + start, LANES), LANES)
+        column = jnp.transpose(jnp.broadcast_to(wanted_ref[0:1, at], (LANES, LANES)))
+        chooser = jnp.concatenate(
+            [
+                (column == lane + float(r)).astype(jnp.float32).astype(jnp.bfloat16)
+                for r in range(0, rows, LANES)
+            ],
+            axis=1,
+        )
+        value = dot(chooser, parts_ref[...])
+        value = value[:, :width] + value[:, width:]
+        for k in range(per_row):
+            out_ref[start // capacity + k] = value[k * capacity : (k + 1) * capacity]
+
+
+def pick_rows(capacity, incoming, parts):
+    devices = incoming.shape[0]
+    rows, both = parts.shape
+    steps = 4
+    return pl.pallas_call(
+        functools.partial(pick_kernel, capacity),
+        grid=(steps,),
+        in_specs=[
+            pl.BlockSpec(memory_space=pl.ANY),
+            pl.BlockSpec((rows, both), lambda i: (0, 0)),
+        ],
+        out_specs=[
+            pl.BlockSpec((devices // steps, capacity, both // 2), lambda i: (i, 0, 0)),
+            pl.BlockSpec((EXTRA, devices * capacity), lambda i: (0, 0)),
+        ],
+        out_shape=[
+            jax.ShapeDtypeStruct((devices, capacity, both // 2), jnp.float32),
+            jax.ShapeDtypeStruct((EXTRA, devices * capacity), jnp.float32),
+        ],
+        scratch_shapes=[
+            pltpu.VMEM((devices, EXTRA, LANES), jnp.float32),
+            pltpu.SemaphoreType.DMA,
+        ],
+        cost_estimate=pl.CostEstimate(
+            flops=2 * devices * capacity * rows * both,
+            bytes_accessed=4 * devices * capacity * both,
+            transcendentals=0,
+        ),
+        compiler_params=pltpu.CompilerParams(vmem_limit_bytes=60 * 2**20),
+        name="pick_rows",
+    )(incoming, parts)
 
 
 def route_kernel(devices, capacity, owner_hbm, row_hbm, latents_hbm, cotangent_hbm,
@@ -147,56 +273,55 @@
     return j % inner * chip + j // inner
 
 
-def backward_kernel(sizes, capacity, incoming_hbm, hidden_hbm, slope_hbm, projected_hbm,
+def backward_kernel(sizes, capacity, incoming_hbm, wanted_hbm, hidden_hbm, slope_hbm, projected_hbm,
                     codebook_hbm, weight_hbm, *refs):
     outer, inner, chip, core = sizes
     devices = outer * inner * chip * core
     mine_hbm, theirs_hbm, refs = refs[:outer], refs[outer : 2 * outer], refs[2 * outer :]
-    (incoming, hidden, slope, projected, codebook, weight, parts, wanted, low, grad, flat,
+    (incoming, wanted, hidden, slope, projected, codebook, weight, parts, low, grad, flat,
      in_sem, out_sem) = refs
     width = projected.shape[1]
     dim_in, rows = codebook.shape
     hidden_size = hidden.shape[0]
     length = flat.shape[2] - EXTRA
     pairs = list(zip(
-        (incoming_hbm, projected_hbm, weight_hbm, slope_hbm, hidden_hbm, codebook_hbm),
-        (incoming, projected, weight, slope, hidden, codebook),
+        (wanted_hbm, projected_hbm, weight_hbm, slope_hbm, hidden_hbm, codebook_hbm),
+        (wanted, projected, weight, slope, hidden, codebook),
     ))
     loads = [pltpu.make_async_copy(a, b, in_sem.at[k]) for k, (a, b) in enumerate(pairs)]
     loads[0].start()
-    loads[0].wait()
+    blocks = width // LANES
+    quarter = devices // 4
+    arrivals = []
+    for n in range(4):
+        part = pl.ds(n * quarter, quarter)
+        arrivals.append(pltpu.make_async_copy(
+            incoming_hbm.at[part, pl.ds(0, blocks * capacity)], incoming.at[part], in_sem.at[6 + n]
+        ))
+        arrivals[n].start()
     for load in loads[1:]:
         load.start()
-
-    blocks = width // LANES
-    for s in range(devices):
-        own = pl.ds(s * capacity, capacity)
-        for j in range(blocks):
-            value = incoming[s, j * capacity : (j + 1) * capacity, :]
-            high = value.astype(jnp.bfloat16)
-            parts[own, j * LANES : (j + 1) * LANES] = high
-            parts[own, width + j * LANES : width + (j + 1) * LANES] = (
-                value - high.astype(jnp.float32)
-            ).astype(jnp.bfloat16)
-    per_row = LANES // capacity
-    for t in range(devices * capacity // LANES):
-        row = None
-        for k in range(per_row):
-            one = incoming[t * per_row + k, blocks * capacity :, :]
-            if k:
-                one = pltpu.roll(one, k * capacity, 1)
-            row = one if row is None else jnp.maximum(row, one)
-        wanted[:, t * LANES : (t + 1) * LANES] = row.astype(jnp.int32)
-
-    loads[1].wait()
-    loads[2].wait()
-    loads[3].wait()
+    for n in range(4):
+        arrivals[n].wait()
+        for s in range(n * quarter, (n + 1) * quarter):
+            own = pl.ds(s * capacity, capacity)
+            for j in range(blocks):
+                value = incoming[s, j * capacity : (j + 1) * capacity, :]
+                high = value.astype(jnp.bfloat16)
+                parts[own, j * LANES : (j + 1) * LANES] = high
+                parts[own, width + j * LANES : width + (j + 1) * LANES] = (
+                    value - high.astype(jnp.float32)
+                ).astype(jnp.bfloat16)
+    for load in loads[:4]:
+        load.wait()
     tile = min(256, rows)
     bias_in = jnp.zeros((1, hidden_size), jnp.float32)
     bias_out = jnp.zeros((1, width), jnp.float32)
     for start in range(0, rows, tile):
         part = pl.ds(start, tile)
-        ids = lax.broadcasted_iota(jnp.int32, (tile, wanted.shape[1]), 0) + start
+        ids = (lax.broadcasted_iota(jnp.int32, (tile, wanted.shape[1]), 0) + start).astype(
+            jnp.float32
+        )
         chooser = (ids == wanted[0:1, :]).astype(jnp.float32)
         times = jnp.sum(chooser, axis=1, keepdims=True)
         both = dot(chooser.astype(jnp.bfloat16), parts[...])
@@ -252,32 +377,37 @@
         copy.wait()
 
 
-def backward(sizes, capacity, incoming, hidden_t, slope, projected, codebook_t, weight_t):
+def backward(sizes, capacity, incoming, wanted, hidden_t, slope, projected, codebook_t, weight_t):
     devices = incoming.shape[0]
     rows, width = projected.shape
     dim_in, hidden_size = codebook_t.shape[0], hidden_t.shape[0]
     length = (dim_in + width) * hidden_size // LANES // devices
-    outer, inner, chip, _ = sizes
+    outer, inner, chip, core = sizes
     piece = jax.ShapeDtypeStruct((inner * chip, length + EXTRA, LANES), jnp.float32)
-    operands = (incoming, hidden_t, slope, projected, codebook_t, weight_t)
+    operands = (incoming, wanted, hidden_t, slope, projected, codebook_t, weight_t)
     vmem = lambda shape, dtype: pltpu.VMEM(shape, dtype)
     slots = devices * capacity
     return pl.pallas_call(
         functools.partial(backward_kernel, sizes, capacity),
-        in_specs=[pl.BlockSpec(memory_space=pl.ANY)] * 6,
+        in_specs=[pl.BlockSpec(memory_space=pl.ANY)] * len(operands),
         out_specs=[pl.BlockSpec(memory_space=pl.ANY)] * (2 * outer),
         out_shape=[piece] * (2 * outer),
-        scratch_shapes=[vmem(a.shape, a.dtype) for a in operands]
+        scratch_shapes=[vmem((devices, incoming.shape[1] - EXTRA, LANES), jnp.float32)]
+        + [vmem(a.shape, a.dtype) for a in operands[1:]]
         + [
             vmem((slots, 2 * width), jnp.bfloat16),
-            vmem((EXTRA, slots), jnp.int32),
             vmem((rows, width), jnp.bfloat16),
             vmem((rows, hidden_size), jnp.bfloat16),
-            vmem((outer, inner * chip * 2, length + EXTRA, LANES), jnp.float32),
-            pltpu.SemaphoreType.DMA((6,)),
+            vmem((outer, inner * chip * core, length + EXTRA, LANES), jnp.float32),
+            pltpu.SemaphoreType.DMA((10,)),
             pltpu.SemaphoreType.DMA((devices,)),
         ],
-        compiler_params=pltpu.CompilerParams(vmem_limit_bytes=56 * 2**20),
+        cost_estimate=pl.CostEstimate(
+            flops=2 * rows * (slots * 2 * width + hidden_size * (2 * width + dim_in)),
+            bytes_accessed=16 * rows * hidden_size,
+            transcendentals=0,
+        ),
+        compiler_params=pltpu.CompilerParams(vmem_limit_bytes=60 * 2**20),
         name="backward",
     )(*operands)
 
@@ -406,23 +536,18 @@
     outgoing, bias_in = lax.optimization_barrier((outgoing, bias_in))
     incoming = lax.all_to_all(outgoing, AXES, split_axis=0, concat_axis=0, tiled=True)
 
-    preact = dot(codebook, weight_in) + bias_in
-    hidden, slope = gelu_parts(preact)
-    hidden = hidden.astype(jnp.bfloat16)
-    projected = dot(hidden, weight_out) + bias_out
-
-    wanted = incoming[:, -EXTRA, :capacity].reshape(-1)
-    asked = wanted[:, None] == jnp.arange(rows, dtype=jnp.float32)[None, :]
-    picked = pick(asked.astype(jnp.bfloat16), projected)
-    incoming, picked = lax.optimization_barrier((incoming, picked))
-    answers = lax.all_to_all(
-        picked.reshape(devices, capacity, width), AXES, split_axis=0, concat_axis=0, tiled=True
-    ).reshape(-1, width)
+    hidden_t, codebook_t, slope, projected, parts = forward(
+        codebook, weight_in, bias_in, weight_out, bias_out
+    )
+    picked, wanted = pick_rows(capacity, incoming, parts)
+    answers = lax.all_to_all(picked, AXES, split_axis=0, concat_axis=0, tiled=True)
 
     pieces = backward(
-        sizes, capacity, incoming, hidden.T, slope, projected, codebook.T, weight_out.T
+        sizes, capacity, incoming, wanted, hidden_t, slope, projected, codebook_t, weight_out.T
     )
     total = sum_chunks(sizes, list(pieces[:outer]), list(pieces[outer:]))
+    total, answers = lax.optimization_barrier((total, answers))
+    answers = answers.reshape(-1, width)
     near = spread_chunks(sizes, total)
 
     slot_ids = jnp.arange(devices * capacity, dtype=jnp.int32)

time: 206 us -> 197 us (0.956)
  waiting for transfers between devices: 53.3 us -> 95.3 us
  local copies, waits for them, and re-layouts: 35.1 us -> 3.61 us
  other arithmetic: 25.9 us -> 5.94 us
  Pallas kernels: 24.7 us -> 38.4 us
  matrix products: 13.4 us -> 2.37 us
    all_to_all x1, waiting for transfers between devices: 0.01 us -> 42.3 us  [per_device(): lax.all_to_all(outgoing, AXES, split_axis=0, concat_axis=0, tiled=True)]
    add x3 -> x0, local copies, waits for them, and re-layouts: 16.2 us -> none  [the longest x2 10.8 us: per_device(): preact = dot(codebook, weight_in) + bias_in]
    pallas_call x0 -> x2, Pallas kernels: none -> 15 us  [the longest x1 8.4 us: forward(): pl.pallas_call(forward_kernel, grid=(rows // tile,), in_specs=[pl.BlockSp...]
    dot_general x2 -> x0, matrix products: 8.63 us -> none  [dot(): return jnp.dot(a, b, preferred_element_type=jnp.float32)]
    mul x1 -> x0, other arithmetic: 7.1 us -> none  [gelu_parts(): tangent * tangent]
    convert_element_type x1 -> x0, other arithmetic: 6.11 us -> none  [per_device(): hidden = hidden.astype(jnp.bfloat16)]
    mul x1 -> x0, local copies, waits for them, and re-layouts: 5.35 us -> none  [gelu_parts(): tangent * tangent]
    tanh x1 -> x0, local copies, waits for them, and re-layouts: 5.34 us -> none  [gelu_parts(): tangent = jnp.tanh(scale_gelu * (x + cubic_term * x * x * x))]
  transfers between devices with their start and end apart: 48 -> 48, of which waited for: 14 -> 17; matrix products, arithmetic and copies ran while one was open for 32% -> 5% of each run, Pallas kernels for 0% -> 4%
where the time goes in v1:
time: 197 us
  waiting for transfers between devices  95.3 us (48%)
  starting transfers between devices  50.3 us (26%)
  Pallas kernels  38.4 us (19%)
  other arithmetic  5.94 us (3%)
  local copies, waits for them, and re-layouts  3.61 us (2%)
  matrix products  2.37 us (1%)
    all_to_all x1, waiting for transfers between devices, per_device(): lax.all_to_all(outgoing, AXES, split_axis=0, concat_axis=0, tiled=True)  42.3 us
    ppermute x40, waiting for transfers between devices, across(): return lax.ppermute(x, axis, [(p, p ^ j) for p in range(size)])  34.5 us
    ppermute x40, starting transfers between devices, across(): return lax.ppermute(x, axis, [(p, p ^ j) for p in range(size)])  28.8 us
    ppermute x6, waiting for transfers between devices, along(): lax.ppermute(x, 'outer', [(o, (o + k) % outer) for o in range(outer)])  18.5 us
    pallas_call x1, Pallas kernels, backward(): pl.pallas_call(functools.partial(backward_kernel, sizes, capacity), in_sp...  13 us
    ppermute x6, starting transfers between devices, along(): lax.ppermute(x, 'outer', [(o, (o + k) % outer) for o in range(outer)])  10.1 us
    pallas_call x1, Pallas kernels, forward(): pl.pallas_call(forward_kernel, grid=(rows // tile,), in_specs=[pl.BlockSp...  8.4 us
    pallas_call x1, Pallas kernels, route(): pl.pallas_call(functools.partial(route_kernel, devices, capacity), grid=(...  8.07 us
  transfers between devices with their start and end apart: 48, of which 17 were waited for; matrix products, arithmetic and copies ran while one was open for 5% of the time, Pallas kernels for 4%

profile of v1, /device:TPU:0, one launch (start us, length us, event | category | flops | bytes accessed | tf_op | source)
XLA Modules:
  0.0 196.9 jit_solution(2935568519187260879)
XLA Ops:
  0.6 8.1 %route.1 = (f32[32,136,128]{2,1,0:T(8,128)}, s32[1,1024]{1,0:T(1,128)}) custom-call(s32[1,1024]{1,0:T(1,128)} %bitcast.40, s32[1,1024]{1,0:T(1,128)} %bitcast.41, f32[1024,256]{1,0:T(8,128)} %latents_hbm.1, f32[1024,256]{1,0:T(8,128)} %cotangent_hbm.1), custom_call_target="tpu_custom_call" | custom-call | tf_op jit(solution)/shard_map/route/pallas_call | solution.py:244
  8.7 7.3 %all-to-all-start = ((f32[32,136,128]{2,1,0:T(8,128)}), f32[32,136,128]{2,1,0:T(8,128)S(1)}, u32[]{:S(2)}, u32[]{:S(2)}) async-start(f32[32,136,128]{2,1,0:T(8,128)} %get-tuple-element.32), calls=%async_computation | async-start | bytes 4456448 | tf_op jit(solution)/shard_map/all_to_all | solution.py:537
  17.0 8.4 %forward.1 = (bf16[1024,1024]{1,0:T(8,128)(2,1)}, bf16[768,1024]{1,0:T(8,128)(2,1)}, f32[1024,1024]{1,0:T(8,128)}, f32[1024,256]{1,0:T(8,128)}, bf16[1024,512]{1,0:T(8,128)(2,1)}) custom-call(bf16[1024,768]{1,0:T(8,128)(2,1)} %codebook_ref.1, bf16[768,1024]{1,0:T(8,128)(2,1)} %weight_in_ref.1, f32[1,1024]{1,0:T(1,128)} %bitcast.42, ...), custom_call_target="tpu_custom_call" | custom-call | flops 2147483648 | bytes 14680064 | tf_op jit(solution)/shard_map/forward/pallas_call | solution.py:62
  25.4 42.3 %all-to-all-done.incoming_hbm = f32[32,136,128]{2,1,0:T(8,128)S(1)} async-done(((f32[32,136,128]{2,1,0:T(8,128)}), f32[32,136,128]{2,1,0:T(8,128)S(1)}, u32[]{:S(2)}, u32[]{:S(2)}) %all-to-all-start) | async-done | bytes 2228256 | tf_op jit(solution)/shard_map/all_to_all | solution.py:537
  69.1 6.6 %pick_rows.1 = (f32[32,64,256]{2,1,0:T(8,128)}, f32[8,2048]{1,0:T(8,128)}) custom-call(f32[32,136,128]{2,1,0:T(8,128)} %copy-done.2, bf16[1024,512]{1,0:T(8,128)(2,1)} %get-tuple-element.34.parts_ref), custom_call_target="tpu_custom_call" | custom-call | flops 2147483648 | bytes 4194304 | tf_op jit(solution)/shard_map/pick_rows/pallas_call | solution.py:139
  75.7 13.0 %backward.1 = (f32[4,264,128]{2,1,0:T(8,128)}, f32[4,264,128]{2,1,0:T(8,128)}, f32[4,264,128]{2,1,0:T(8,128)}, f32[4,264,128]{2,1,0:T(8,128)}, f32[4,264,128]{2,...) custom-call(f32[32,136,128]{2,1,0:T(8,128)} %copy-done.2, ...), custom_call_target="tpu_custom_call" | custom-call | flops 4831838208 | bytes 16777216 | tf_op jit(solution)/shard_map/backward/pallas_call | solution.py:390
  89.3 4.2 %all-to-all-start.1 = ((f32[32,64,256]{2,1,0:T(8,128)}), f32[32,64,256]{2,1,0:T(8,128)S(1)}, u32[]{:S(2)}, u32[]{:S(2)}) async-start(f32[32,64,256]{2,1,0:T(8,128)} %get-tuple-element.48), calls=%async_computation.1 | async-start | bytes 4194304 | tf_op jit(solution)/shard_map/all_to_all | solution.py:543
  95.2 1.7 collective-permute-start.1
  97.9 1.5 collective-permute-start.5
  100.6 17.0 %collective-permute-done.1 = f32[2,264,128]{2,1,0:T(8,128)S(1)} collective-permute-done((f32[2,264,128]{2,1,0:T(8,128)S(1)}, f32[2,264,128]{2,1,0:T(8,128)S(1)}, u32[]{:S(2)}, u32[]{:S(2)}) %collective-permute-start.1) | collective-permute-done | bytes 270368 | tf_op jit(solution)/shard_map/ppermute | solution.py:490
  118.6 2.6 %collective-permute-start.2 = (f32[264,128]{1,0:T(8,128)S(1)}, f32[264,128]{1,0:T(8,128)S(1)}, u32[]{:S(2)}, u32[]{:S(2)}) collective-permute-start(f32[264,128]{1,0:T(8,128)S(1)} %slice_bitcast_fusion.6), channel_id=1, source_target_pairs={{0,2},{2,0},{1,3},{3,1},{4,6},{6,4},{5,7},{7,5},{8,10},{10,8},{9,1... | collective-permute-start | bytes 405512 | tf_op jit(solution)/shard_map/ppermute | solution.py:490
  123.6 3.6 %collective-permute-done.9 = f32[2,264,128]{2,1,0:T(8,128)S(1)} collective-permute-done((f32[2,264,128]{2,1,0:T(8,128)S(1)}, f32[2,264,128]{2,1,0:T(8,128)S(1)}, u32[]{:S(2)}, u32[]{:S(2)}) %collective-permute-start.9) | collective-permute-done | bytes 270368 | tf_op jit(solution)/shard_map/ppermute | solution.py:490
  127.3 1.8 collective-permute-start.10
  129.3 1.4 collective-permute-done.2
  130.7 3.1 %collective-permute-start.3 = (f32[264,128]{1,0:T(8,128)S(1)}, f32[264,128]{1,0:T(8,128)S(1)}, u32[]{:S(2)}, u32[]{:S(2)}) collective-permute-start(f32[264,128]{1,0:T(8,128)S(1)} %fusion.17), channel_id=1, source_target_pairs={{0,24},{8,0},{16,8},{24,16},{1,25},{9,1},{17,9},{25,17},{2,26},{10... | collective-permute-start | bytes 405512 | tf_op jit(solution)/shard_map/ppermute | solution.py:485
  134.1 2.1 %collective-permute-start.11 = (f32[264,128]{1,0:T(8,128)S(1)}, f32[264,128]{1,0:T(8,128)S(1)}, u32[]{:S(2)}, u32[]{:S(2)}) collective-permute-start(f32[264,128]{1,0:T(8,128)S(1)} %fusion.15), channel_id=1, source_target_pairs={{0,8},{8,16},{16,24},{24,0},{1,9},{9,17},{17,25},{25,1},{2,10},{10... | collective-permute-start | bytes 405512 | tf_op jit(solution)/shard_map/ppermute | solution.py:485
  136.2 1.6 collective-permute-done.3
  137.8 16.3 %collective-permute-done.7 = f32[264,128]{1,0:T(8,128)S(1)} collective-permute-done((f32[264,128]{1,0:T(8,128)S(1)}, f32[264,128]{1,0:T(8,128)S(1)}, u32[]{:S(2)}, u32[]{:S(2)}) %collective-permute-start.7) | collective-permute-done | bytes 135200 | tf_op jit(solution)/shard_map/ppermute | solution.py:485
  156.0 2.0 collective-permute-start.16
  158.3 3.9 %collective-permute-start.15 = (f32[264,128]{1,0:T(8,128)S(1)}, f32[264,128]{1,0:T(8,128)S(1)}, u32[]{:S(2)}, u32[]{:S(2)}) collective-permute-start(f32[264,128]{1,0:T(8,128)S(1)} %fusion.14.refs_0_), channel_id=1, source_target_pairs={{0,24},{8,0},{16,8},{24,16},{1,25},{9,1},{17,9},{25,17},{2,26},{10... | collective-permute-start | bytes 405512 | tf_op jit(solution)/shard_map/ppermute | solution.py:485
  162.2 2.4 %fusion = f32[1024,512]{1,0:T(8,128)S(1)} fusion(s32[1024]{0:T(1024)S(1)} %bitcast.43, bf16[2048,256]{1,0:T(8,128)(2,1)S(1)} %get-tuple-element.58, bf16[2048,256]{1,0:T(8,128)(2,1)S(1)} %get-tuple-element.57), kind=kOutput, calls=%fused_computation.1 | convolution fusion | flops 2153775104 | bytes 4198400 | tf_op jit(solution)/shard_map/dot_general | solution.py:34
  166.3 2.0 %collective-permute-start.24 = (f32[264,128]{1,0:T(8,128)S(1)}, f32[264,128]{1,0:T(8,128)S(1)}, u32[]{:S(2)}, u32[]{:S(2)}) collective-permute-start(f32[264,128]{1,0:T(8,128)S(1)} %collective-permute-done.23.refs_8_), channel_id=1, source_target_pairs={{0,4},{4,0},{1,5},{5,1},{2,6},{6,2},{3,7},{7,3},{8,12},{12,8},{9,1... | collective-permute-start | bytes 405512 | tf_op jit(solution)/shard_map/ppermute | solution.py:490
  170.2 2.1 %collective-permute-start.20 = (f32[264,128]{1,0:T(8,128)S(1)}, f32[264,128]{1,0:T(8,128)S(1)}, u32[]{:S(2)}, u32[]{:S(2)}) collective-permute-start(f32[264,128]{1,0:T(8,128)S(1)} %collective-permute-done.19.refs_4_), channel_id=1, source_target_pairs={{0,2},{2,0},{1,3},{3,1},{4,6},{6,4},{5,7},{7,5},{8,10},{10,8},{9,1... | collective-permute-start | bytes 405512 | tf_op jit(solution)/shard_map/ppermute | solution.py:490
  173.7 1.4 collective-permute-done.21.refs_6_
  175.7 1.5 collective-permute-start.28
  178.7 1.9 collective-permute-start.26
  181.1 2.0 %collective-permute-done.27.refs_13_ = f32[264,128]{1,0:T(8,128)S(1)} collective-permute-done((f32[264,128]{1,0:T(8,128)S(1)}, f32[264,128]{1,0:T(8,128)S(1)}, u32[]{:S(2)}, u32[]{:S(2)}) %collective-permute-start.27) | collective-permute-done | bytes 135200 | tf_op jit(solution)/shard_map/ppermute | solution.py:490
  183.8 1.7 collective-permute-done.26.refs_11_
  185.5 1.6 collective-permute-start.29
  187.6 2.0 %collective-permute-done.22.refs_7_ = f32[264,128]{1,0:T(8,128)S(1)} collective-permute-done((f32[264,128]{1,0:T(8,128)S(1)}, f32[264,128]{1,0:T(8,128)S(1)}, u32[]{:S(2)}, u32[]{:S(2)}) %collective-permute-start.22) | collective-permute-done | bytes 135200 | tf_op jit(solution)/shard_map/ppermute | solution.py:490
  190.1 2.0 %collective-permute-done.29.refs_15_ = f32[264,128]{1,0:T(8,128)S(1)} collective-permute-done((f32[264,128]{1,0:T(8,128)S(1)}, f32[264,128]{1,0:T(8,128)S(1)}, u32[]{:S(2)}, u32[]{:S(2)}) %collective-permute-start.29) | collective-permute-done | bytes 135200 | tf_op jit(solution)/shard_map/ppermute | solution.py:490
  193.4 2.3 %assemble.1 = (f32[768,1024]{1,0:T(8,128)}, f32[1024,256]{1,0:T(8,128)}, f32[2,8,128]{2,1,0:T(8,128)S(1)}) custom-call(f32[264,128]{1,0:T(8,128)S(1)} %fusion.14.refs_0_, f32[264,128]{1,0:T(8,128)S(1)} %collective-permute-done.16.refs_1_, f32[264,128]{1,0:T(8,128)S(1)} %collective-permute-done.17.refs_2_, f32[264,128]{1,0:T(8,128)S(1)} %collective-permute-done.18.refs_3_, ...), custom_call_target="tpu_custom_call" | custom-call | tf_op jit(solution)/shard_map/assemble/pallas_call | solution.py:465
  (109 shorter events, 24.7 us)
Async XLA Ops:
  8.7 59.0 %all-to-all-start = ((f32[32,136,128]{2,1,0:T(8,128)}), f32[32,136,128]{2,1,0:T(8,128)S(1)}, u32[]{:S(2)}, u32[]{:S(2)}) async-start(f32[32,136,128]{2,1,0:T(8,128)} %get-tuple-element.32), calls=%async_computation | async-start | bytes 4456448 | tf_op jit(solution)/shard_map/all_to_all | solution.py:537
  88.8 8.0 %collective-permute-start.4 = (f32[4,264,128]{2,1,0:T(8,128)}, f32[4,264,128]{2,1,0:T(8,128)}, u32[]{:S(2)}, u32[]{:S(2)}) collective-permute-start(f32[4,264,128]{2,1,0:T(8,128)} %get-tuple-element.43), channel_id=1, source_target_pairs={{0,1},{1,0},{2,3},{3,2},{4,5},{5,4},{6,7},{7,6},{8,9},{9,8},{10,11... | collective-permute-start | bytes 1622024 | tf_op jit(solution)/shard_map/ppermute | solution.py:490
  89.3 64.8 %all-to-all-start.1 = ((f32[32,64,256]{2,1,0:T(8,128)}), f32[32,64,256]{2,1,0:T(8,128)S(1)}, u32[]{:S(2)}, u32[]{:S(2)}) async-start(f32[32,64,256]{2,1,0:T(8,128)} %get-tuple-element.48), calls=%async_computation.1 | async-start | bytes 4194304 | tf_op jit(solution)/shard_map/all_to_all | solution.py:543
  93.6 5.8 %collective-permute-start.8 = (f32[4,264,128]{2,1,0:T(8,128)}, f32[4,264,128]{2,1,0:T(8,128)S(1)}, u32[]{:S(2)}, u32[]{:S(2)}) collective-permute-start(f32[4,264,128]{2,1,0:T(8,128)} %get-tuple-element.45), channel_id=1, source_target_pairs={{0,1},{1,0},{2,3},{3,2},{4,5},{5,4},{6,7},{7,6},{8,9},{9,8},{10,11... | collective-permute-start | bytes 1622024 | tf_op jit(solution)/shard_map/ppermute | solution.py:490
  93.7 6.4 %collective-permute-start.12 = (f32[4,264,128]{2,1,0:T(8,128)}, f32[4,264,128]{2,1,0:T(8,128)S(1)}, u32[]{:S(2)}, u32[]{:S(2)}) collective-permute-start(f32[4,264,128]{2,1,0:T(8,128)} %get-tuple-element.47), channel_id=1, source_target_pairs={{0,1},{1,0},{2,3},{3,2},{4,5},{5,4},{6,7},{7,6},{8,9},{9,8},{10,11... | collective-permute-start | bytes 1622024 | tf_op jit(solution)/shard_map/ppermute | solution.py:490
  95.2 22.4 %collective-permute-start.1 = (f32[2,264,128]{2,1,0:T(8,128)S(1)}, f32[2,264,128]{2,1,0:T(8,128)S(1)}, u32[]{:S(2)}, u32[]{:S(2)}) collective-permute-start(f32[2,264,128]{2,1,0:T(8,128)S(1)} %slice_add_fusion.7), channel_id=1, source_target_pairs={{0,4},{4,0},{1,5},{5,1},{2,6},{6,2},{3,7},{7,3},{8,12},{12,8},{9,1... | collective-permute-start | bytes 811016 | tf_op jit(solution)/shard_map/ppermute | solution.py:490
  97.9 23.4 %collective-permute-start.5 = (f32[2,264,128]{2,1,0:T(8,128)S(1)}, f32[2,264,128]{2,1,0:T(8,128)S(1)}, u32[]{:S(2)}, u32[]{:S(2)}) collective-permute-start(f32[2,264,128]{2,1,0:T(8,128)S(1)} %slice_add_fusion.5), channel_id=1, source_target_pairs={{0,2},{2,0},{1,3},{3,1},{4,6},{6,4},{5,7},{7,5},{8,10},{10,8},{9,1... | collective-permute-start | bytes 811016 | tf_op jit(solution)/shard_map/ppermute | solution.py:490
  99.4 27.8 %collective-permute-start.9 = (f32[2,264,128]{2,1,0:T(8,128)S(1)}, f32[2,264,128]{2,1,0:T(8,128)S(1)}, u32[]{:S(2)}, u32[]{:S(2)}) collective-permute-start(f32[2,264,128]{2,1,0:T(8,128)S(1)} %slice_add_fusion.3), channel_id=1, source_target_pairs={{0,4},{4,0},{1,5},{5,1},{2,6},{6,2},{3,7},{7,3},{8,12},{12,8},{9,1... | collective-permute-start | bytes 811016 | tf_op jit(solution)/shard_map/ppermute | solution.py:490
  100.1 29.0 %collective-permute-start.13 = (f32[2,264,128]{2,1,0:T(8,128)S(1)}, f32[2,264,128]{2,1,0:T(8,128)S(1)}, u32[]{:S(2)}, u32[]{:S(2)}) collective-permute-start(f32[2,264,128]{2,1,0:T(8,128)S(1)} %slice_add_fusion.1), channel_id=1, source_target_pairs={{0,2},{2,0},{1,3},{3,1},{4,6},{6,4},{5,7},{7,5},{8,10},{10,8},{9,1... | collective-permute-start | bytes 811016 | tf_op jit(solution)/shard_map/ppermute | solution.py:490
  118.6 12.0 %collective-permute-start.2 = (f32[264,128]{1,0:T(8,128)S(1)}, f32[264,128]{1,0:T(8,128)S(1)}, u32[]{:S(2)}, u32[]{:S(2)}) collective-permute-start(f32[264,128]{1,0:T(8,128)S(1)} %slice_bitcast_fusion.6), channel_id=1, source_target_pairs={{0,2},{2,0},{1,3},{3,1},{4,6},{6,4},{5,7},{7,5},{8,10},{10,8},{9,1... | collective-permute-start | bytes 405512 | tf_op jit(solution)/shard_map/ppermute | solution.py:490
  122.3 11.5 %collective-permute-start.6 = (f32[264,128]{1,0:T(8,128)S(1)}, f32[264,128]{1,0:T(8,128)S(1)}, u32[]{:S(2)}, u32[]{:S(2)}) collective-permute-start(f32[264,128]{1,0:T(8,128)S(1)} %slice_bitcast_fusion.4), channel_id=1, source_target_pairs={{0,4},{4,0},{1,5},{5,1},{2,6},{6,2},{3,7},{7,3},{8,12},{12,8},{9,1... | collective-permute-start | bytes 405512 | tf_op jit(solution)/shard_map/ppermute | solution.py:490
  127.3 6.8 %collective-permute-start.10 = (f32[264,128]{1,0:T(8,128)S(1)}, f32[264,128]{1,0:T(8,128)S(1)}, u32[]{:S(2)}, u32[]{:S(2)}) collective-permute-start(f32[264,128]{1,0:T(8,128)S(1)} %slice_bitcast_fusion.2), channel_id=1, source_target_pairs={{0,2},{2,0},{1,3},{3,1},{4,6},{6,4},{5,7},{7,5},{8,10},{10,8},{9,1... | collective-permute-start | bytes 405512 | tf_op jit(solution)/shard_map/ppermute | solution.py:490
  129.2 7.0 %collective-permute-start.14 = (f32[264,128]{1,0:T(8,128)S(1)}, f32[264,128]{1,0:T(8,128)S(1)}, u32[]{:S(2)}, u32[]{:S(2)}) collective-permute-start(f32[264,128]{1,0:T(8,128)S(1)} %slice_bitcast_fusion), channel_id=1, source_target_pairs={{0,4},{4,0},{1,5},{5,1},{2,6},{6,2},{3,7},{7,3},{8,12},{12,8},{9,1... | collective-permute-start | bytes 405512 | tf_op jit(solution)/shard_map/ppermute | solution.py:490
  130.7 7.1 %collective-permute-start.3 = (f32[264,128]{1,0:T(8,128)S(1)}, f32[264,128]{1,0:T(8,128)S(1)}, u32[]{:S(2)}, u32[]{:S(2)}) collective-permute-start(f32[264,128]{1,0:T(8,128)S(1)} %fusion.17), channel_id=1, source_target_pairs={{0,24},{8,0},{16,8},{24,16},{1,25},{9,1},{17,9},{25,17},{2,26},{10... | collective-permute-start | bytes 405512 | tf_op jit(solution)/shard_map/ppermute | solution.py:485
  133.8 20.3 %collective-permute-start.7 = (f32[264,128]{1,0:T(8,128)S(1)}, f32[264,128]{1,0:T(8,128)S(1)}, u32[]{:S(2)}, u32[]{:S(2)}) collective-permute-start(f32[264,128]{1,0:T(8,128)S(1)} %fusion.16), channel_id=1, source_target_pairs={{0,16},{8,24},{16,0},{24,8},{1,17},{9,25},{17,1},{25,9},{2,18},{10... | collective-permute-start | bytes 405512 | tf_op jit(solution)/shard_map/ppermute | solution.py:485
  134.1 19.9 %collective-permute-start.11 = (f32[264,128]{1,0:T(8,128)S(1)}, f32[264,128]{1,0:T(8,128)S(1)}, u32[]{:S(2)}, u32[]{:S(2)}) collective-permute-start(f32[264,128]{1,0:T(8,128)S(1)} %fusion.15), channel_id=1, source_target_pairs={{0,8},{8,16},{16,24},{24,0},{1,9},{9,17},{17,25},{25,1},{2,10},{10... | collective-permute-start | bytes 405512 | tf_op jit(solution)/shard_map/ppermute | solution.py:485
  154.2 11.0 %collective-permute-start.23 = (f32[264,128]{1,0:T(8,128)S(1)}, f32[264,128]{1,0:T(8,128)S(1)}, u32[]{:S(2)}, u32[]{:S(2)}) collective-permute-start(f32[264,128]{1,0:T(8,128)S(1)} %fusion.14.refs_0_), channel_id=1, source_target_pairs={{0,16},{8,24},{16,0},{24,8},{1,17},{9,25},{17,1},{25,9},{2,18},{10... | collective-permute-start | bytes 405512 | tf_op jit(solution)/shard_map/ppermute | solution.py:485
  155.0 10.3 %collective-permute-start.19 = (f32[264,128]{1,0:T(8,128)S(1)}, f32[264,128]{1,0:T(8,128)S(1)}, u32[]{:S(2)}, u32[]{:S(2)}) collective-permute-start(f32[264,128]{1,0:T(8,128)S(1)} %fusion.14.refs_0_), channel_id=1, source_target_pairs={{0,8},{8,16},{16,24},{24,0},{1,9},{9,17},{17,25},{25,1},{2,10},{10... | collective-permute-start | bytes 405512 | tf_op jit(solution)/shard_map/ppermute | solution.py:485
  155.0 11.3 %collective-permute-start.17 = (f32[264,128]{1,0:T(8,128)S(1)}, f32[264,128]{1,0:T(8,128)S(1)}, u32[]{:S(2)}, u32[]{:S(2)}) collective-permute-start(f32[264,128]{1,0:T(8,128)S(1)} %fusion.14.refs_0_), channel_id=1, source_target_pairs={{0,2},{2,0},{1,3},{3,1},{4,6},{6,4},{5,7},{7,5},{8,10},{10,8},{9,1... | collective-permute-start | bytes 405512 | tf_op jit(solution)/shard_map/ppermute | solution.py:490
  156.0 12.2 %collective-permute-start.16 = (f32[264,128]{1,0:T(8,128)S(1)}, f32[264,128]{1,0:T(8,128)S(1)}, u32[]{:S(2)}, u32[]{:S(2)}) collective-permute-start(f32[264,128]{1,0:T(8,128)S(1)} %fusion.14.refs_0_), channel_id=1, source_target_pairs={{0,4},{4,0},{1,5},{5,1},{2,6},{6,2},{3,7},{7,3},{8,12},{12,8},{9,1... | collective-permute-start | bytes 405512 | tf_op jit(solution)/shard_map/ppermute | solution.py:490
  158.3 9.9 %collective-permute-start.15 = (f32[264,128]{1,0:T(8,128)S(1)}, f32[264,128]{1,0:T(8,128)S(1)}, u32[]{:S(2)}, u32[]{:S(2)}) collective-permute-start(f32[264,128]{1,0:T(8,128)S(1)} %fusion.14.refs_0_), channel_id=1, source_target_pairs={{0,24},{8,0},{16,8},{24,16},{1,25},{9,1},{17,9},{25,17},{2,26},{10... | collective-permute-start | bytes 405512 | tf_op jit(solution)/shard_map/ppermute | solution.py:485
  165.2 7.0 %collective-permute-start.25 = (f32[264,128]{1,0:T(8,128)S(1)}, f32[264,128]{1,0:T(8,128)S(1)}, u32[]{:S(2)}, u32[]{:S(2)}) collective-permute-start(f32[264,128]{1,0:T(8,128)S(1)} %collective-permute-done.23.refs_8_), channel_id=1, source_target_pairs={{0,2},{2,0},{1,3},{3,1},{4,6},{6,4},{5,7},{7,5},{8,10},{10,8},{9,1... | collective-permute-start | bytes 405512 | tf_op jit(solution)/shard_map/ppermute | solution.py:490
  166.3 6.4 %collective-permute-start.24 = (f32[264,128]{1,0:T(8,128)S(1)}, f32[264,128]{1,0:T(8,128)S(1)}, u32[]{:S(2)}, u32[]{:S(2)}) collective-permute-start(f32[264,128]{1,0:T(8,128)S(1)} %collective-permute-done.23.refs_8_), channel_id=1, source_target_pairs={{0,4},{4,0},{1,5},{5,1},{2,6},{6,2},{3,7},{7,3},{8,12},{12,8},{9,1... | collective-permute-start | bytes 405512 | tf_op jit(solution)/shard_map/ppermute | solution.py:490
  168.3 6.9 %collective-permute-start.21 = (f32[264,128]{1,0:T(8,128)S(1)}, f32[264,128]{1,0:T(8,128)S(1)}, u32[]{:S(2)}, u32[]{:S(2)}) collective-permute-start(f32[264,128]{1,0:T(8,128)S(1)} %collective-permute-done.19.refs_4_), channel_id=1, source_target_pairs={{0,4},{4,0},{1,5},{5,1},{2,6},{6,2},{3,7},{7,3},{8,12},{12,8},{9,1... | collective-permute-start | bytes 405512 | tf_op jit(solution)/shard_map/ppermute | solution.py:490
  170.2 5.5 %collective-permute-start.20 = (f32[264,128]{1,0:T(8,128)S(1)}, f32[264,128]{1,0:T(8,128)S(1)}, u32[]{:S(2)}, u32[]{:S(2)}) collective-permute-start(f32[264,128]{1,0:T(8,128)S(1)} %collective-permute-done.19.refs_4_), channel_id=1, source_target_pairs={{0,2},{2,0},{1,3},{3,1},{4,6},{6,4},{5,7},{7,5},{8,10},{10,8},{9,1... | collective-permute-start | bytes 405512 | tf_op jit(solution)/shard_map/ppermute | solution.py:490
  172.8 5.9 %collective-permute-start.18 = (f32[264,128]{1,0:T(8,128)S(1)}, f32[264,128]{1,0:T(8,128)S(1)}, u32[]{:S(2)}, u32[]{:S(2)}) collective-permute-start(f32[264,128]{1,0:T(8,128)S(1)} %collective-permute-done.16.refs_1_), channel_id=1, source_target_pairs={{0,2},{2,0},{1,3},{3,1},{4,6},{6,4},{5,7},{7,5},{8,10},{10,8},{9,1... | collective-permute-start | bytes 405512 | tf_op jit(solution)/shard_map/ppermute | solution.py:490
  177.3 5.9 %collective-permute-start.27 = (f32[264,128]{1,0:T(8,128)S(1)}, f32[264,128]{1,0:T(8,128)S(1)}, u32[]{:S(2)}, u32[]{:S(2)}) collective-permute-start(f32[264,128]{1,0:T(8,128)S(1)} %collective-permute-done.15.refs_12_), channel_id=1, source_target_pairs={{0,2},{2,0},{1,3},{3,1},{4,6},{6,4},{5,7},{7,5},{8,10},{10,8},{9,1... | collective-permute-start | bytes 405512 | tf_op jit(solution)/shard_map/ppermute | solution.py:490
  178.7 6.8 %collective-permute-start.26 = (f32[264,128]{1,0:T(8,128)S(1)}, f32[264,128]{1,0:T(8,128)S(1)}, u32[]{:S(2)}, u32[]{:S(2)}) collective-permute-start(f32[264,128]{1,0:T(8,128)S(1)} %collective-permute-done.24.refs_9_), channel_id=1, source_target_pairs={{0,2},{2,0},{1,3},{3,1},{4,6},{6,4},{5,7},{7,5},{8,10},{10,8},{9,1... | collective-permute-start | bytes 405512 | tf_op jit(solution)/shard_map/ppermute | solution.py:490
  181.1 5.9 %collective-permute-start.36 = (f32[264,128]{1,0:T(8,128)S(1)}, f32[264,128]{1,0:T(8,128)S(1)}, u32[]{:S(2)}, u32[]{:S(2)}) collective-permute-start(f32[264,128]{1,0:T(8,128)S(1)} %collective-permute-done.21.refs_6_), channel_id=1, source_target_pairs={{0,1},{1,0},{2,3},{3,2},{4,5},{5,4},{6,7},{7,6},{8,9},{9,8},{10,11... | collective-permute-start | bytes 405512 | tf_op jit(solution)/shard_map/ppermute | solution.py:490
  183.2 6.4 %collective-permute-start.22 = (f32[264,128]{1,0:T(8,128)S(1)}, f32[264,128]{1,0:T(8,128)S(1)}, u32[]{:S(2)}, u32[]{:S(2)}) collective-permute-start(f32[264,128]{1,0:T(8,128)S(1)} %collective-permute-done.20.refs_5_), channel_id=1, source_target_pairs={{0,4},{4,0},{1,5},{5,1},{2,6},{6,2},{3,7},{7,3},{8,12},{12,8},{9,1... | collective-permute-start | bytes 405512 | tf_op jit(solution)/shard_map/ppermute | solution.py:490
  183.6 6.0 %collective-permute-start.33 = (f32[264,128]{1,0:T(8,128)S(1)}, f32[264,128]{1,0:T(8,128)S(1)}, u32[]{:S(2)}, u32[]{:S(2)}) collective-permute-start(f32[264,128]{1,0:T(8,128)S(1)} %collective-permute-done.18.refs_3_), channel_id=1, source_target_pairs={{0,1},{1,0},{2,3},{3,2},{4,5},{5,4},{6,7},{7,6},{8,9},{9,8},{10,11... | collective-permute-start | bytes 405512 | tf_op jit(solution)/shard_map/ppermute | solution.py:490
  185.5 6.6 %collective-permute-start.29 = (f32[264,128]{1,0:T(8,128)S(1)}, f32[264,128]{1,0:T(8,128)S(1)}, u32[]{:S(2)}, u32[]{:S(2)}) collective-permute-start(f32[264,128]{1,0:T(8,128)S(1)} %collective-permute-done.27.refs_13_), channel_id=1, source_target_pairs={{0,4},{4,0},{1,5},{5,1},{2,6},{6,2},{3,7},{7,3},{8,12},{12,8},{9,1... | collective-permute-start | bytes 405512 | tf_op jit(solution)/shard_map/ppermute | solution.py:490
  (25 other events, 147.3 us)

commit v2 on v1

--- a/solution.py
+++ b/solution.py
@@ -93,7 +93,7 @@
     )(codebook, weight_in, bias_in.reshape(1, -1), weight_out, bias_out.reshape(1, -1))
 
 
-def pick_kernel(capacity, incoming_hbm, parts_ref, out_ref, wanted_ref, asked_ref, sem):
+def pick_kernel(capacity, incoming_hbm, parts_hbm, out_ref, wanted_ref, asked_ref, parts_ref, sems):
     devices = asked_ref.shape[0]
     rows, both = parts_ref.shape
     width = both // 2
@@ -104,32 +104,36 @@
     def _():
         payload = incoming_hbm.shape[1] - EXTRA
         load = pltpu.make_async_copy(
-            incoming_hbm.at[pl.ds(0, devices), pl.ds(payload, EXTRA)], asked_ref, sem
+            incoming_hbm.at[pl.ds(0, devices), pl.ds(payload, EXTRA)], asked_ref, sems.at[0]
         )
         load.start()
+        more = pltpu.make_async_copy(parts_hbm, parts_ref, sems.at[1])
+        more.start()
         load.wait()
         for t in range(devices // per_row):
             row = asked_ref[t * per_row]
             for k in range(1, per_row):
                 row = jnp.maximum(row, pltpu.roll(asked_ref[t * per_row + k], k * capacity, 1))
             wanted_ref[:, t * LANES : (t + 1) * LANES] = row
+        more.wait()
 
     tile = out_ref.shape[0] * capacity
     lane = lax.broadcasted_iota(jnp.int32, (LANES, LANES), 1).astype(jnp.float32)
+    choosers = []
     for start in range(0, tile, LANES):
         at = pl.ds(pl.multiple_of(step * tile + start, LANES), LANES)
         column = jnp.transpose(jnp.broadcast_to(wanted_ref[0:1, at], (LANES, LANES)))
-        chooser = jnp.concatenate(
+        choosers.append(jnp.concatenate(
             [
                 (column == lane + float(r)).astype(jnp.float32).astype(jnp.bfloat16)
                 for r in range(0, rows, LANES)
             ],
             axis=1,
-        )
-        value = dot(chooser, parts_ref[...])
-        value = value[:, :width] + value[:, width:]
-        for k in range(per_row):
-            out_ref[start // capacity + k] = value[k * capacity : (k + 1) * capacity]
+        ))
+    value = dot(jnp.concatenate(choosers, axis=0), parts_ref[...])
+    value = value[:, :width] + value[:, width:]
+    for k in range(out_ref.shape[0]):
+        out_ref[k] = value[k * capacity : (k + 1) * capacity]
 
 
 def pick_rows(capacity, incoming, parts):
@@ -139,10 +143,7 @@
     return pl.pallas_call(
         functools.partial(pick_kernel, capacity),
         grid=(steps,),
-        in_specs=[
-            pl.BlockSpec(memory_space=pl.ANY),
-            pl.BlockSpec((rows, both), lambda i: (0, 0)),
-        ],
+        in_specs=[pl.BlockSpec(memory_space=pl.ANY)] * 2,
         out_specs=[
             pl.BlockSpec((devices // steps, capacity, both // 2), lambda i: (i, 0, 0)),
             pl.BlockSpec((EXTRA, devices * capacity), lambda i: (0, 0)),
@@ -153,7 +154,8 @@
         ],
         scratch_shapes=[
             pltpu.VMEM((devices, EXTRA, LANES), jnp.float32),
-            pltpu.SemaphoreType.DMA,
+            pltpu.VMEM((rows, both), jnp.bfloat16),
+            pltpu.SemaphoreType.DMA((2,)),
         ],
         cost_estimate=pl.CostEstimate(
             flops=2 * devices * capacity * rows * both,
@@ -238,7 +240,7 @@
 
 def route(devices, capacity, code_owner, code_row, latents, cotangent):
     count, width = latents.shape
-    per_step = max(1, 256 // capacity)
+    per_step = max(1, 512 // capacity)
     block = width // LANES * capacity + EXTRA
     whole = lambda *shape: pl.BlockSpec(shape, lambda i: (0,) * len(shape))
     return pl.pallas_call(
@@ -314,7 +316,7 @@
                 ).astype(jnp.bfloat16)
     for load in loads[:4]:
         load.wait()
-    tile = min(256, rows)
+    tile = min(512, rows)
     bias_in = jnp.zeros((1, hidden_size), jnp.float32)
     bias_out = jnp.zeros((1, width), jnp.float32)
     for start in range(0, rows, tile):
@@ -490,9 +492,9 @@
     return lax.ppermute(x, axis, [(p, p ^ j) for p in range(size)])
 
 
-def sum_chunks(sizes, mine, theirs):
+def sum_chunks(sizes, mine, theirs, answers):
     outer, inner, chip, _ = sizes
-    total = None
+    chunks = [None] * outer
     for k in range(outer - 1, -1, -1):
         slow, fast = ("inner", "chip") if k % 2 else ("chip", "inner")
         low = sizes[AXES.index(fast)]
@@ -501,13 +503,14 @@
         for j in range(1, sizes[AXES.index(slow)]):
             here = slice(j * low, (j + 1) * low)
             part = part + across(sizes, slow, mine[k][here] + arrived[here], j)
-        chunk = part[0]
+        chunks[k] = part[0]
         for j in range(1, low):
-            chunk = chunk + across(sizes, fast, part[j], j)
-        if k:
-            chunk = along(sizes, chunk, k)
-        total = chunk if total is None else total + chunk
-    return total
+            chunks[k] = chunks[k] + across(sizes, fast, part[j], j)
+    chunks, answers = lax.optimization_barrier((chunks, answers))
+    total = chunks[0]
+    for k in range(outer - 1, 0, -1):
+        total = total + along(sizes, chunks[k], k)
+    return total, answers
 
 
 def spread_chunks(sizes, total):
@@ -545,8 +548,7 @@
     pieces = backward(
         sizes, capacity, incoming, wanted, hidden_t, slope, projected, codebook_t, weight_out.T
     )
-    total = sum_chunks(sizes, list(pieces[:outer]), list(pieces[outer:]))
-    total, answers = lax.optimization_barrier((total, answers))
+    total, answers = sum_chunks(sizes, list(pieces[:outer]), list(pieces[outer:]), answers)
     answers = answers.reshape(-1, width)
     near = spread_chunks(sizes, total)
 

time: 197 us -> 198 us (level)
  waiting for transfers between devices: 95.3 us -> 101 us
  Pallas kernels: 38.4 us -> 35.6 us
    all_to_all x1, waiting for transfers between devices: 0.01 us -> 8.23 us  [per_device(): lax.all_to_all(picked, AXES, split_axis=0, concat_axis=0, tiled=True)]
    ppermute x6, waiting for transfers between devices: 18.5 us -> 15.3 us  [along(): lax.ppermute(x, 'outer', [(o, (o + k) % outer) for o in range(outer)])]
  transfers between devices with their start and end apart: 48 -> 48, of which waited for: 17 -> 18; matrix products, arithmetic and copies ran while one was open for 5% -> 5% of each run, Pallas kernels for 4% -> 4%
where the time goes in v2:
time: 198 us
  waiting for transfers between devices  101 us (51%)
  starting transfers between devices  48.4 us (24%)
  Pallas kernels  35.6 us (18%)
  other arithmetic  5.93 us (3%)
  local copies, waits for them, and re-layouts  3.61 us (2%)
  matrix products  2.37 us (1%)
    all_to_all x1, waiting for transfers between devices, per_device(): lax.all_to_all(outgoing, AXES, split_axis=0, concat_axis=0, tiled=True)  42.3 us
    ppermute x40, waiting for transfers between devices, across(): return lax.ppermute(x, axis, [(p, p ^ j) for p in range(size)])  35.2 us
    ppermute x40, starting transfers between devices, across(): return lax.ppermute(x, axis, [(p, p ^ j) for p in range(size)])  28.1 us
    ppermute x6, waiting for transfers between devices, along(): lax.ppermute(x, 'outer', [(o, (o + k) % outer) for o in range(outer)])  15.3 us
    pallas_call x1, Pallas kernels, backward(): pl.pallas_call(functools.partial(backward_kernel, sizes, capacity), in_sp...  12.7 us
    ppermute x6, starting transfers between devices, along(): lax.ppermute(x, 'outer', [(o, (o + k) % outer) for o in range(outer)])  8.85 us
    pallas_call x1, Pallas kernels, forward(): pl.pallas_call(forward_kernel, grid=(rows // tile,), in_specs=[pl.BlockSp...  8.4 us
    all_to_all x1, waiting for transfers between devices, per_device(): lax.all_to_all(picked, AXES, split_axis=0, concat_axis=0, tiled=True)  8.23 us
  transfers between devices with their start and end apart: 48, of which 18 were waited for; matrix products, arithmetic and copies ran while one was open for 5% of the time, Pallas kernels for 4%

profile of v2, /device:TPU:0, one launch (start us, length us, event | category | flops | bytes accessed | tf_op | source)
XLA Modules:
  0.0 197.8 jit_solution(18431284431622244762)
XLA Ops:
  0.6 7.0 %route.1 = (f32[32,136,128]{2,1,0:T(8,128)}, s32[1,1024]{1,0:T(1,128)}) custom-call(s32[1,1024]{1,0:T(1,128)} %bitcast.38, s32[1,1024]{1,0:T(1,128)} %bitcast.39, f32[1024,256]{1,0:T(8,128)} %latents_hbm.1, f32[1024,256]{1,0:T(8,128)} %cotangent_hbm.1), custom_call_target="tpu_custom_call" | custom-call | tf_op jit(solution)/shard_map/route/pallas_call | solution.py:246
  7.6 7.3 %all-to-all-start = ((f32[32,136,128]{2,1,0:T(8,128)}), f32[32,136,128]{2,1,0:T(8,128)S(1)}, u32[]{:S(2)}, u32[]{:S(2)}) async-start(f32[32,136,128]{2,1,0:T(8,128)} %get-tuple-element.35), calls=%async_computation | async-start | bytes 4456448 | tf_op jit(solution)/shard_map/all_to_all | solution.py:540
  16.0 8.4 %forward.1 = (bf16[1024,1024]{1,0:T(8,128)(2,1)}, bf16[768,1024]{1,0:T(8,128)(2,1)}, f32[1024,1024]{1,0:T(8,128)}, f32[1024,256]{1,0:T(8,128)}, bf16[1024,512]{1,0:T(8,128)(2,1)}) custom-call(bf16[1024,768]{1,0:T(8,128)(2,1)} %codebook_ref.1, bf16[768,1024]{1,0:T(8,128)(2,1)} %weight_in_ref.1, f32[1,1024]{1,0:T(1,128)} %bitcast.40, ...), custom_call_target="tpu_custom_call" | custom-call | flops 2147483648 | bytes 14680064 | tf_op jit(solution)/shard_map/forward/pallas_call | solution.py:62
  24.4 42.3 %all-to-all-done.incoming_hbm = f32[32,136,128]{2,1,0:T(8,128)S(1)} async-done(((f32[32,136,128]{2,1,0:T(8,128)}), f32[32,136,128]{2,1,0:T(8,128)S(1)}, u32[]{:S(2)}, u32[]{:S(2)}) %all-to-all-start) | async-done | bytes 2228256 | tf_op jit(solution)/shard_map/all_to_all | solution.py:540
  66.7 1.4 copy-done.2
  68.0 5.2 %pick_rows.1 = (f32[32,64,256]{2,1,0:T(8,128)}, f32[8,2048]{1,0:T(8,128)}) custom-call(f32[32,136,128]{2,1,0:T(8,128)} %copy-done.2, bf16[1024,512]{1,0:T(8,128)(2,1)} %get-tuple-element.37.parts_hbm), custom_call_target="tpu_custom_call" | custom-call | flops 2147483648 | bytes 4194304 | tf_op jit(solution)/shard_map/pick_rows/pallas_call | solution.py:143
  73.3 12.7 %backward.1 = (f32[4,264,128]{2,1,0:T(8,128)}, f32[4,264,128]{2,1,0:T(8,128)}, f32[4,264,128]{2,1,0:T(8,128)}, f32[4,264,128]{2,1,0:T(8,128)}, f32[4,264,128]{2,...) custom-call(f32[32,136,128]{2,1,0:T(8,128)} %copy-done.2, ...), custom_call_target="tpu_custom_call" | custom-call | flops 4831838208 | bytes 16777216 | tf_op jit(solution)/shard_map/backward/pallas_call | solution.py:392
  86.6 4.2 %all-to-all-start.1 = ((f32[32,64,256]{2,1,0:T(8,128)}), f32[32,64,256]{2,1,0:T(8,128)S(1)}, u32[]{:S(2)}, u32[]{:S(2)}) async-start(f32[32,64,256]{2,1,0:T(8,128)} %get-tuple-element.51), calls=%async_computation.1 | async-start | bytes 4194304 | tf_op jit(solution)/shard_map/all_to_all | solution.py:546
  92.4 1.7 collective-permute-start.1
  95.1 1.5 collective-permute-start.4
  97.8 19.8 %collective-permute-done.1 = f32[2,264,128]{2,1,0:T(8,128)S(1)} collective-permute-done((f32[2,264,128]{2,1,0:T(8,128)S(1)}, f32[2,264,128]{2,1,0:T(8,128)S(1)}, u32[]{:S(2)}, u32[]{:S(2)}) %collective-permute-start.1) | collective-permute-done | bytes 270368 | tf_op jit(solution)/shard_map/ppermute | solution.py:492
  118.7 1.9 collective-permute-start.2
  122.2 3.0 %collective-permute-done.7 = f32[2,264,128]{2,1,0:T(8,128)S(1)} collective-permute-done((f32[2,264,128]{2,1,0:T(8,128)S(1)}, f32[2,264,128]{2,1,0:T(8,128)S(1)}, u32[]{:S(2)}, u32[]{:S(2)}) %collective-permute-start.7) | collective-permute-done | bytes 270368 | tf_op jit(solution)/shard_map/ppermute | solution.py:492
  126.1 1.3 collective-permute-start.11
  127.6 3.7 %collective-permute-done.8 = f32[264,128]{1,0:T(8,128)S(1)} collective-permute-done((f32[264,128]{1,0:T(8,128)S(1)}, f32[264,128]{1,0:T(8,128)S(1)}, u32[]{:S(2)}, u32[]{:S(2)}) %collective-permute-start.8) | collective-permute-done | bytes 135200 | tf_op jit(solution)/shard_map/ppermute | solution.py:492
  131.5 8.2 %all-to-all-done.1 = f32[32,64,256]{2,1,0:T(8,128)S(1)} async-done(((f32[32,64,256]{2,1,0:T(8,128)}), f32[32,64,256]{2,1,0:T(8,128)S(1)}, u32[]{:S(2)}, u32[]{:S(2)}) %all-to-all-start.1) | async-done | bytes 2097184 | tf_op jit(solution)/shard_map/all_to_all | solution.py:546
  139.7 1.6 collective-permute-start.12
  141.9 4.0 %collective-permute-done.12 = f32[264,128]{1,0:T(8,128)S(1)} collective-permute-done((f32[264,128]{1,0:T(8,128)S(1)}, f32[264,128]{1,0:T(8,128)S(1)}, u32[]{:S(2)}, u32[]{:S(2)}) %collective-permute-start.12) | collective-permute-done | bytes 135200 | tf_op jit(solution)/shard_map/ppermute | solution.py:487
  145.9 7.4 %collective-permute-done.13 = f32[264,128]{1,0:T(8,128)S(1)} collective-permute-done((f32[264,128]{1,0:T(8,128)S(1)}, f32[264,128]{1,0:T(8,128)S(1)}, u32[]{:S(2)}, u32[]{:S(2)}) %collective-permute-start.13) | collective-permute-done | bytes 135200 | tf_op jit(solution)/shard_map/ppermute | solution.py:487
  153.5 2.9 %collective-permute-start.23 = (f32[264,128]{1,0:T(8,128)S(1)}, f32[264,128]{1,0:T(8,128)S(1)}, u32[]{:S(2)}, u32[]{:S(2)}) collective-permute-start(f32[264,128]{1,0:T(8,128)S(1)} %add_add_fusion.refs_0_), channel_id=1, source_target_pairs={{0,16},{8,24},{16,0},{24,8},{1,17},{9,25},{17,1},{25,9},{2,18},{10... | collective-permute-start | bytes 405512 | tf_op jit(solution)/shard_map/ppermute | solution.py:487
  156.4 2.4 %collective-permute-start.16 = (f32[264,128]{1,0:T(8,128)S(1)}, f32[264,128]{1,0:T(8,128)S(1)}, u32[]{:S(2)}, u32[]{:S(2)}) collective-permute-start(f32[264,128]{1,0:T(8,128)S(1)} %add_add_fusion.refs_0_), channel_id=1, source_target_pairs={{0,4},{4,0},{1,5},{5,1},{2,6},{6,2},{3,7},{7,3},{8,12},{12,8},{9,1... | collective-permute-start | bytes 405512 | tf_op jit(solution)/shard_map/ppermute | solution.py:492
  158.8 3.8 %collective-permute-start.15 = (f32[264,128]{1,0:T(8,128)S(1)}, f32[264,128]{1,0:T(8,128)S(1)}, u32[]{:S(2)}, u32[]{:S(2)}) collective-permute-start(f32[264,128]{1,0:T(8,128)S(1)} %add_add_fusion.refs_0_), channel_id=1, source_target_pairs={{0,24},{8,0},{16,8},{24,16},{1,25},{9,1},{17,9},{25,17},{2,26},{10... | collective-permute-start | bytes 405512 | tf_op jit(solution)/shard_map/ppermute | solution.py:487
  162.9 3.7 %collective-permute-done.23.refs_8_ = f32[264,128]{1,0:T(8,128)S(1)} collective-permute-done((f32[264,128]{1,0:T(8,128)S(1)}, f32[264,128]{1,0:T(8,128)S(1)}, u32[]{:S(2)}, u32[]{:S(2)}) %collective-permute-start.23) | collective-permute-done | bytes 135200 | tf_op jit(solution)/shard_map/ppermute | solution.py:487
  166.6 2.4 %collective-permute-start.24 = (f32[264,128]{1,0:T(8,128)S(1)}, f32[264,128]{1,0:T(8,128)S(1)}, u32[]{:S(2)}, u32[]{:S(2)}) collective-permute-start(f32[264,128]{1,0:T(8,128)S(1)} %collective-permute-done.23.refs_8_), channel_id=1, source_target_pairs={{0,4},{4,0},{1,5},{5,1},{2,6},{6,2},{3,7},{7,3},{8,12},{12,8},{9,1... | collective-permute-start | bytes 405512 | tf_op jit(solution)/shard_map/ppermute | solution.py:492
  169.8 2.4 %fusion = f32[1024,512]{1,0:T(8,128)S(1)} fusion(s32[1024]{0:T(1024)S(1)} %bitcast.41, bf16[2048,256]{1,0:T(8,128)(2,1)S(1)} %get-tuple-element.64, bf16[2048,256]{1,0:T(8,128)(2,1)S(1)} %get-tuple-element.63), kind=kOutput, calls=%fused_computation.1 | convolution fusion | flops 2153775104 | bytes 4198400 | tf_op jit(solution)/shard_map/dot_general | solution.py:34
  172.1 1.5 collective-permute-start.20
  173.7 1.4 collective-permute-start.18
  175.9 1.7 collective-permute-start.28
  182.3 1.8 collective-permute-done.27.refs_13_
  186.8 2.2 %collective-permute-start.29 = (f32[264,128]{1,0:T(8,128)S(1)}, f32[264,128]{1,0:T(8,128)S(1)}, u32[]{:S(2)}, u32[]{:S(2)}) collective-permute-start(f32[264,128]{1,0:T(8,128)S(1)} %collective-permute-done.27.refs_13_), channel_id=1, source_target_pairs={{0,4},{4,0},{1,5},{5,1},{2,6},{6,2},{3,7},{7,3},{8,12},{12,8},{9,1... | collective-permute-start | bytes 405512 | tf_op jit(solution)/shard_map/ppermute | solution.py:492
  191.1 1.9 collective-permute-done.29.refs_15_
  194.4 2.3 %assemble.1 = (f32[768,1024]{1,0:T(8,128)}, f32[1024,256]{1,0:T(8,128)}, f32[2,8,128]{2,1,0:T(8,128)S(1)}) custom-call(f32[264,128]{1,0:T(8,128)S(1)} %add_add_fusion.refs_0_, f32[264,128]{1,0:T(8,128)S(1)} %collective-permute-done.16.refs_1_, f32[264,128]{1,0:T(8,128)S(1)} %collective-permute-done.17.refs_2_, ...), custom_call_target="tpu_custom_call" | custom-call | tf_op jit(solution)/shard_map/assemble/pallas_call | solution.py:467
  (110 shorter events, 23.9 us)
Async XLA Ops:
  7.6 59.0 %all-to-all-start = ((f32[32,136,128]{2,1,0:T(8,128)}), f32[32,136,128]{2,1,0:T(8,128)S(1)}, u32[]{:S(2)}, u32[]{:S(2)}) async-start(f32[32,136,128]{2,1,0:T(8,128)} %get-tuple-element.35), calls=%async_computation | async-start | bytes 4456448 | tf_op jit(solution)/shard_map/all_to_all | solution.py:540
  86.1 8.0 %collective-permute-start.3 = (f32[4,264,128]{2,1,0:T(8,128)}, f32[4,264,128]{2,1,0:T(8,128)}, u32[]{:S(2)}, u32[]{:S(2)}) collective-permute-start(f32[4,264,128]{2,1,0:T(8,128)} %get-tuple-element.46), channel_id=1, source_target_pairs={{0,1},{1,0},{2,3},{3,2},{4,5},{5,4},{6,7},{7,6},{8,9},{9,8},{10,11... | collective-permute-start | bytes 1622024 | tf_op jit(solution)/shard_map/ppermute | solution.py:492
  86.6 53.1 %all-to-all-start.1 = ((f32[32,64,256]{2,1,0:T(8,128)}), f32[32,64,256]{2,1,0:T(8,128)S(1)}, u32[]{:S(2)}, u32[]{:S(2)}) async-start(f32[32,64,256]{2,1,0:T(8,128)} %get-tuple-element.51), calls=%async_computation.1 | async-start | bytes 4194304 | tf_op jit(solution)/shard_map/all_to_all | solution.py:546
  90.8 5.8 %collective-permute-start.6 = (f32[4,264,128]{2,1,0:T(8,128)}, f32[4,264,128]{2,1,0:T(8,128)S(1)}, u32[]{:S(2)}, u32[]{:S(2)}) collective-permute-start(f32[4,264,128]{2,1,0:T(8,128)} %get-tuple-element.48), channel_id=1, source_target_pairs={{0,1},{1,0},{2,3},{3,2},{4,5},{5,4},{6,7},{7,6},{8,9},{9,8},{10,11... | collective-permute-start | bytes 1622024 | tf_op jit(solution)/shard_map/ppermute | solution.py:492
  90.9 6.4 %collective-permute-start.9 = (f32[4,264,128]{2,1,0:T(8,128)}, f32[4,264,128]{2,1,0:T(8,128)S(1)}, u32[]{:S(2)}, u32[]{:S(2)}) collective-permute-start(f32[4,264,128]{2,1,0:T(8,128)} %get-tuple-element.50), channel_id=1, source_target_pairs={{0,1},{1,0},{2,3},{3,2},{4,5},{5,4},{6,7},{7,6},{8,9},{9,8},{10,11... | collective-permute-start | bytes 1622024 | tf_op jit(solution)/shard_map/ppermute | solution.py:492
  92.4 25.2 %collective-permute-start.1 = (f32[2,264,128]{2,1,0:T(8,128)S(1)}, f32[2,264,128]{2,1,0:T(8,128)S(1)}, u32[]{:S(2)}, u32[]{:S(2)}) collective-permute-start(f32[2,264,128]{2,1,0:T(8,128)S(1)} %slice_add_fusion.7), channel_id=1, source_target_pairs={{0,2},{2,0},{1,3},{3,1},{4,6},{6,4},{5,7},{7,5},{8,10},{10,8},{9,1... | collective-permute-start | bytes 811016 | tf_op jit(solution)/shard_map/ppermute | solution.py:492
  95.1 25.5 %collective-permute-start.4 = (f32[2,264,128]{2,1,0:T(8,128)S(1)}, f32[2,264,128]{2,1,0:T(8,128)S(1)}, u32[]{:S(2)}, u32[]{:S(2)}) collective-permute-start(f32[2,264,128]{2,1,0:T(8,128)S(1)} %slice_add_fusion.5), channel_id=1, source_target_pairs={{0,4},{4,0},{1,5},{5,1},{2,6},{6,2},{3,7},{7,3},{8,12},{12,8},{9,1... | collective-permute-start | bytes 811016 | tf_op jit(solution)/shard_map/ppermute | solution.py:492
  96.7 28.5 %collective-permute-start.7 = (f32[2,264,128]{2,1,0:T(8,128)S(1)}, f32[2,264,128]{2,1,0:T(8,128)S(1)}, u32[]{:S(2)}, u32[]{:S(2)}) collective-permute-start(f32[2,264,128]{2,1,0:T(8,128)S(1)} %slice_add_fusion.3), channel_id=1, source_target_pairs={{0,2},{2,0},{1,3},{3,1},{4,6},{6,4},{5,7},{7,5},{8,10},{10,8},{9,1... | collective-permute-start | bytes 811016 | tf_op jit(solution)/shard_map/ppermute | solution.py:492
  97.3 28.7 %collective-permute-start.10 = (f32[2,264,128]{2,1,0:T(8,128)S(1)}, f32[2,264,128]{2,1,0:T(8,128)S(1)}, u32[]{:S(2)}, u32[]{:S(2)}) collective-permute-start(f32[2,264,128]{2,1,0:T(8,128)S(1)} %slice_add_fusion.1), channel_id=1, source_target_pairs={{0,4},{4,0},{1,5},{5,1},{2,6},{6,2},{3,7},{7,3},{8,12},{12,8},{9,1... | collective-permute-start | bytes 811016 | tf_op jit(solution)/shard_map/ppermute | solution.py:492
  118.7 8.8 %collective-permute-start.2 = (f32[264,128]{1,0:T(8,128)S(1)}, f32[264,128]{1,0:T(8,128)S(1)}, u32[]{:S(2)}, u32[]{:S(2)}) collective-permute-start(f32[264,128]{1,0:T(8,128)S(1)} %slice_bitcast_fusion.6), channel_id=1, source_target_pairs={{0,4},{4,0},{1,5},{5,1},{2,6},{6,2},{3,7},{7,3},{8,12},{12,8},{9,1... | collective-permute-start | bytes 405512 | tf_op jit(solution)/shard_map/ppermute | solution.py:492
  121.6 6.0 %collective-permute-start.5 = (f32[264,128]{1,0:T(8,128)S(1)}, f32[264,128]{1,0:T(8,128)S(1)}, u32[]{:S(2)}, u32[]{:S(2)}) collective-permute-start(f32[264,128]{1,0:T(8,128)S(1)} %slice_bitcast_fusion.4), channel_id=1, source_target_pairs={{0,2},{2,0},{1,3},{3,1},{4,6},{6,4},{5,7},{7,5},{8,10},{10,8},{9,1... | collective-permute-start | bytes 405512 | tf_op jit(solution)/shard_map/ppermute | solution.py:492
  125.2 6.1 %collective-permute-start.8 = (f32[264,128]{1,0:T(8,128)S(1)}, f32[264,128]{1,0:T(8,128)S(1)}, u32[]{:S(2)}, u32[]{:S(2)}) collective-permute-start(f32[264,128]{1,0:T(8,128)S(1)} %slice_bitcast_fusion.2), channel_id=1, source_target_pairs={{0,4},{4,0},{1,5},{5,1},{2,6},{6,2},{3,7},{7,3},{8,12},{12,8},{9,1... | collective-permute-start | bytes 405512 | tf_op jit(solution)/shard_map/ppermute | solution.py:492
  139.7 6.2 %collective-permute-start.12 = (f32[264,128]{1,0:T(8,128)S(1)}, f32[264,128]{1,0:T(8,128)S(1)}, u32[]{:S(2)}, u32[]{:S(2)}) collective-permute-start(f32[264,128]{1,0:T(8,128)S(1)} %fusion.13), channel_id=1, source_target_pairs={{0,24},{8,0},{16,8},{24,16},{1,25},{9,1},{17,9},{25,17},{2,26},{10... | collective-permute-start | bytes 405512 | tf_op jit(solution)/shard_map/ppermute | solution.py:487
  141.3 12.0 %collective-permute-start.13 = (f32[264,128]{1,0:T(8,128)S(1)}, f32[264,128]{1,0:T(8,128)S(1)}, u32[]{:S(2)}, u32[]{:S(2)}) collective-permute-start(f32[264,128]{1,0:T(8,128)S(1)} %fusion.14), channel_id=1, source_target_pairs={{0,16},{8,24},{16,0},{24,8},{1,17},{9,25},{17,1},{25,9},{2,18},{10... | collective-permute-start | bytes 405512 | tf_op jit(solution)/shard_map/ppermute | solution.py:487
  141.3 12.0 %collective-permute-start.14 = (f32[264,128]{1,0:T(8,128)S(1)}, f32[264,128]{1,0:T(8,128)S(1)}, u32[]{:S(2)}, u32[]{:S(2)}) collective-permute-start(f32[264,128]{1,0:T(8,128)S(1)} %fusion.15), channel_id=1, source_target_pairs={{0,8},{8,16},{16,24},{24,0},{1,9},{9,17},{17,25},{25,1},{2,10},{10... | collective-permute-start | bytes 405512 | tf_op jit(solution)/shard_map/ppermute | solution.py:487
  153.4 5.4 %collective-permute-start.30 = (f32[264,128]{1,0:T(8,128)S(1)}, f32[264,128]{1,0:T(8,128)S(1)}, u32[]{:S(2)}, u32[]{:S(2)}) collective-permute-start(f32[264,128]{1,0:T(8,128)S(1)} %add_add_fusion.refs_0_), channel_id=1, source_target_pairs={{0,1},{1,0},{2,3},{3,2},{4,5},{5,4},{6,7},{7,6},{8,9},{9,8},{10,11... | collective-permute-start | bytes 405512 | tf_op jit(solution)/shard_map/ppermute | solution.py:492
  153.5 13.2 %collective-permute-start.23 = (f32[264,128]{1,0:T(8,128)S(1)}, f32[264,128]{1,0:T(8,128)S(1)}, u32[]{:S(2)}, u32[]{:S(2)}) collective-permute-start(f32[264,128]{1,0:T(8,128)S(1)} %add_add_fusion.refs_0_), channel_id=1, source_target_pairs={{0,16},{8,24},{16,0},{24,8},{1,17},{9,25},{17,1},{25,9},{2,18},{10... | collective-permute-start | bytes 405512 | tf_op jit(solution)/shard_map/ppermute | solution.py:487
  156.3 10.3 %collective-permute-start.19 = (f32[264,128]{1,0:T(8,128)S(1)}, f32[264,128]{1,0:T(8,128)S(1)}, u32[]{:S(2)}, u32[]{:S(2)}) collective-permute-start(f32[264,128]{1,0:T(8,128)S(1)} %add_add_fusion.refs_0_), channel_id=1, source_target_pairs={{0,8},{8,16},{16,24},{24,0},{1,9},{9,17},{17,25},{25,1},{2,10},{10... | collective-permute-start | bytes 405512 | tf_op jit(solution)/shard_map/ppermute | solution.py:487
  156.3 10.3 %collective-permute-start.17 = (f32[264,128]{1,0:T(8,128)S(1)}, f32[264,128]{1,0:T(8,128)S(1)}, u32[]{:S(2)}, u32[]{:S(2)}) collective-permute-start(f32[264,128]{1,0:T(8,128)S(1)} %add_add_fusion.refs_0_), channel_id=1, source_target_pairs={{0,2},{2,0},{1,3},{3,1},{4,6},{6,4},{5,7},{7,5},{8,10},{10,8},{9,1... | collective-permute-start | bytes 405512 | tf_op jit(solution)/shard_map/ppermute | solution.py:492
  156.4 12.7 %collective-permute-start.16 = (f32[264,128]{1,0:T(8,128)S(1)}, f32[264,128]{1,0:T(8,128)S(1)}, u32[]{:S(2)}, u32[]{:S(2)}) collective-permute-start(f32[264,128]{1,0:T(8,128)S(1)} %add_add_fusion.refs_0_), channel_id=1, source_target_pairs={{0,4},{4,0},{1,5},{5,1},{2,6},{6,2},{3,7},{7,3},{8,12},{12,8},{9,1... | collective-permute-start | bytes 405512 | tf_op jit(solution)/shard_map/ppermute | solution.py:492
  158.8 10.4 %collective-permute-start.15 = (f32[264,128]{1,0:T(8,128)S(1)}, f32[264,128]{1,0:T(8,128)S(1)}, u32[]{:S(2)}, u32[]{:S(2)}) collective-permute-start(f32[264,128]{1,0:T(8,128)S(1)} %add_add_fusion.refs_0_), channel_id=1, source_target_pairs={{0,24},{8,0},{16,8},{24,16},{1,25},{9,1},{17,9},{25,17},{2,26},{10... | collective-permute-start | bytes 405512 | tf_op jit(solution)/shard_map/ppermute | solution.py:487
  166.6 5.5 %collective-permute-start.38 = (f32[264,128]{1,0:T(8,128)S(1)}, f32[264,128]{1,0:T(8,128)S(1)}, u32[]{:S(2)}, u32[]{:S(2)}) collective-permute-start(f32[264,128]{1,0:T(8,128)S(1)} %collective-permute-done.23.refs_8_), channel_id=1, source_target_pairs={{0,1},{1,0},{2,3},{3,2},{4,5},{5,4},{6,7},{7,6},{8,9},{9,8},{10,11... | collective-permute-start | bytes 405512 | tf_op jit(solution)/shard_map/ppermute | solution.py:492
  166.6 7.0 %collective-permute-start.25 = (f32[264,128]{1,0:T(8,128)S(1)}, f32[264,128]{1,0:T(8,128)S(1)}, u32[]{:S(2)}, u32[]{:S(2)}) collective-permute-start(f32[264,128]{1,0:T(8,128)S(1)} %collective-permute-done.23.refs_8_), channel_id=1, source_target_pairs={{0,2},{2,0},{1,3},{3,1},{4,6},{6,4},{5,7},{7,5},{8,10},{10,8},{9,1... | collective-permute-start | bytes 405512 | tf_op jit(solution)/shard_map/ppermute | solution.py:492
  166.6 7.0 %collective-permute-start.24 = (f32[264,128]{1,0:T(8,128)S(1)}, f32[264,128]{1,0:T(8,128)S(1)}, u32[]{:S(2)}, u32[]{:S(2)}) collective-permute-start(f32[264,128]{1,0:T(8,128)S(1)} %collective-permute-done.23.refs_8_), channel_id=1, source_target_pairs={{0,4},{4,0},{1,5},{5,1},{2,6},{6,2},{3,7},{7,3},{8,12},{12,8},{9,1... | collective-permute-start | bytes 405512 | tf_op jit(solution)/shard_map/ppermute | solution.py:492
  169.1 6.0 %collective-permute-start.34 = (f32[264,128]{1,0:T(8,128)S(1)}, f32[264,128]{1,0:T(8,128)S(1)}, u32[]{:S(2)}, u32[]{:S(2)}) collective-permute-start(f32[264,128]{1,0:T(8,128)S(1)} %collective-permute-done.19.refs_4_), channel_id=1, source_target_pairs={{0,1},{1,0},{2,3},{3,2},{4,5},{5,4},{6,7},{7,6},{8,9},{9,8},{10,11... | collective-permute-start | bytes 405512 | tf_op jit(solution)/shard_map/ppermute | solution.py:492
  169.2 6.7 %collective-permute-start.21 = (f32[264,128]{1,0:T(8,128)S(1)}, f32[264,128]{1,0:T(8,128)S(1)}, u32[]{:S(2)}, u32[]{:S(2)}) collective-permute-start(f32[264,128]{1,0:T(8,128)S(1)} %collective-permute-done.19.refs_4_), channel_id=1, source_target_pairs={{0,4},{4,0},{1,5},{5,1},{2,6},{6,2},{3,7},{7,3},{8,12},{12,8},{9,1... | collective-permute-start | bytes 405512 | tf_op jit(solution)/shard_map/ppermute | solution.py:492
  172.1 6.8 %collective-permute-start.20 = (f32[264,128]{1,0:T(8,128)S(1)}, f32[264,128]{1,0:T(8,128)S(1)}, u32[]{:S(2)}, u32[]{:S(2)}) collective-permute-start(f32[264,128]{1,0:T(8,128)S(1)} %collective-permute-done.19.refs_4_), channel_id=1, source_target_pairs={{0,2},{2,0},{1,3},{3,1},{4,6},{6,4},{5,7},{7,5},{8,10},{10,8},{9,1... | collective-permute-start | bytes 405512 | tf_op jit(solution)/shard_map/ppermute | solution.py:492
  173.6 6.5 %collective-permute-start.31 = (f32[264,128]{1,0:T(8,128)S(1)}, f32[264,128]{1,0:T(8,128)S(1)}, u32[]{:S(2)}, u32[]{:S(2)}) collective-permute-start(f32[264,128]{1,0:T(8,128)S(1)} %collective-permute-done.16.refs_1_), channel_id=1, source_target_pairs={{0,1},{1,0},{2,3},{3,2},{4,5},{5,4},{6,7},{7,6},{8,9},{9,8},{10,11... | collective-permute-start | bytes 405512 | tf_op jit(solution)/shard_map/ppermute | solution.py:492
  173.7 7.0 %collective-permute-start.18 = (f32[264,128]{1,0:T(8,128)S(1)}, f32[264,128]{1,0:T(8,128)S(1)}, u32[]{:S(2)}, u32[]{:S(2)}) collective-permute-start(f32[264,128]{1,0:T(8,128)S(1)} %collective-permute-done.16.refs_1_), channel_id=1, source_target_pairs={{0,2},{2,0},{1,3},{3,1},{4,6},{6,4},{5,7},{7,5},{8,10},{10,8},{9,1... | collective-permute-start | bytes 405512 | tf_op jit(solution)/shard_map/ppermute | solution.py:492
  181.1 5.7 %collective-permute-start.26 = (f32[264,128]{1,0:T(8,128)S(1)}, f32[264,128]{1,0:T(8,128)S(1)}, u32[]{:S(2)}, u32[]{:S(2)}) collective-permute-start(f32[264,128]{1,0:T(8,128)S(1)} %collective-permute-done.24.refs_9_), channel_id=1, source_target_pairs={{0,2},{2,0},{1,3},{3,1},{4,6},{6,4},{5,7},{7,5},{8,10},{10,8},{9,1... | collective-permute-start | bytes 405512 | tf_op jit(solution)/shard_map/ppermute | solution.py:492
  184.6 6.0 %collective-permute-start.22 = (f32[264,128]{1,0:T(8,128)S(1)}, f32[264,128]{1,0:T(8,128)S(1)}, u32[]{:S(2)}, u32[]{:S(2)}) collective-permute-start(f32[264,128]{1,0:T(8,128)S(1)} %collective-permute-done.20.refs_5_), channel_id=1, source_target_pairs={{0,4},{4,0},{1,5},{5,1},{2,6},{6,2},{3,7},{7,3},{8,12},{12,8},{9,1... | collective-permute-start | bytes 405512 | tf_op jit(solution)/shard_map/ppermute | solution.py:492
  186.8 6.2 %collective-permute-start.29 = (f32[264,128]{1,0:T(8,128)S(1)}, f32[264,128]{1,0:T(8,128)S(1)}, u32[]{:S(2)}, u32[]{:S(2)}) collective-permute-start(f32[264,128]{1,0:T(8,128)S(1)} %collective-permute-done.27.refs_13_), channel_id=1, source_target_pairs={{0,4},{4,0},{1,5},{5,1},{2,6},{6,2},{3,7},{7,3},{8,12},{12,8},{9,1... | collective-permute-start | bytes 405512 | tf_op jit(solution)/shard_map/ppermute | solution.py:492
  (25 other events, 160.4 us)

commit v3 on v2

--- a/solution.py
+++ b/solution.py
@@ -93,12 +93,21 @@
     )(codebook, weight_in, bias_in.reshape(1, -1), weight_out, bias_out.reshape(1, -1))
 
 
-def pick_kernel(capacity, incoming_hbm, parts_hbm, out_ref, wanted_ref, asked_ref, parts_ref, sems):
+def join_wanted(capacity, asked_ref, wanted_ref):
+    per_row = LANES // capacity
+    for t in range(asked_ref.shape[0] // per_row):
+        row = asked_ref[t * per_row]
+        for k in range(1, per_row):
+            row = jnp.maximum(row, pltpu.roll(asked_ref[t * per_row + k], k * capacity, 1))
+        wanted_ref[:, t * LANES : (t + 1) * LANES] = row
+
+
+def pick_kernel(capacity, incoming_hbm, parts_hbm, *refs):
+    out_refs, (wanted_ref, asked_ref, parts_ref, sems) = refs[:-4], refs[-4:]
     devices = asked_ref.shape[0]
     rows, both = parts_ref.shape
     width = both // 2
     step = pl.program_id(0)
-    per_row = LANES // capacity
 
     @pl.when(step == 0)
     def _():
@@ -110,14 +119,10 @@
         more = pltpu.make_async_copy(parts_hbm, parts_ref, sems.at[1])
         more.start()
         load.wait()
-        for t in range(devices // per_row):
-            row = asked_ref[t * per_row]
-            for k in range(1, per_row):
-                row = jnp.maximum(row, pltpu.roll(asked_ref[t * per_row + k], k * capacity, 1))
-            wanted_ref[:, t * LANES : (t + 1) * LANES] = row
+        join_wanted(capacity, asked_ref, wanted_ref)
         more.wait()
 
-    tile = out_ref.shape[0] * capacity
+    tile = out_refs[0].shape[0] * capacity
     lane = lax.broadcasted_iota(jnp.int32, (LANES, LANES), 1).astype(jnp.float32)
     choosers = []
     for start in range(0, tile, LANES):
@@ -132,27 +137,24 @@
         ))
     value = dot(jnp.concatenate(choosers, axis=0), parts_ref[...])
     value = value[:, :width] + value[:, width:]
-    for k in range(out_ref.shape[0]):
-        out_ref[k] = value[k * capacity : (k + 1) * capacity]
+    for j, out_ref in enumerate(out_refs):
+        for k in range(out_ref.shape[0]):
+            out_ref[k] = value[k * capacity : (k + 1) * capacity, j * LANES : (j + 1) * LANES]
 
 
 def pick_rows(capacity, incoming, parts):
     devices = incoming.shape[0]
     rows, both = parts.shape
     steps = 4
+    blocks = both // 2 // LANES
     return pl.pallas_call(
         functools.partial(pick_kernel, capacity),
         grid=(steps,),
         in_specs=[pl.BlockSpec(memory_space=pl.ANY)] * 2,
-        out_specs=[
-            pl.BlockSpec((devices // steps, capacity, both // 2), lambda i: (i, 0, 0)),
-            pl.BlockSpec((EXTRA, devices * capacity), lambda i: (0, 0)),
-        ],
-        out_shape=[
-            jax.ShapeDtypeStruct((devices, capacity, both // 2), jnp.float32),
-            jax.ShapeDtypeStruct((EXTRA, devices * capacity), jnp.float32),
-        ],
+        out_specs=[pl.BlockSpec((devices // steps, capacity, LANES), lambda i: (i, 0, 0))] * blocks,
+        out_shape=[jax.ShapeDtypeStruct((devices, capacity, LANES), jnp.float32)] * blocks,
         scratch_shapes=[
+            pltpu.VMEM((EXTRA, devices * capacity), jnp.float32),
             pltpu.VMEM((devices, EXTRA, LANES), jnp.float32),
             pltpu.VMEM((rows, both), jnp.bfloat16),
             pltpu.SemaphoreType.DMA((2,)),
@@ -162,7 +164,7 @@
             bytes_accessed=4 * devices * capacity * both,
             transcendentals=0,
         ),
-        compiler_params=pltpu.CompilerParams(vmem_limit_bytes=60 * 2**20),
+        compiler_params=pltpu.CompilerParams(vmem_limit_bytes=24 * 2**20),
         name="pick_rows",
     )(incoming, parts)
 
@@ -275,20 +277,21 @@
     return j % inner * chip + j // inner
 
 
-def backward_kernel(sizes, capacity, incoming_hbm, wanted_hbm, hidden_hbm, slope_hbm, projected_hbm,
+def backward_kernel(sizes, capacity, incoming_hbm, hidden_hbm, slope_hbm, projected_hbm,
                     codebook_hbm, weight_hbm, *refs):
     outer, inner, chip, core = sizes
     devices = outer * inner * chip * core
     mine_hbm, theirs_hbm, refs = refs[:outer], refs[outer : 2 * outer], refs[2 * outer :]
-    (incoming, wanted, hidden, slope, projected, codebook, weight, parts, low, grad, flat,
+    (asked, incoming, hidden, slope, projected, codebook, weight, parts, wanted, low, grad, flat,
      in_sem, out_sem) = refs
     width = projected.shape[1]
     dim_in, rows = codebook.shape
     hidden_size = hidden.shape[0]
     length = flat.shape[2] - EXTRA
     pairs = list(zip(
-        (wanted_hbm, projected_hbm, weight_hbm, slope_hbm, hidden_hbm, codebook_hbm),
-        (wanted, projected, weight, slope, hidden, codebook),
+        (incoming_hbm.at[pl.ds(0, devices), pl.ds(width // LANES * capacity, EXTRA)],
+         projected_hbm, weight_hbm, slope_hbm, hidden_hbm, codebook_hbm),
+        (asked, projected, weight, slope, hidden, codebook),
     ))
     loads = [pltpu.make_async_copy(a, b, in_sem.at[k]) for k, (a, b) in enumerate(pairs)]
     loads[0].start()
@@ -314,7 +317,9 @@
                 parts[own, width + j * LANES : width + (j + 1) * LANES] = (
                     value - high.astype(jnp.float32)
                 ).astype(jnp.bfloat16)
-    for load in loads[:4]:
+    loads[0].wait()
+    join_wanted(capacity, asked, wanted)
+    for load in loads[1:4]:
         load.wait()
     tile = min(512, rows)
     bias_in = jnp.zeros((1, hidden_size), jnp.float32)
@@ -379,14 +384,14 @@
         copy.wait()
 
 
-def backward(sizes, capacity, incoming, wanted, hidden_t, slope, projected, codebook_t, weight_t):
+def backward(sizes, capacity, incoming, hidden_t, slope, projected, codebook_t, weight_t):
     devices = incoming.shape[0]
     rows, width = projected.shape
     dim_in, hidden_size = codebook_t.shape[0], hidden_t.shape[0]
     length = (dim_in + width) * hidden_size // LANES // devices
     outer, inner, chip, core = sizes
     piece = jax.ShapeDtypeStruct((inner * chip, length + EXTRA, LANES), jnp.float32)
-    operands = (incoming, wanted, hidden_t, slope, projected, codebook_t, weight_t)
+    operands = (incoming, hidden_t, slope, projected, codebook_t, weight_t)
     vmem = lambda shape, dtype: pltpu.VMEM(shape, dtype)
     slots = devices * capacity
     return pl.pallas_call(
@@ -394,10 +399,14 @@
         in_specs=[pl.BlockSpec(memory_space=pl.ANY)] * len(operands),
         out_specs=[pl.BlockSpec(memory_space=pl.ANY)] * (2 * outer),
         out_shape=[piece] * (2 * outer),
-        scratch_shapes=[vmem((devices, incoming.shape[1] - EXTRA, LANES), jnp.float32)]
+        scratch_shapes=[
+            vmem((devices, EXTRA, LANES), jnp.float32),
+            vmem((devices, incoming.shape[1] - EXTRA, LANES), jnp.float32),
+        ]
         + [vmem(a.shape, a.dtype) for a in operands[1:]]
         + [
             vmem((slots, 2 * width), jnp.bfloat16),
+            vmem((EXTRA, slots), jnp.float32),
             vmem((rows, width), jnp.bfloat16),
             vmem((rows, hidden_size), jnp.bfloat16),
             vmem((outer, inner * chip * core, length + EXTRA, LANES), jnp.float32),
@@ -409,7 +418,7 @@
             bytes_accessed=16 * rows * hidden_size,
             transcendentals=0,
         ),
-        compiler_params=pltpu.CompilerParams(vmem_limit_bytes=60 * 2**20),
+        compiler_params=pltpu.CompilerParams(vmem_limit_bytes=40 * 2**20),
         name="backward",
     )(*operands)
 
@@ -492,7 +501,7 @@
     return lax.ppermute(x, axis, [(p, p ^ j) for p in range(size)])
 
 
-def sum_chunks(sizes, mine, theirs, answers):
+def sum_chunks(sizes, mine, theirs, first_answers):
     outer, inner, chip, _ = sizes
     chunks = [None] * outer
     for k in range(outer - 1, -1, -1):
@@ -506,23 +515,24 @@
         chunks[k] = part[0]
         for j in range(1, low):
             chunks[k] = chunks[k] + across(sizes, fast, part[j], j)
-    chunks, answers = lax.optimization_barrier((chunks, answers))
+    chunks, first_answers = lax.optimization_barrier((chunks, first_answers))
     total = chunks[0]
     for k in range(outer - 1, 0, -1):
         total = total + along(sizes, chunks[k], k)
-    return total, answers
-
-
-def spread_chunks(sizes, total):
+    return total, first_answers
+
+
+def spread_chunks(sizes, total, second):
     outer, inner, chip, _ = sizes
     near = []
-    for k in range(outer):
+    lines = [along(sizes, total, k) if k else total for k in range(outer)]
+    lines[outer // 2], second = lax.optimization_barrier((lines[outer // 2], second))
+    for k, x in enumerate(lines):
         slow, fast = ("inner", "chip") if k % 2 else ("chip", "inner")
-        x = along(sizes, total, k) if k else total
         row = [across(sizes, fast, x, j) if j else x for j in range(sizes[AXES.index(fast)])]
         for j in range(sizes[AXES.index(slow)]):
             near += [across(sizes, slow, x, j) if j else x for x in row]
-    return near
+    return near, second
 
 
 def per_device(
@@ -542,22 +552,27 @@
     hidden_t, codebook_t, slope, projected, parts = forward(
         codebook, weight_in, bias_in, weight_out, bias_out
     )
-    picked, wanted = pick_rows(capacity, incoming, parts)
-    answers = lax.all_to_all(picked, AXES, split_axis=0, concat_axis=0, tiled=True)
-
     pieces = backward(
-        sizes, capacity, incoming, wanted, hidden_t, slope, projected, codebook_t, weight_out.T
+        sizes, capacity, incoming, hidden_t, slope, projected, codebook_t, weight_out.T
     )
-    total, answers = sum_chunks(sizes, list(pieces[:outer]), list(pieces[outer:]), answers)
-    answers = answers.reshape(-1, width)
-    near = spread_chunks(sizes, total)
+    mine, theirs = list(pieces[:outer]), list(pieces[outer:])
+    theirs[0], incoming = lax.optimization_barrier((theirs[0], incoming))
+
+    def exchange(x):
+        x = lax.all_to_all(x, AXES, split_axis=0, concat_axis=0, tiled=True)
+        return x.reshape(-1, x.shape[-1])
+
+    picked = pick_rows(capacity, incoming, parts)
+    total, first = sum_chunks(sizes, mine, theirs, exchange(picked[0]))
+    near, second = spread_chunks(sizes, total, list(picked[1:]))
 
     slot_ids = jnp.arange(devices * capacity, dtype=jnp.int32)
-    from_slot = slots.reshape(-1, 1) == slot_ids[None, :]
-    chosen = pick(from_slot.astype(jnp.bfloat16), answers)
+    from_slot = (slots.reshape(-1, 1) == slot_ids[None, :]).astype(jnp.bfloat16)
+    first = pick(from_slot, first)
+    late = len(near) - inner * chip
+    near[late], first = lax.optimization_barrier((near[late], first))
+    chosen = jnp.concatenate([first] + [pick(from_slot, exchange(x)) for x in second], axis=1)
     latent_grad = cotangent - 0.25 * (chosen - latents)
-    late = len(near) - inner * chip
-    near[late], latent_grad = lax.optimization_barrier((near[late], latent_grad))
 
     chunks = near + [across(sizes, "core", x, 1) for x in near]
     gw_in, gw_out, biases = assemble(sizes, chunks, dim_in, hidden_size, width)

time: 198 us -> 222 us (1.12); the launches traced: 198 us -> 218 us
  starting transfers between devices: 48.4 us -> 53.8 us
  local copies, waits for them, and re-layouts: 3.61 us -> 8.69 us
  other arithmetic: 5.93 us -> 9.76 us
  waiting for transfers between devices: 101 us -> 104 us
    ppermute x6, waiting for transfers between devices: 15.3 us -> 32.4 us  [along(): lax.ppermute(x, 'outer', [(o, (o + k) % outer) for o in range(outer)])]
    all_to_all x1 -> x2, waiting for transfers between devices: 8.23 us -> 0.01 us  [exchange(): x = lax.all_to_all(x, AXES, split_axis=0, concat_axis=0, tiled=True)]
    ppermute x40, waiting for transfers between devices: 35.2 us -> 29.3 us  [across(): return lax.ppermute(x, axis, [(p, p ^ j) for p in range(size)])]
    unnamed x19 -> x27, local copies, waits for them, and re-layouts: 2.41 us -> 7.49 us
    add x8, other arithmetic: 4.24 us -> 8.02 us  [sum_chunks(): part = part + across(sizes, slow, mine[k][here] + arrived[here], j)]
    pallas_call x1, Pallas kernels: 12.7 us -> 15.6 us  [backward(): pl.pallas_call(functools.partial(backward_kernel, sizes, capacity), in_sp...]
    all_to_all x1 -> x2, starting transfers between devices: 4.17 us -> 6.79 us  [exchange(): x = lax.all_to_all(x, AXES, split_axis=0, concat_axis=0, tiled=True)]
  transfers between devices with their start and end apart: 48 -> 49, of which waited for: 18 -> 16; matrix products, arithmetic and copies ran while one was open for 5% -> 6% of each run, Pallas kernels for 4% -> 7%
where the time goes in v3:
time: 222 us; the launch traced here: 218 us
  waiting for transfers between devices  104 us (47%)
  starting transfers between devices  53.8 us (24%)
  Pallas kernels  37.3 us (17%)
  other arithmetic  9.76 us (4%)
  local copies, waits for them, and re-layouts  8.69 us (4%)
  matrix products  2.99 us (1%)
    all_to_all x1, waiting for transfers between devices, per_device(): lax.all_to_all(outgoing, AXES, split_axis=0, concat_axis=0, tiled=True)  42.3 us
    ppermute x6, waiting for transfers between devices, along(): lax.ppermute(x, 'outer', [(o, (o + k) % outer) for o in range(outer)])  32.4 us
    ppermute x40, waiting for transfers between devices, across(): return lax.ppermute(x, axis, [(p, p ^ j) for p in range(size)])  29.3 us
    ppermute x40, starting transfers between devices, across(): return lax.ppermute(x, axis, [(p, p ^ j) for p in range(size)])  29 us
    pallas_call x1, Pallas kernels, backward(): pl.pallas_call(functools.partial(backward_kernel, sizes, capacity), in_sp...  15.6 us
    ppermute x6, starting transfers between devices, along(): lax.ppermute(x, 'outer', [(o, (o + k) % outer) for o in range(outer)])  10.7 us
    pallas_call x1, Pallas kernels, forward(): pl.pallas_call(forward_kernel, grid=(rows // tile,), in_specs=[pl.BlockSp...  8.4 us
    add x8, other arithmetic, sum_chunks(): part = part + across(sizes, slow, mine[k][here] + arrived[here], j)  8.02 us
  transfers between devices with their start and end apart: 49, of which 16 were waited for; matrix products, arithmetic and copies ran while one was open for 6% of the time, Pallas kernels for 7%

profile of v3, /device:TPU:0, one launch (start us, length us, event | category | flops | bytes accessed | tf_op | source)
XLA Modules:
  0.0 217.5 jit_solution(17316818081528358298)
XLA Ops:
  0.6 7.0 %route.1 = (f32[32,136,128]{2,1,0:T(8,128)}, s32[1,1024]{1,0:T(1,128)}) custom-call(s32[1,1024]{1,0:T(1,128)} %bitcast.40, s32[1,1024]{1,0:T(1,128)} %bitcast.41, f32[1024,256]{1,0:T(8,128)} %latents_hbm.1, f32[1024,256]{1,0:T(8,128)} %cotangent_hbm.1), custom_call_target="tpu_custom_call" | custom-call | tf_op jit(solution)/shard_map/route/pallas_call | solution.py:248
  7.6 7.3 %all-to-all-start = ((f32[32,136,128]{2,1,0:T(8,128)}), f32[32,136,128]{2,1,0:T(8,128)S(1)}, u32[]{:S(2)}, u32[]{:S(2)}) async-start(f32[32,136,128]{2,1,0:T(8,128)} %get-tuple-element.39), calls=%async_computation | async-start | bytes 4456448 | tf_op jit(solution)/shard_map/all_to_all | solution.py:550
  16.0 8.4 %forward.1 = (bf16[1024,1024]{1,0:T(8,128)(2,1)}, bf16[768,1024]{1,0:T(8,128)(2,1)}, f32[1024,1024]{1,0:T(8,128)}, f32[1024,256]{1,0:T(8,128)}, bf16[1024,512]{1,0:T(8,128)(2,1)}) custom-call(bf16[1024,768]{1,0:T(8,128)(2,1)} %codebook_ref.1, bf16[768,1024]{1,0:T(8,128)(2,1)} %weight_in_ref.1, f32[1,1024]{1,0:T(1,128)} %bitcast.42, ...), custom_call_target="tpu_custom_call" | custom-call | flops 2147483648 | bytes 14680064 | tf_op jit(solution)/shard_map/forward/pallas_call | solution.py:62
  24.4 42.3 %all-to-all-done.incoming_hbm = f32[32,136,128]{2,1,0:T(8,128)S(1)} async-done(((f32[32,136,128]{2,1,0:T(8,128)}), f32[32,136,128]{2,1,0:T(8,128)S(1)}, u32[]{:S(2)}, u32[]{:S(2)}) %all-to-all-start) | async-done | bytes 2228256 | tf_op jit(solution)/shard_map/all_to_all | solution.py:550
  67.7 1.6 copy-done.5
  71.9 15.6 %backward.1 = (f32[4,264,128]{2,1,0:T(8,128)S(1)}, f32[4,264,128]{2,1,0:T(8,128)S(1)}, f32[4,264,128]{2,1,0:T(8,128)S(1)}, f32[4,264,128]{2,1,0:T(8,128)S(1)}, f...) custom-call(f32[32,136,128]{2,1,0:T(8,128)S(1)} %all-to-all-done.incoming_hbm, ...), custom_call_target="tpu_custom_call" | custom-call | flops 4831838208 | bytes 16777216 | tf_op jit(solution)/shard_map/backward/pallas_call | solution.py:397
  88.7 4.0 %pick_rows.1 = (f32[32,64,128]{2,1,0:T(8,128)}, f32[32,64,128]{2,1,0:T(8,128)}) custom-call(f32[32,136,128]{2,1,0:T(8,128)S(1)} %all-to-all-done.incoming_hbm, bf16[1024,512]{1,0:T(8,128)(2,1)S(1)} %copy-done.7), custom_call_target="tpu_custom_call" | custom-call | flops 2147483648 | bytes 4194304 | tf_op jit(solution)/shard_map/pick_rows/pallas_call | solution.py:150
  92.8 4.0 %all-to-all-start.1 = ((f32[32,64,128]{2,1,0:T(8,128)}), f32[32,64,128]{2,1,0:T(8,128)S(1)}, u32[]{:S(2)}, u32[]{:S(2)}) async-start(f32[32,64,128]{2,1,0:T(8,128)} %get-tuple-element.56), calls=%async_computation.1 | async-start | bytes 2097152 | tf_op jit(solution)/shard_map/all_to_all | solution.py:562
  97.8 1.8 collective-permute-start.1
  100.6 1.5 collective-permute-start.4
  105.1 10.6 %collective-permute-done.1 = f32[2,264,128]{2,1,0:T(8,128)S(1)} collective-permute-done((f32[2,264,128]{2,1,0:T(8,128)S(1)}, f32[2,264,128]{2,1,0:T(8,128)S(1)}, u32[]{:S(2)}, u32[]{:S(2)}) %collective-permute-start.1) | collective-permute-done | bytes 270368 | tf_op jit(solution)/shard_map/ppermute | solution.py:501
  120.0 3.0 %collective-permute-done.7 = f32[2,264,128]{2,1,0:T(8,128)S(1)} collective-permute-done((f32[2,264,128]{2,1,0:T(8,128)S(1)}, f32[2,264,128]{2,1,0:T(8,128)S(1)}, u32[]{:S(2)}, u32[]{:S(2)}) %collective-permute-start.7) | collective-permute-done | bytes 270368 | tf_op jit(solution)/shard_map/ppermute | solution.py:501
  124.0 1.5 collective-permute-start.8
  127.2 1.8 collective-permute-done.8
  129.1 2.5 %collective-permute-done.11 = f32[264,128]{1,0:T(8,128)S(1)} collective-permute-done((f32[264,128]{1,0:T(8,128)S(1)}, f32[264,128]{1,0:T(8,128)S(1)}, u32[]{:S(2)}, u32[]{:S(2)}) %collective-permute-start.11) | collective-permute-done | bytes 135200 | tf_op jit(solution)/shard_map/ppermute | solution.py:501
  131.6 3.1 %collective-permute-start.12 = (f32[264,128]{1,0:T(8,128)S(1)}, f32[264,128]{1,0:T(8,128)S(1)}, u32[]{:S(2)}, u32[]{:S(2)}) collective-permute-start(f32[264,128]{1,0:T(8,128)S(1)} %fusion.18), channel_id=1, source_target_pairs={{0,24},{8,0},{16,8},{24,16},{1,25},{9,1},{17,9},{25,17},{2,26},{10... | collective-permute-start | bytes 405512 | tf_op jit(solution)/shard_map/ppermute | solution.py:496
  136.1 2.6 %collective-permute-done.12 = f32[264,128]{1,0:T(8,128)S(1)} collective-permute-done((f32[264,128]{1,0:T(8,128)S(1)}, f32[264,128]{1,0:T(8,128)S(1)}, u32[]{:S(2)}, u32[]{:S(2)}) %collective-permute-start.12) | collective-permute-done | bytes 135200 | tf_op jit(solution)/shard_map/ppermute | solution.py:496
  138.8 6.7 %collective-permute-done.13 = f32[264,128]{1,0:T(8,128)S(1)} collective-permute-done((f32[264,128]{1,0:T(8,128)S(1)}, f32[264,128]{1,0:T(8,128)S(1)}, u32[]{:S(2)}, u32[]{:S(2)}) %collective-permute-start.13) | collective-permute-done | bytes 135200 | tf_op jit(solution)/shard_map/ppermute | solution.py:496
  145.5 2.2 %collective-permute-start.16 = (f32[264,128]{1,0:T(8,128)S(1)}, f32[264,128]{1,0:T(8,128)S(1)}, u32[]{:S(2)}, u32[]{:S(2)}) collective-permute-start(f32[264,128]{1,0:T(8,128)S(1)} %add_add_fusion.refs_0_), channel_id=1, source_target_pairs={{0,16},{8,24},{16,0},{24,8},{1,17},{9,25},{17,1},{25,9},{2,18},{10... | collective-permute-start | bytes 405512 | tf_op jit(solution)/shard_map/ppermute | solution.py:496
  147.7 5.5 %collective-permute-done.16.refs_8_ = f32[264,128]{1,0:T(8,128)S(1)} collective-permute-done((f32[264,128]{1,0:T(8,128)S(1)}, f32[264,128]{1,0:T(8,128)S(1)}, u32[]{:S(2)}, u32[]{:S(2)}) %collective-permute-start.16) | collective-permute-done | bytes 135200 | tf_op jit(solution)/shard_map/ppermute | solution.py:496
  153.2 2.8 %all-to-all-start.2 = ((f32[32,64,128]{2,1,0:T(8,128)}), f32[32,64,128]{2,1,0:T(8,128)S(1)}, u32[]{:S(2)}, u32[]{:S(2)}) async-start(f32[32,64,128]{2,1,0:T(8,128)} %get-tuple-element.65), calls=%async_computation.2 | async-start | bytes 2097152 | tf_op jit(solution)/shard_map/all_to_all | solution.py:562
  156.2 1.7 collective-permute-start.20
  160.9 2.3 %collective-permute-start.15 = (f32[264,128]{1,0:T(8,128)S(1)}, f32[264,128]{1,0:T(8,128)S(1)}, u32[]{:S(2)}, u32[]{:S(2)}) collective-permute-start(f32[264,128]{1,0:T(8,128)S(1)} %add_add_fusion.refs_0_), channel_id=1, source_target_pairs={{0,24},{8,0},{16,8},{24,16},{1,25},{9,1},{17,9},{25,17},{2,26},{10... | collective-permute-start | bytes 405512 | tf_op jit(solution)/shard_map/ppermute | solution.py:496
  163.4 17.6 %collective-permute-done.20.refs_4_ = f32[264,128]{1,0:T(8,128)S(1)} collective-permute-done((f32[264,128]{1,0:T(8,128)S(1)}, f32[264,128]{1,0:T(8,128)S(1)}, u32[]{:S(2)}, u32[]{:S(2)}) %collective-permute-start.20) | collective-permute-done | bytes 135200 | tf_op jit(solution)/shard_map/ppermute | solution.py:496
  187.2 1.6 collective-permute-start.25
  191.8 3.6 %collective-permute-done.19.refs_3_ = f32[264,128]{1,0:T(8,128)S(1)} collective-permute-done((f32[264,128]{1,0:T(8,128)S(1)}, f32[264,128]{1,0:T(8,128)S(1)}, u32[]{:S(2)}, u32[]{:S(2)}) %collective-permute-start.19) | collective-permute-done | bytes 135200 | tf_op jit(solution)/shard_map/ppermute | solution.py:501
  195.4 1.6 collective-permute-start.27
  197.6 1.5 collective-permute-start.23
  201.0 1.6 collective-permute-start.26
  203.5 1.5 collective-permute-start.29
  206.9 1.7 collective-permute-done.29.refs_15_
  210.0 2.3 %assemble.1 = (f32[768,1024]{1,0:T(8,128)}, f32[1024,256]{1,0:T(8,128)}, f32[2,8,128]{2,1,0:T(8,128)S(1)}) custom-call(f32[264,128]{1,0:T(8,128)S(1)} %add_add_fusion.refs_0_, f32[264,128]{1,0:T(8,128)S(1)} %collective-permute-done.17.refs_1_, f32[264,128]{1,0:T(8,128)S(1)} %collective-permute-done.18.refs_2_, ...), custom_call_target="tpu_custom_call" | custom-call | tf_op jit(solution)/shard_map/assemble/pallas_call | solution.py:476
  (124 shorter events, 43.5 us)
Async XLA Ops:
  7.6 59.0 %all-to-all-start = ((f32[32,136,128]{2,1,0:T(8,128)}), f32[32,136,128]{2,1,0:T(8,128)S(1)}, u32[]{:S(2)}, u32[]{:S(2)}) async-start(f32[32,136,128]{2,1,0:T(8,128)} %get-tuple-element.39), calls=%async_computation | async-start | bytes 4456448 | tf_op jit(solution)/shard_map/all_to_all | solution.py:550
  87.6 9.2 %collective-permute-start = (f32[4,264,128]{2,1,0:T(8,128)}, f32[4,264,128]{2,1,0:T(8,128)}, u32[]{:S(2)}, u32[]{:S(2)}) collective-permute-start(f32[4,264,128]{2,1,0:T(8,128)} %get-tuple-element.47), channel_id=1, source_target_pairs={{0,1},{1,0},{2,3},{3,2},{4,5},{5,4},{6,7},{7,6},{8,9},{9,8},{10,11... | collective-permute-start | bytes 1622024 | tf_op jit(solution)/shard_map/ppermute | solution.py:501
  87.7 12.0 %collective-permute-start.3 = (f32[4,264,128]{2,1,0:T(8,128)}, f32[4,264,128]{2,1,0:T(8,128)}, u32[]{:S(2)}, u32[]{:S(2)}) collective-permute-start(f32[4,264,128]{2,1,0:T(8,128)} %get-tuple-element.49), channel_id=1, source_target_pairs={{0,1},{1,0},{2,3},{3,2},{4,5},{5,4},{6,7},{7,6},{8,9},{9,8},{10,11... | collective-permute-start | bytes 1622024 | tf_op jit(solution)/shard_map/ppermute | solution.py:501
  88.2 14.0 %collective-permute-start.6 = (f32[4,264,128]{2,1,0:T(8,128)}, f32[4,264,128]{2,1,0:T(8,128)}, u32[]{:S(2)}, u32[]{:S(2)}) collective-permute-start(f32[4,264,128]{2,1,0:T(8,128)} %get-tuple-element.51), channel_id=1, source_target_pairs={{0,1},{1,0},{2,3},{3,2},{4,5},{5,4},{6,7},{7,6},{8,9},{9,8},{10,11... | collective-permute-start | bytes 1622024 | tf_op jit(solution)/shard_map/ppermute | solution.py:501
  88.2 15.5 %collective-permute-start.9 = (f32[4,264,128]{2,1,0:T(8,128)}, f32[4,264,128]{2,1,0:T(8,128)}, u32[]{:S(2)}, u32[]{:S(2)}) collective-permute-start(f32[4,264,128]{2,1,0:T(8,128)} %get-tuple-element.53), channel_id=1, source_target_pairs={{0,1},{1,0},{2,3},{3,2},{4,5},{5,4},{6,7},{7,6},{8,9},{9,8},{10,11... | collective-permute-start | bytes 1622024 | tf_op jit(solution)/shard_map/ppermute | solution.py:501
  92.8 38.9 %all-to-all-start.1 = ((f32[32,64,128]{2,1,0:T(8,128)}), f32[32,64,128]{2,1,0:T(8,128)S(1)}, u32[]{:S(2)}, u32[]{:S(2)}) async-start(f32[32,64,128]{2,1,0:T(8,128)} %get-tuple-element.56), calls=%async_computation.1 | async-start | bytes 2097152 | tf_op jit(solution)/shard_map/all_to_all | solution.py:562
  97.8 17.9 %collective-permute-start.1 = (f32[2,264,128]{2,1,0:T(8,128)S(1)}, f32[2,264,128]{2,1,0:T(8,128)S(1)}, u32[]{:S(2)}, u32[]{:S(2)}) collective-permute-start(f32[2,264,128]{2,1,0:T(8,128)S(1)} %slice_add_fusion.8), channel_id=1, source_target_pairs={{0,2},{2,0},{1,3},{3,1},{4,6},{6,4},{5,7},{7,5},{8,10},{10,8},{9,1... | collective-permute-start | bytes 811016 | tf_op jit(solution)/shard_map/ppermute | solution.py:501
  100.6 17.3 %collective-permute-start.4 = (f32[2,264,128]{2,1,0:T(8,128)S(1)}, f32[2,264,128]{2,1,0:T(8,128)S(1)}, u32[]{:S(2)}, u32[]{:S(2)}) collective-permute-start(f32[2,264,128]{2,1,0:T(8,128)S(1)} %slice_add_fusion.6), channel_id=1, source_target_pairs={{0,4},{4,0},{1,5},{5,1},{2,6},{6,2},{3,7},{7,3},{8,12},{12,8},{9,1... | collective-permute-start | bytes 811016 | tf_op jit(solution)/shard_map/ppermute | solution.py:501
  103.2 19.8 %collective-permute-start.7 = (f32[2,264,128]{2,1,0:T(8,128)S(1)}, f32[2,264,128]{2,1,0:T(8,128)S(1)}, u32[]{:S(2)}, u32[]{:S(2)}) collective-permute-start(f32[2,264,128]{2,1,0:T(8,128)S(1)} %slice_add_fusion.4), channel_id=1, source_target_pairs={{0,2},{2,0},{1,3},{3,1},{4,6},{6,4},{5,7},{7,5},{8,10},{10,8},{9,1... | collective-permute-start | bytes 811016 | tf_op jit(solution)/shard_map/ppermute | solution.py:501
  104.8 20.7 %collective-permute-start.10 = (f32[2,264,128]{2,1,0:T(8,128)S(1)}, f32[2,264,128]{2,1,0:T(8,128)S(1)}, u32[]{:S(2)}, u32[]{:S(2)}) collective-permute-start(f32[2,264,128]{2,1,0:T(8,128)S(1)} %slice_add_fusion.2), channel_id=1, source_target_pairs={{0,4},{4,0},{1,5},{5,1},{2,6},{6,2},{3,7},{7,3},{8,12},{12,8},{9,1... | collective-permute-start | bytes 811016 | tf_op jit(solution)/shard_map/ppermute | solution.py:501
  116.8 10.4 %collective-permute-start.2 = (f32[264,128]{1,0:T(8,128)S(1)}, f32[264,128]{1,0:T(8,128)S(1)}, u32[]{:S(2)}, u32[]{:S(2)}) collective-permute-start(f32[264,128]{1,0:T(8,128)S(1)} %slice_bitcast_fusion.6), channel_id=1, source_target_pairs={{0,4},{4,0},{1,5},{5,1},{2,6},{6,2},{3,7},{7,3},{8,12},{12,8},{9,1... | collective-permute-start | bytes 405512 | tf_op jit(solution)/shard_map/ppermute | solution.py:501
  119.0 8.2 %collective-permute-start.5 = (f32[264,128]{1,0:T(8,128)S(1)}, f32[264,128]{1,0:T(8,128)S(1)}, u32[]{:S(2)}, u32[]{:S(2)}) collective-permute-start(f32[264,128]{1,0:T(8,128)S(1)} %slice_bitcast_fusion.4), channel_id=1, source_target_pairs={{0,2},{2,0},{1,3},{3,1},{4,6},{6,4},{5,7},{7,5},{8,10},{10,8},{9,1... | collective-permute-start | bytes 405512 | tf_op jit(solution)/shard_map/ppermute | solution.py:501
  131.6 7.1 %collective-permute-start.12 = (f32[264,128]{1,0:T(8,128)S(1)}, f32[264,128]{1,0:T(8,128)S(1)}, u32[]{:S(2)}, u32[]{:S(2)}) collective-permute-start(f32[264,128]{1,0:T(8,128)S(1)} %fusion.18), channel_id=1, source_target_pairs={{0,24},{8,0},{16,8},{24,16},{1,25},{9,1},{17,9},{25,17},{2,26},{10... | collective-permute-start | bytes 405512 | tf_op jit(solution)/shard_map/ppermute | solution.py:496
  134.7 10.7 %collective-permute-start.13 = (f32[264,128]{1,0:T(8,128)S(1)}, f32[264,128]{1,0:T(8,128)S(1)}, u32[]{:S(2)}, u32[]{:S(2)}) collective-permute-start(f32[264,128]{1,0:T(8,128)S(1)} %fusion.19), channel_id=1, source_target_pairs={{0,16},{8,24},{16,0},{24,8},{1,17},{9,25},{17,1},{25,9},{2,18},{10... | collective-permute-start | bytes 405512 | tf_op jit(solution)/shard_map/ppermute | solution.py:496
  134.7 10.7 %collective-permute-start.14 = (f32[264,128]{1,0:T(8,128)S(1)}, f32[264,128]{1,0:T(8,128)S(1)}, u32[]{:S(2)}, u32[]{:S(2)}) collective-permute-start(f32[264,128]{1,0:T(8,128)S(1)} %fusion.20), channel_id=1, source_target_pairs={{0,8},{8,16},{16,24},{24,0},{1,9},{9,17},{17,25},{25,1},{2,10},{10... | collective-permute-start | bytes 405512 | tf_op jit(solution)/shard_map/ppermute | solution.py:496
  145.5 7.7 %collective-permute-start.16 = (f32[264,128]{1,0:T(8,128)S(1)}, f32[264,128]{1,0:T(8,128)S(1)}, u32[]{:S(2)}, u32[]{:S(2)}) collective-permute-start(f32[264,128]{1,0:T(8,128)S(1)} %add_add_fusion.refs_0_), channel_id=1, source_target_pairs={{0,16},{8,24},{16,0},{24,8},{1,17},{9,25},{17,1},{25,9},{2,18},{10... | collective-permute-start | bytes 405512 | tf_op jit(solution)/shard_map/ppermute | solution.py:496
  153.2 60.2 %all-to-all-start.2 = ((f32[32,64,128]{2,1,0:T(8,128)}), f32[32,64,128]{2,1,0:T(8,128)S(1)}, u32[]{:S(2)}, u32[]{:S(2)}) async-start(f32[32,64,128]{2,1,0:T(8,128)} %get-tuple-element.65), calls=%async_computation.2 | async-start | bytes 2097152 | tf_op jit(solution)/shard_map/all_to_all | solution.py:562
  156.0 24.9 %collective-permute-start.30 = (f32[264,128]{1,0:T(8,128)S(1)}, f32[264,128]{1,0:T(8,128)S(1)}, u32[]{:S(2)}, u32[]{:S(2)}) collective-permute-start(f32[264,128]{1,0:T(8,128)S(1)} %add_add_fusion.refs_0_), channel_id=1, source_target_pairs={{0,1},{1,0},{2,3},{3,2},{4,5},{5,4},{6,7},{7,6},{8,9},{9,8},{10,11... | collective-permute-start | bytes 405512 | tf_op jit(solution)/shard_map/ppermute | solution.py:501
  156.2 24.8 %collective-permute-start.20 = (f32[264,128]{1,0:T(8,128)S(1)}, f32[264,128]{1,0:T(8,128)S(1)}, u32[]{:S(2)}, u32[]{:S(2)}) collective-permute-start(f32[264,128]{1,0:T(8,128)S(1)} %add_add_fusion.refs_0_), channel_id=1, source_target_pairs={{0,8},{8,16},{16,24},{24,0},{1,9},{9,17},{17,25},{25,1},{2,10},{10... | collective-permute-start | bytes 405512 | tf_op jit(solution)/shard_map/ppermute | solution.py:496
  157.9 24.5 %collective-permute-start.18 = (f32[264,128]{1,0:T(8,128)S(1)}, f32[264,128]{1,0:T(8,128)S(1)}, u32[]{:S(2)}, u32[]{:S(2)}) collective-permute-start(f32[264,128]{1,0:T(8,128)S(1)} %add_add_fusion.refs_0_), channel_id=1, source_target_pairs={{0,2},{2,0},{1,3},{3,1},{4,6},{6,4},{5,7},{7,5},{8,10},{10,8},{9,1... | collective-permute-start | bytes 405512 | tf_op jit(solution)/shard_map/ppermute | solution.py:501
  159.4 24.5 %collective-permute-start.17 = (f32[264,128]{1,0:T(8,128)S(1)}, f32[264,128]{1,0:T(8,128)S(1)}, u32[]{:S(2)}, u32[]{:S(2)}) collective-permute-start(f32[264,128]{1,0:T(8,128)S(1)} %add_add_fusion.refs_0_), channel_id=1, source_target_pairs={{0,4},{4,0},{1,5},{5,1},{2,6},{6,2},{3,7},{7,3},{8,12},{12,8},{9,1... | collective-permute-start | bytes 405512 | tf_op jit(solution)/shard_map/ppermute | solution.py:501
  160.9 23.0 %collective-permute-start.15 = (f32[264,128]{1,0:T(8,128)S(1)}, f32[264,128]{1,0:T(8,128)S(1)}, u32[]{:S(2)}, u32[]{:S(2)}) collective-permute-start(f32[264,128]{1,0:T(8,128)S(1)} %add_add_fusion.refs_0_), channel_id=1, source_target_pairs={{0,24},{8,0},{16,8},{24,16},{1,25},{9,1},{17,9},{25,17},{2,26},{10... | collective-permute-start | bytes 405512 | tf_op jit(solution)/shard_map/ppermute | solution.py:496
  181.0 6.2 %collective-permute-start.22 = (f32[264,128]{1,0:T(8,128)S(1)}, f32[264,128]{1,0:T(8,128)S(1)}, u32[]{:S(2)}, u32[]{:S(2)}) collective-permute-start(f32[264,128]{1,0:T(8,128)S(1)} %collective-permute-done.20.refs_4_), channel_id=1, source_target_pairs={{0,4},{4,0},{1,5},{5,1},{2,6},{6,2},{3,7},{7,3},{8,12},{12,8},{9,1... | collective-permute-start | bytes 405512 | tf_op jit(solution)/shard_map/ppermute | solution.py:501
  182.5 6.3 %collective-permute-start.21 = (f32[264,128]{1,0:T(8,128)S(1)}, f32[264,128]{1,0:T(8,128)S(1)}, u32[]{:S(2)}, u32[]{:S(2)}) collective-permute-start(f32[264,128]{1,0:T(8,128)S(1)} %collective-permute-done.20.refs_4_), channel_id=1, source_target_pairs={{0,2},{2,0},{1,3},{3,1},{4,6},{6,4},{5,7},{7,5},{8,10},{10,8},{9,1... | collective-permute-start | bytes 405512 | tf_op jit(solution)/shard_map/ppermute | solution.py:501
  184.0 6.3 %collective-permute-start.32 = (f32[264,128]{1,0:T(8,128)S(1)}, f32[264,128]{1,0:T(8,128)S(1)}, u32[]{:S(2)}, u32[]{:S(2)}) collective-permute-start(f32[264,128]{1,0:T(8,128)S(1)} %collective-permute-done.18.refs_2_), channel_id=1, source_target_pairs={{0,1},{1,0},{2,3},{3,2},{4,5},{5,4},{6,7},{7,6},{8,9},{9,8},{10,11... | collective-permute-start | bytes 405512 | tf_op jit(solution)/shard_map/ppermute | solution.py:501
  184.0 7.1 %collective-permute-start.31 = (f32[264,128]{1,0:T(8,128)S(1)}, f32[264,128]{1,0:T(8,128)S(1)}, u32[]{:S(2)}, u32[]{:S(2)}) collective-permute-start(f32[264,128]{1,0:T(8,128)S(1)} %collective-permute-done.17.refs_1_), channel_id=1, source_target_pairs={{0,1},{1,0},{2,3},{3,2},{4,5},{5,4},{6,7},{7,6},{8,9},{9,8},{10,11... | collective-permute-start | bytes 405512 | tf_op jit(solution)/shard_map/ppermute | solution.py:501
  186.0 11.0 %collective-permute-start.38 = (f32[264,128]{1,0:T(8,128)S(1)}, f32[264,128]{1,0:T(8,128)S(1)}, u32[]{:S(2)}, u32[]{:S(2)}) collective-permute-start(f32[264,128]{1,0:T(8,128)S(1)} %collective-permute-done.16.refs_8_), channel_id=1, source_target_pairs={{0,1},{1,0},{2,3},{3,2},{4,5},{5,4},{6,7},{7,6},{8,9},{9,8},{10,11... | collective-permute-start | bytes 405512 | tf_op jit(solution)/shard_map/ppermute | solution.py:501
  187.2 9.8 %collective-permute-start.25 = (f32[264,128]{1,0:T(8,128)S(1)}, f32[264,128]{1,0:T(8,128)S(1)}, u32[]{:S(2)}, u32[]{:S(2)}) collective-permute-start(f32[264,128]{1,0:T(8,128)S(1)} %collective-permute-done.16.refs_8_), channel_id=1, source_target_pairs={{0,2},{2,0},{1,3},{3,1},{4,6},{6,4},{5,7},{7,5},{8,10},{10,8},{9,1... | collective-permute-start | bytes 405512 | tf_op jit(solution)/shard_map/ppermute | solution.py:501
  188.8 8.7 %collective-permute-start.24 = (f32[264,128]{1,0:T(8,128)S(1)}, f32[264,128]{1,0:T(8,128)S(1)}, u32[]{:S(2)}, u32[]{:S(2)}) collective-permute-start(f32[264,128]{1,0:T(8,128)S(1)} %collective-permute-done.16.refs_8_), channel_id=1, source_target_pairs={{0,4},{4,0},{1,5},{5,1},{2,6},{6,2},{3,7},{7,3},{8,12},{12,8},{9,1... | collective-permute-start | bytes 405512 | tf_op jit(solution)/shard_map/ppermute | solution.py:501
  191.0 6.5 %collective-permute-start.28 = (f32[264,128]{1,0:T(8,128)S(1)}, f32[264,128]{1,0:T(8,128)S(1)}, u32[]{:S(2)}, u32[]{:S(2)}) collective-permute-start(f32[264,128]{1,0:T(8,128)S(1)} %collective-permute-done.15.refs_12_), channel_id=1, source_target_pairs={{0,4},{4,0},{1,5},{5,1},{2,6},{6,2},{3,7},{7,3},{8,12},{12,8},{9,1... | collective-permute-start | bytes 405512 | tf_op jit(solution)/shard_map/ppermute | solution.py:501
  197.6 5.9 %collective-permute-start.23 = (f32[264,128]{1,0:T(8,128)S(1)}, f32[264,128]{1,0:T(8,128)S(1)}, u32[]{:S(2)}, u32[]{:S(2)}) collective-permute-start(f32[264,128]{1,0:T(8,128)S(1)} %collective-permute-done.21.refs_5_), channel_id=1, source_target_pairs={{0,4},{4,0},{1,5},{5,1},{2,6},{6,2},{3,7},{7,3},{8,12},{12,8},{9,1... | collective-permute-start | bytes 405512 | tf_op jit(solution)/shard_map/ppermute | solution.py:501
  201.0 5.9 %collective-permute-start.26 = (f32[264,128]{1,0:T(8,128)S(1)}, f32[264,128]{1,0:T(8,128)S(1)}, u32[]{:S(2)}, u32[]{:S(2)}) collective-permute-start(f32[264,128]{1,0:T(8,128)S(1)} %collective-permute-done.24.refs_9_), channel_id=1, source_target_pairs={{0,2},{2,0},{1,3},{3,1},{4,6},{6,4},{5,7},{7,5},{8,10},{10,8},{9,1... | collective-permute-start | bytes 405512 | tf_op jit(solution)/shard_map/ppermute | solution.py:501
  (30 other events, 153.2 us)

commit v4 on v3

--- a/solution.py
+++ b/solution.py
@@ -103,7 +103,7 @@
 
 
 def pick_kernel(capacity, incoming_hbm, parts_hbm, *refs):
-    out_refs, (wanted_ref, asked_ref, parts_ref, sems) = refs[:-4], refs[-4:]
+    out_ref, wanted_ref, asked_ref, parts_ref, sems = refs
     devices = asked_ref.shape[0]
     rows, both = parts_ref.shape
     width = both // 2
@@ -122,7 +122,7 @@
         join_wanted(capacity, asked_ref, wanted_ref)
         more.wait()
 
-    tile = out_refs[0].shape[0] * capacity
+    tile = out_ref.shape[0] * capacity
     lane = lax.broadcasted_iota(jnp.int32, (LANES, LANES), 1).astype(jnp.float32)
     choosers = []
     for start in range(0, tile, LANES):
@@ -137,22 +137,20 @@
         ))
     value = dot(jnp.concatenate(choosers, axis=0), parts_ref[...])
     value = value[:, :width] + value[:, width:]
-    for j, out_ref in enumerate(out_refs):
-        for k in range(out_ref.shape[0]):
-            out_ref[k] = value[k * capacity : (k + 1) * capacity, j * LANES : (j + 1) * LANES]
+    for k in range(out_ref.shape[0]):
+        out_ref[k] = value[k * capacity : (k + 1) * capacity]
 
 
 def pick_rows(capacity, incoming, parts):
     devices = incoming.shape[0]
     rows, both = parts.shape
     steps = 4
-    blocks = both // 2 // LANES
     return pl.pallas_call(
         functools.partial(pick_kernel, capacity),
         grid=(steps,),
         in_specs=[pl.BlockSpec(memory_space=pl.ANY)] * 2,
-        out_specs=[pl.BlockSpec((devices // steps, capacity, LANES), lambda i: (i, 0, 0))] * blocks,
-        out_shape=[jax.ShapeDtypeStruct((devices, capacity, LANES), jnp.float32)] * blocks,
+        out_specs=pl.BlockSpec((devices // steps, capacity, both // 2), lambda i: (i, 0, 0)),
+        out_shape=jax.ShapeDtypeStruct((devices, capacity, both // 2), jnp.float32),
         scratch_shapes=[
             pltpu.VMEM((EXTRA, devices * capacity), jnp.float32),
             pltpu.VMEM((devices, EXTRA, LANES), jnp.float32),
@@ -164,7 +162,7 @@
             bytes_accessed=4 * devices * capacity * both,
             transcendentals=0,
         ),
-        compiler_params=pltpu.CompilerParams(vmem_limit_bytes=24 * 2**20),
+        compiler_params=pltpu.CompilerParams(vmem_limit_bytes=60 * 2**20),
         name="pick_rows",
     )(incoming, parts)
 
@@ -418,64 +416,51 @@
             bytes_accessed=16 * rows * hidden_size,
             transcendentals=0,
         ),
-        compiler_params=pltpu.CompilerParams(vmem_limit_bytes=40 * 2**20),
+        compiler_params=pltpu.CompilerParams(vmem_limit_bytes=60 * 2**20),
         name="backward",
     )(*operands)
 
 
-def assemble_kernel(sizes, *refs):
-    outer, inner, chip, core = sizes
-    devices = outer * inner * chip * core
-    pieces, (weight_in, weight_out, biases, sems, bias_sem) = refs[:devices], refs[devices:]
-    length = pieces[0].shape[0] - EXTRA
+def assemble_kernel(outer, total_hbm, weight_in, weight_out, biases, held, in_sem, out_sem):
+    devices, length = held.shape[0], held.shape[1] - EXTRA
     dim_in, hidden_size = weight_in.shape
     band = hidden_size // outer
     base = band // LANES * dim_in
-    first = lax.axis_index("outer")
-    plane = lax.axis_index("inner") * chip + lax.axis_index("chip")
-    me = lax.axis_index("core")
+    loads = [
+        pltpu.make_async_copy(total_hbm.at[d], held.at[d], in_sem.at[d]) for d in range(devices)
+    ]
+    for load in loads:
+        load.start()
     copies = []
-    for n, piece in enumerate(pieces):
-        c, n = divmod(n, devices // core)
-        k, j = divmod(n, inner * chip)
-        n += c * (devices // core)
-        o = lax.rem(first + outer - k, outer)
-        e = lax.bitwise_xor(plane, place(sizes, k, j)) * core + lax.bitwise_xor(me, c)
-        at = e * length
-        source = piece.at[pl.ds(0, length)]
-
-        def copy_to(target, row, column):
-            rows = pl.ds(pl.multiple_of(row, length), length)
-            lanes = pl.ds(pl.multiple_of(column * LANES, LANES), LANES)
-            return pltpu.make_async_copy(source, target.at[rows, lanes], sems.at[n])
-
-        @pl.when(at < base)
-        def _():
-            column = o * (band // LANES) + lax.div(at, dim_in)
-            copy_to(weight_in, lax.rem(at, dim_in), column).start()
-
-        @pl.when(at >= base)
-        def _():
-            copy_to(weight_out, o * band + lax.rem(at - base, band), lax.div(at - base, band)).start()
-
-        @pl.when((o == 0) & (e < 2))
-        def _():
-            copy = pltpu.make_async_copy(
-                piece.at[pl.ds(length, EXTRA)], biases.at[jnp.minimum(e, 1)], bias_sem
-            )
-            copy.start()
-            copy.wait()
-
-        copies.append(copy_to(weight_in, 0, 0))
+    for d in range(devices):
+        o, at = divmod(d * length, devices // outer * length)
+        if at < base:
+            target, column, row = weight_in, o * (band // LANES) + at // dim_in, at % dim_in
+        else:
+            column, row = divmod(at - base, band)
+            target, row = weight_out, o * band + row
+        loads[d].wait()
+        copies.append(pltpu.make_async_copy(
+            held.at[d, pl.ds(0, length)],
+            target.at[pl.ds(row, length), pl.ds(column * LANES, LANES)],
+            out_sem.at[d],
+        ))
+        copies[-1].start()
+        if d < 2:
+            copies.append(pltpu.make_async_copy(
+                held.at[d, pl.ds(length, EXTRA)], biases.at[d], out_sem.at[devices + d]
+            ))
+            copies[-1].start()
     for copy in copies:
         copy.wait()
 
 
-def assemble(sizes, pieces, dim_in, hidden_size, width):
+def assemble(outer, total, dim_in, hidden_size, width):
     hbm = pl.BlockSpec(memory_space=pl.ANY)
+    devices = total.shape[0]
     return pl.pallas_call(
-        functools.partial(assemble_kernel, sizes),
-        in_specs=[hbm] * len(pieces),
+        functools.partial(assemble_kernel, outer),
+        in_specs=[hbm],
         out_specs=[hbm] * 3,
         out_shape=[
             jax.ShapeDtypeStruct((dim_in, hidden_size), jnp.float32),
@@ -483,12 +468,13 @@
             jax.ShapeDtypeStruct((2, EXTRA, LANES), jnp.float32),
         ],
         scratch_shapes=[
-            pltpu.SemaphoreType.DMA((len(pieces),)),
-            pltpu.SemaphoreType.DMA,
-        ],
-        compiler_params=pltpu.CompilerParams(vmem_limit_bytes=4 * 2**20),
+            pltpu.VMEM(total.shape, jnp.float32),
+            pltpu.SemaphoreType.DMA((devices,)),
+            pltpu.SemaphoreType.DMA((devices + 2,)),
+        ],
+        compiler_params=pltpu.CompilerParams(vmem_limit_bytes=60 * 2**20),
         name="assemble",
-    )(*pieces)
+    )(total)
 
 
 def along(sizes, x, k):
@@ -501,7 +487,7 @@
     return lax.ppermute(x, axis, [(p, p ^ j) for p in range(size)])
 
 
-def sum_chunks(sizes, mine, theirs, first_answers):
+def sum_chunks(sizes, mine, theirs, answers):
     outer, inner, chip, _ = sizes
     chunks = [None] * outer
     for k in range(outer - 1, -1, -1):
@@ -515,24 +501,11 @@
         chunks[k] = part[0]
         for j in range(1, low):
             chunks[k] = chunks[k] + across(sizes, fast, part[j], j)
-    chunks, first_answers = lax.optimization_barrier((chunks, first_answers))
+    chunks, answers = lax.optimization_barrier((chunks, answers))
     total = chunks[0]
     for k in range(outer - 1, 0, -1):
         total = total + along(sizes, chunks[k], k)
-    return total, first_answers
-
-
-def spread_chunks(sizes, total, second):
-    outer, inner, chip, _ = sizes
-    near = []
-    lines = [along(sizes, total, k) if k else total for k in range(outer)]
-    lines[outer // 2], second = lax.optimization_barrier((lines[outer // 2], second))
-    for k, x in enumerate(lines):
-        slow, fast = ("inner", "chip") if k % 2 else ("chip", "inner")
-        row = [across(sizes, fast, x, j) if j else x for j in range(sizes[AXES.index(fast)])]
-        for j in range(sizes[AXES.index(slow)]):
-            near += [across(sizes, slow, x, j) if j else x for x in row]
-    return near, second
+    return total, answers
 
 
 def per_device(
@@ -557,25 +530,17 @@
     )
     mine, theirs = list(pieces[:outer]), list(pieces[outer:])
     theirs[0], incoming = lax.optimization_barrier((theirs[0], incoming))
-
-    def exchange(x):
-        x = lax.all_to_all(x, AXES, split_axis=0, concat_axis=0, tiled=True)
-        return x.reshape(-1, x.shape[-1])
-
     picked = pick_rows(capacity, incoming, parts)
-    total, first = sum_chunks(sizes, mine, theirs, exchange(picked[0]))
-    near, second = spread_chunks(sizes, total, list(picked[1:]))
+    answers = lax.all_to_all(picked, AXES, split_axis=0, concat_axis=0, tiled=True)
+
+    total, answers = sum_chunks(sizes, mine, theirs, answers)
+    total = lax.all_gather(total[None], AXES, axis=0, tiled=True)
+    gw_in, gw_out, biases = assemble(outer, total, dim_in, hidden_size, width)
 
     slot_ids = jnp.arange(devices * capacity, dtype=jnp.int32)
-    from_slot = (slots.reshape(-1, 1) == slot_ids[None, :]).astype(jnp.bfloat16)
-    first = pick(from_slot, first)
-    late = len(near) - inner * chip
-    near[late], first = lax.optimization_barrier((near[late], first))
-    chosen = jnp.concatenate([first] + [pick(from_slot, exchange(x)) for x in second], axis=1)
+    from_slot = slots.reshape(-1, 1) == slot_ids[None, :]
+    chosen = pick(from_slot.astype(jnp.bfloat16), answers.reshape(-1, width))
     latent_grad = cotangent - 0.25 * (chosen - latents)
-
-    chunks = near + [across(sizes, "core", x, 1) for x in near]
-    gw_in, gw_out, biases = assemble(sizes, chunks, dim_in, hidden_size, width)
     biases = biases.reshape(-1)
     gb_in, gb_out = biases[:hidden_size], biases[hidden_size : hidden_size + width]
     return (latent_grad, gw_in, gb_in, gw_out, gb_out)

time: 222 us -> 238 us (1.072); the launches traced: 218 us -> 237 us
  waiting for transfers between devices: 104 us -> 147 us
  starting transfers between devices: 53.8 us -> 23.9 us
  between operations: 0.98 us -> 14.2 us
  local copies, waits for them, and re-layouts: 8.69 us -> 5.31 us
  other arithmetic: 9.76 us -> 6.7 us
    all_gather x0 -> x1, waiting for transfers between devices: none -> 58.3 us  [per_device(): total = lax.all_gather(total[None], AXES, axis=0, tiled=True)]
    ppermute x6 -> x3, waiting for transfers between devices: 32.4 us -> 11.4 us  [along(): lax.ppermute(x, 'outer', [(o, (o + k) % outer) for o in range(outer)])]
    ppermute x40 -> x12, starting transfers between devices: 29 us -> 10.1 us  [across(): return lax.ppermute(x, axis, [(p, p ^ j) for p in range(size)])]
    ppermute x6 -> x3, starting transfers between devices: 10.7 us -> 2.27 us  [along(): lax.ppermute(x, 'outer', [(o, (o + k) % outer) for o in range(outer)])]
    all_to_all x2 -> x1, waiting for transfers between devices: 0.01 us -> 8.14 us  [per_device(): lax.all_to_all(picked, AXES, split_axis=0, concat_axis=0, tiled=True)]
    unnamed x27 -> x19, local copies, waits for them, and re-layouts: 7.49 us -> 2.76 us
    add x8, other arithmetic: 8.02 us -> 4.35 us  [sum_chunks(): part = part + across(sizes, slow, mine[k][here] + arrived[here], j)]
    pallas_call x1, Pallas kernels: 15.6 us -> 12.8 us  [backward(): pl.pallas_call(functools.partial(backward_kernel, sizes, capacity), in_sp...]
  transfers between devices with their start and end apart: 49 -> 18, of which waited for: 16 -> 10; matrix products, arithmetic and copies ran while one was open for 6% -> 4% of each run, Pallas kernels for 7% -> 6%
where the time goes in v4:
time: 238 us; the launch traced here: 237 us
  waiting for transfers between devices  147 us (62%)
  Pallas kernels  38.1 us (16%)
  starting transfers between devices  23.9 us (10%)
  between operations  14.2 us (6%)
  other arithmetic  6.7 us (3%)
  local copies, waits for them, and re-layouts  5.31 us (2%)
    all_gather x1, waiting for transfers between devices, per_device(): total = lax.all_gather(total[None], AXES, axis=0, tiled=True)  58.3 us
    all_to_all x1, waiting for transfers between devices, per_device(): lax.all_to_all(outgoing, AXES, split_axis=0, concat_axis=0, tiled=True)  42.3 us
    ppermute x12, waiting for transfers between devices, across(): return lax.ppermute(x, axis, [(p, p ^ j) for p in range(size)])  26.6 us
    pallas_call x1, Pallas kernels, backward(): pl.pallas_call(functools.partial(backward_kernel, sizes, capacity), in_sp...  12.8 us
    ppermute x3, waiting for transfers between devices, along(): lax.ppermute(x, 'outer', [(o, (o + k) % outer) for o in range(outer)])  11.4 us
    ppermute x12, starting transfers between devices, across(): return lax.ppermute(x, axis, [(p, p ^ j) for p in range(size)])  10.1 us
    pallas_call x1, Pallas kernels, forward(): pl.pallas_call(forward_kernel, grid=(rows // tile,), in_specs=[pl.BlockSp...  8.4 us
    all_to_all x1, waiting for transfers between devices, per_device(): lax.all_to_all(picked, AXES, split_axis=0, concat_axis=0, tiled=True)  8.14 us
  transfers between devices with their start and end apart: 18, of which 10 were waited for; matrix products, arithmetic and copies ran while one was open for 4% of the time, Pallas kernels for 6%

profile of v4, /device:TPU:0, one launch (start us, length us, event | category | flops | bytes accessed | tf_op | source)
XLA Modules:
  0.0 237.3 jit_solution(8295881684503662116)
XLA Ops:
  7.2 7.0 %route.1 = (f32[32,136,128]{2,1,0:T(8,128)}, s32[1,1024]{1,0:T(1,128)}) custom-call(s32[1,1024]{1,0:T(1,128)} %bitcast.39, s32[1,1024]{1,0:T(1,128)} %bitcast.40, f32[1024,256]{1,0:T(8,128)} %latents_hbm.1, f32[1024,256]{1,0:T(8,128)} %cotangent_hbm.1), custom_call_target="tpu_custom_call" | custom-call | tf_op jit(solution)/shard_map/route/pallas_call | solution.py:246
  14.2 7.3 %all-to-all-start = ((f32[32,136,128]{2,1,0:T(8,128)}), f32[32,136,128]{2,1,0:T(8,128)S(1)}, u32[]{:S(2)}, u32[]{:S(2)}) async-start(f32[32,136,128]{2,1,0:T(8,128)} %get-tuple-element.34), calls=%async_computation | async-start | bytes 4456448 | tf_op jit(solution)/shard_map/all_to_all | solution.py:523
  21.5 1.0 copy.14
  22.5 8.4 %forward.1 = (bf16[1024,1024]{1,0:T(8,128)(2,1)}, bf16[768,1024]{1,0:T(8,128)(2,1)}, f32[1024,1024]{1,0:T(8,128)}, f32[1024,256]{1,0:T(8,128)}, bf16[1024,512]{1,0:T(8,128)(2,1)}) custom-call(bf16[1024,768]{1,0:T(8,128)(2,1)} %codebook_ref.1, bf16[768,1024]{1,0:T(8,128)(2,1)} %weight_in_ref.1, f32[1,1024]{1,0:T(1,128)} %bitcast.42, ...), custom_call_target="tpu_custom_call" | custom-call | flops 2147483648 | bytes 14680064 | tf_op jit(solution)/shard_map/forward/pallas_call | solution.py:62
  30.9 42.3 %all-to-all-done.incoming_hbm = f32[32,136,128]{2,1,0:T(8,128)S(1)} async-done(((f32[32,136,128]{2,1,0:T(8,128)}), f32[32,136,128]{2,1,0:T(8,128)S(1)}, u32[]{:S(2)}, u32[]{:S(2)}) %all-to-all-start) | async-done | bytes 2228256 | tf_op jit(solution)/shard_map/all_to_all | solution.py:523
  73.2 1.4 copy-done.2
  74.6 12.8 %backward.1 = (f32[4,264,128]{2,1,0:T(8,128)}, f32[4,264,128]{2,1,0:T(8,128)}, f32[4,264,128]{2,1,0:T(8,128)}, f32[4,264,128]{2,1,0:T(8,128)}, f32[4,264,128]{2,...) custom-call(f32[32,136,128]{2,1,0:T(8,128)} %copy-done.2, ...), custom_call_target="tpu_custom_call" | custom-call | flops 4831838208 | bytes 16777216 | tf_op jit(solution)/shard_map/backward/pallas_call | solution.py:395
  88.0 5.2 %pick_rows.1 = f32[32,64,256]{2,1,0:T(8,128)} custom-call(f32[32,136,128]{2,1,0:T(8,128)} %copy-done.2, bf16[1024,512]{1,0:T(8,128)(2,1)} %get-tuple-element.50.parts_hbm), custom_call_target="tpu_custom_call" | custom-call | flops 2147483648 | bytes 4194304 | tf_op jit(solution)/shard_map/pick_rows/pallas_call | solution.py:148
  93.2 4.0 %all-to-all-start.1 = ((f32[32,64,256]{2,1,0:T(8,128)}), f32[32,64,256]{2,1,0:T(8,128)S(1)}, u32[]{:S(2)}, u32[]{:S(2)}) async-start(f32[32,64,256]{2,1,0:T(8,128)} %pick_rows.1), calls=%async_computation.1 | async-start | bytes 4194304 | tf_op jit(solution)/shard_map/all_to_all | solution.py:534
  98.0 1.1 slice_add_fusion.7
  99.1 1.8 collective-permute-start.1
  101.0 1.1 slice_add_fusion.5
  102.0 1.5 collective-permute-start.4
  104.6 19.7 %collective-permute-done.1 = f32[2,264,128]{2,1,0:T(8,128)S(1)} collective-permute-done((f32[2,264,128]{2,1,0:T(8,128)S(1)}, f32[2,264,128]{2,1,0:T(8,128)S(1)}, u32[]{:S(2)}, u32[]{:S(2)}) %collective-permute-start.1) | collective-permute-done | bytes 270368 | tf_op jit(solution)/shard_map/ppermute | solution.py:487
  124.3 1.0 fusion.12
  125.3 1.9 collective-permute-start.2
  127.2 1.0 fusion.11
  128.8 3.0 %collective-permute-done.7 = f32[2,264,128]{2,1,0:T(8,128)S(1)} collective-permute-done((f32[2,264,128]{2,1,0:T(8,128)S(1)}, f32[2,264,128]{2,1,0:T(8,128)S(1)}, u32[]{:S(2)}, u32[]{:S(2)}) %collective-permute-start.7) | collective-permute-done | bytes 270368 | tf_op jit(solution)/shard_map/ppermute | solution.py:487
  131.9 0.8 collective-permute-start.8
  132.8 1.3 collective-permute-start.11
  134.2 3.7 %collective-permute-done.8 = f32[264,128]{1,0:T(8,128)S(1)} collective-permute-done((f32[264,128]{1,0:T(8,128)S(1)}, f32[264,128]{1,0:T(8,128)S(1)}, u32[]{:S(2)}, u32[]{:S(2)}) %collective-permute-start.8) | collective-permute-done | bytes 135200 | tf_op jit(solution)/shard_map/ppermute | solution.py:487
  138.1 8.1 %all-to-all-done.1 = f32[32,64,256]{2,1,0:T(8,128)S(1)} async-done(((f32[32,64,256]{2,1,0:T(8,128)}), f32[32,64,256]{2,1,0:T(8,128)S(1)}, u32[]{:S(2)}, u32[]{:S(2)}) %all-to-all-start.1) | async-done | bytes 2097184 | tf_op jit(solution)/shard_map/all_to_all | solution.py:534
  146.3 1.7 collective-permute-start.12
  148.5 4.0 %collective-permute-done.12 = f32[264,128]{1,0:T(8,128)S(1)} collective-permute-done((f32[264,128]{1,0:T(8,128)S(1)}, f32[264,128]{1,0:T(8,128)S(1)}, u32[]{:S(2)}, u32[]{:S(2)}) %collective-permute-start.12) | collective-permute-done | bytes 135200 | tf_op jit(solution)/shard_map/ppermute | solution.py:482
  152.5 7.4 %collective-permute-done.13 = f32[264,128]{1,0:T(8,128)S(1)} collective-permute-done((f32[264,128]{1,0:T(8,128)S(1)}, f32[264,128]{1,0:T(8,128)S(1)}, u32[]{:S(2)}, u32[]{:S(2)}) %collective-permute-start.13) | collective-permute-done | bytes 135200 | tf_op jit(solution)/shard_map/ppermute | solution.py:482
  159.9 0.7 add_add_fusion
  161.4 2.4 %fusion = f32[1024,512]{1,0:T(8,128)S(1)} fusion(s32[1024]{0:T(1024)S(1)} %bitcast.43, bf16[2048,256]{1,0:T(8,128)(2,1)S(1)} %get-tuple-element.60, bf16[2048,256]{1,0:T(8,128)(2,1)S(1)} %get-tuple-element.59), kind=kOutput, calls=%fused_computation.1 | convolution fusion | flops 2153775104 | bytes 4198400 | tf_op jit(solution)/shard_map/dot_general | solution.py:34
  163.8 1.2 fusion.8
  165.0 58.3 %all-gather.3.cloned.1.call-done = f32[8448,128]{1,0:T(8,128)} async-done(((f32[264,128]{1,0:T(8,128)}), f32[8448,128]{1,0:T(8,128)}) %all-gather.3.cloned.1.call-update) | async-done | bytes 4325392 | tf_op jit(solution)/shard_map/all_gather | solution.py:537
  223.3 4.7 %assemble.1 = (f32[768,1024]{1,0:T(8,128)}, f32[1024,256]{1,0:T(8,128)}, f32[2,8,128]{2,1,0:T(8,128)}) custom-call(f32[32,264,128]{2,1,0:T(8,128)} %bitcast.37), custom_call_target="tpu_custom_call" | custom-call | tf_op jit(solution)/shard_map/assemble/pallas_call | solution.py:461
  228.0 1.3 slice_bitcast_fusion.8
  229.3 1.2 slice.134
  (51 shorter events, 4.8 us)
Async XLA Ops:
  14.1 7.3 %copy-start.7 = (bf16[1024,256]{1,0:T(8,128)(2,1)S(1)}, bf16[1024,256]{1,0:T(8,128)(2,1)}, u32[]{:S(2)}) copy-start(bf16[1024,256]{1,0:T(8,128)(2,1)} %weight_out_ref.1) | copy-start | bytes 1572868
  14.2 59.0 %all-to-all-start = ((f32[32,136,128]{2,1,0:T(8,128)}), f32[32,136,128]{2,1,0:T(8,128)S(1)}, u32[]{:S(2)}, u32[]{:S(2)}) async-start(f32[32,136,128]{2,1,0:T(8,128)} %get-tuple-element.34), calls=%async_computation | async-start | bytes 4456448 | tf_op jit(solution)/shard_map/all_to_all | solution.py:523
  73.2 1.4 copy-start.2
  87.4 10.7 %collective-permute-start = (f32[4,264,128]{2,1,0:T(8,128)}, f32[4,264,128]{2,1,0:T(8,128)}, u32[]{:S(2)}, u32[]{:S(2)}) collective-permute-start(f32[4,264,128]{2,1,0:T(8,128)} %get-tuple-element.42), channel_id=1, source_target_pairs={{0,1},{1,0},{2,3},{3,2},{4,5},{5,4},{6,7},{7,6},{8,9},{9,8},{10,11... | collective-permute-start | bytes 1622024 | tf_op jit(solution)/shard_map/ppermute | solution.py:487
  87.5 13.5 %collective-permute-start.3 = (f32[4,264,128]{2,1,0:T(8,128)}, f32[4,264,128]{2,1,0:T(8,128)}, u32[]{:S(2)}, u32[]{:S(2)}) collective-permute-start(f32[4,264,128]{2,1,0:T(8,128)} %get-tuple-element.44), channel_id=1, source_target_pairs={{0,1},{1,0},{2,3},{3,2},{4,5},{5,4},{6,7},{7,6},{8,9},{9,8},{10,11... | collective-permute-start | bytes 1622024 | tf_op jit(solution)/shard_map/ppermute | solution.py:487
  93.2 10.4 %copy-start.4 = (f32[4,264,128]{2,1,0:T(8,128)S(1)}, f32[4,264,128]{2,1,0:T(8,128)}, u32[]{:S(2)}) copy-start(f32[4,264,128]{2,1,0:T(8,128)} %get-tuple-element.45) | copy-start | bytes 1622020
  93.2 53.1 %all-to-all-start.1 = ((f32[32,64,256]{2,1,0:T(8,128)}), f32[32,64,256]{2,1,0:T(8,128)S(1)}, u32[]{:S(2)}, u32[]{:S(2)}) async-start(f32[32,64,256]{2,1,0:T(8,128)} %pick_rows.1), calls=%async_computation.1 | async-start | bytes 4194304 | tf_op jit(solution)/shard_map/all_to_all | solution.py:534
  97.2 7.0 %copy-start.3 = (f32[4,264,128]{2,1,0:T(8,128)S(1)}, f32[4,264,128]{2,1,0:T(8,128)}, u32[]{:S(2)}) copy-start(f32[4,264,128]{2,1,0:T(8,128)} %get-tuple-element.47) | copy-start | bytes 1622020
  97.2 126.1 %all-gather.3.cloned.1.call-start = ((), (), s32[]{:S(2)}) async-start(), calls=%async_computation.2 | async-start | bytes 4460544 | tf_op jit(solution)/shard_map/all_gather | solution.py:537
  97.5 26.8 %copy-start.6 = (f32[4,264,128]{2,1,0:T(8,128)S(1)}, f32[4,264,128]{2,1,0:T(8,128)}, u32[]{:S(2)}) copy-start(f32[4,264,128]{2,1,0:T(8,128)} %get-tuple-element.40) | copy-start | bytes 1622020
  97.5 6.1 %collective-permute-start.6 = (f32[4,264,128]{2,1,0:T(8,128)}, f32[4,264,128]{2,1,0:T(8,128)S(1)}, u32[]{:S(2)}, u32[]{:S(2)}) collective-permute-start(f32[4,264,128]{2,1,0:T(8,128)} %get-tuple-element.46), channel_id=1, source_target_pairs={{0,1},{1,0},{2,3},{3,2},{4,5},{5,4},{6,7},{7,6},{8,9},{9,8},{10,11... | collective-permute-start | bytes 1622024 | tf_op jit(solution)/shard_map/ppermute | solution.py:487
  97.8 6.5 %collective-permute-start.9 = (f32[4,264,128]{2,1,0:T(8,128)}, f32[4,264,128]{2,1,0:T(8,128)S(1)}, u32[]{:S(2)}, u32[]{:S(2)}) collective-permute-start(f32[4,264,128]{2,1,0:T(8,128)} %get-tuple-element.48), channel_id=1, source_target_pairs={{0,1},{1,0},{2,3},{3,2},{4,5},{5,4},{6,7},{7,6},{8,9},{9,8},{10,11... | collective-permute-start | bytes 1622024 | tf_op jit(solution)/shard_map/ppermute | solution.py:487
  99.1 28.1 %copy-start.5 = (f32[4,264,128]{2,1,0:T(8,128)S(1)}, f32[4,264,128]{2,1,0:T(8,128)}, u32[]{:S(2)}) copy-start(f32[4,264,128]{2,1,0:T(8,128)} %get-tuple-element.43) | copy-start | bytes 1622020
  99.1 25.1 %collective-permute-start.1 = (f32[2,264,128]{2,1,0:T(8,128)S(1)}, f32[2,264,128]{2,1,0:T(8,128)S(1)}, u32[]{:S(2)}, u32[]{:S(2)}) collective-permute-start(f32[2,264,128]{2,1,0:T(8,128)S(1)} %slice_add_fusion.7), channel_id=1, source_target_pairs={{0,2},{2,0},{1,3},{3,1},{4,6},{6,4},{5,7},{7,5},{8,10},{10,8},{9,1... | collective-permute-start | bytes 811016 | tf_op jit(solution)/shard_map/ppermute | solution.py:487
  102.0 25.1 %collective-permute-start.4 = (f32[2,264,128]{2,1,0:T(8,128)S(1)}, f32[2,264,128]{2,1,0:T(8,128)S(1)}, u32[]{:S(2)}, u32[]{:S(2)}) collective-permute-start(f32[2,264,128]{2,1,0:T(8,128)S(1)} %slice_add_fusion.5), channel_id=1, source_target_pairs={{0,4},{4,0},{1,5},{5,1},{2,6},{6,2},{3,7},{7,3},{8,12},{12,8},{9,1... | collective-permute-start | bytes 811016 | tf_op jit(solution)/shard_map/ppermute | solution.py:487
  103.6 28.2 %collective-permute-start.7 = (f32[2,264,128]{2,1,0:T(8,128)S(1)}, f32[2,264,128]{2,1,0:T(8,128)S(1)}, u32[]{:S(2)}, u32[]{:S(2)}) collective-permute-start(f32[2,264,128]{2,1,0:T(8,128)S(1)} %slice_add_fusion.3), channel_id=1, source_target_pairs={{0,2},{2,0},{1,3},{3,1},{4,6},{6,4},{5,7},{7,5},{8,10},{10,8},{9,1... | collective-permute-start | bytes 811016 | tf_op jit(solution)/shard_map/ppermute | solution.py:487
  104.3 28.4 %collective-permute-start.10 = (f32[2,264,128]{2,1,0:T(8,128)S(1)}, f32[2,264,128]{2,1,0:T(8,128)S(1)}, u32[]{:S(2)}, u32[]{:S(2)}) collective-permute-start(f32[2,264,128]{2,1,0:T(8,128)S(1)} %slice_add_fusion.1), channel_id=1, source_target_pairs={{0,4},{4,0},{1,5},{5,1},{2,6},{6,2},{3,7},{7,3},{8,12},{12,8},{9,1... | collective-permute-start | bytes 811016 | tf_op jit(solution)/shard_map/ppermute | solution.py:487
  125.3 8.8 %collective-permute-start.2 = (f32[264,128]{1,0:T(8,128)S(1)}, f32[264,128]{1,0:T(8,128)S(1)}, u32[]{:S(2)}, u32[]{:S(2)}) collective-permute-start(f32[264,128]{1,0:T(8,128)S(1)} %slice_bitcast_fusion.6), channel_id=1, source_target_pairs={{0,4},{4,0},{1,5},{5,1},{2,6},{6,2},{3,7},{7,3},{8,12},{12,8},{9,1... | collective-permute-start | bytes 405512 | tf_op jit(solution)/shard_map/ppermute | solution.py:487
  128.2 6.0 %collective-permute-start.5 = (f32[264,128]{1,0:T(8,128)S(1)}, f32[264,128]{1,0:T(8,128)S(1)}, u32[]{:S(2)}, u32[]{:S(2)}) collective-permute-start(f32[264,128]{1,0:T(8,128)S(1)} %slice_bitcast_fusion.4), channel_id=1, source_target_pairs={{0,2},{2,0},{1,3},{3,1},{4,6},{6,4},{5,7},{7,5},{8,10},{10,8},{9,1... | collective-permute-start | bytes 405512 | tf_op jit(solution)/shard_map/ppermute | solution.py:487
  131.9 6.1 %collective-permute-start.8 = (f32[264,128]{1,0:T(8,128)S(1)}, f32[264,128]{1,0:T(8,128)S(1)}, u32[]{:S(2)}, u32[]{:S(2)}) collective-permute-start(f32[264,128]{1,0:T(8,128)S(1)} %slice_bitcast_fusion.2), channel_id=1, source_target_pairs={{0,4},{4,0},{1,5},{5,1},{2,6},{6,2},{3,7},{7,3},{8,12},{12,8},{9,1... | collective-permute-start | bytes 405512 | tf_op jit(solution)/shard_map/ppermute | solution.py:487
  132.8 5.3 %collective-permute-start.11 = (f32[264,128]{1,0:T(8,128)S(1)}, f32[264,128]{1,0:T(8,128)S(1)}, u32[]{:S(2)}, u32[]{:S(2)}) collective-permute-start(f32[264,128]{1,0:T(8,128)S(1)} %slice_bitcast_fusion), channel_id=1, source_target_pairs={{0,2},{2,0},{1,3},{3,1},{4,6},{6,4},{5,7},{7,5},{8,10},{10,8},{9,1... | collective-permute-start | bytes 405512 | tf_op jit(solution)/shard_map/ppermute | solution.py:487
  146.3 6.3 %collective-permute-start.12 = (f32[264,128]{1,0:T(8,128)S(1)}, f32[264,128]{1,0:T(8,128)S(1)}, u32[]{:S(2)}, u32[]{:S(2)}) collective-permute-start(f32[264,128]{1,0:T(8,128)S(1)} %fusion.13), channel_id=1, source_target_pairs={{0,24},{8,0},{16,8},{24,16},{1,25},{9,1},{17,9},{25,17},{2,26},{10... | collective-permute-start | bytes 405512 | tf_op jit(solution)/shard_map/ppermute | solution.py:482
  148.0 12.0 %collective-permute-start.13 = (f32[264,128]{1,0:T(8,128)S(1)}, f32[264,128]{1,0:T(8,128)S(1)}, u32[]{:S(2)}, u32[]{:S(2)}) collective-permute-start(f32[264,128]{1,0:T(8,128)S(1)} %fusion.14), channel_id=1, source_target_pairs={{0,16},{8,24},{16,0},{24,8},{1,17},{9,25},{17,1},{25,9},{2,18},{10... | collective-permute-start | bytes 405512 | tf_op jit(solution)/shard_map/ppermute | solution.py:482
  148.0 12.0 %collective-permute-start.14 = (f32[264,128]{1,0:T(8,128)S(1)}, f32[264,128]{1,0:T(8,128)S(1)}, u32[]{:S(2)}, u32[]{:S(2)}) collective-permute-start(f32[264,128]{1,0:T(8,128)S(1)} %fusion.15), channel_id=1, source_target_pairs={{0,8},{8,16},{16,24},{24,0},{1,9},{9,17},{17,25},{25,1},{2,10},{10... | collective-permute-start | bytes 405512 | tf_op jit(solution)/shard_map/ppermute | solution.py:482
  160.7 0.7 copy-start.8
  161.4 2.4 %copy-start = (f32[1024,256]{1,0:T(8,128)S(1)}, f32[1024,256]{1,0:T(8,128)}, u32[]{:S(2)}) copy-start(f32[1024,256]{1,0:T(8,128)} %cotangent_hbm.1) | copy-start | bytes 3145732
  161.4 2.4 %copy-start.1 = (f32[1024,256]{1,0:T(8,128)S(1)}, f32[1024,256]{1,0:T(8,128)}, u32[]{:S(2)}) copy-start(f32[1024,256]{1,0:T(8,128)} %latents_hbm.1) | copy-start | bytes 3145732
Sparse Core Ops, SparseCore 0:
  160.8 62.4 all-gather.2

commit v5 on v2

--- a/solution.py
+++ b/solution.py
@@ -345,10 +345,9 @@
     for k in range(outer):
         for e in range(pieces * core):
             flat[k, e, length:, :] = jnp.zeros((EXTRA, LANES), jnp.float32)
-    biases = [bias_in[:, k : k + LANES] for k in range(0, hidden_size, LANES)]
-    biases += [bias_out[:, k : k + LANES] for k in range(0, width, LANES)]
-    for j, bias in enumerate(biases):
-        flat[home, j // EXTRA, length + j % EXTRA : length + j % EXTRA + 1, :] = bias
+    for e, bias in enumerate((bias_in, bias_out)):
+        for j in range(bias.shape[1] // LANES):
+            flat[home, e, length + j : length + j + 1, :] = bias[:, j * LANES : (j + 1) * LANES]
 
     loads[4].wait()
     loads[5].wait()
@@ -417,7 +416,8 @@
 def assemble_kernel(sizes, *refs):
     outer, inner, chip, core = sizes
     devices = outer * inner * chip * core
-    pieces, (weight_in, weight_out, biases, sems, bias_sem) = refs[:devices], refs[devices:]
+    pieces, refs = refs[:devices], refs[devices:]
+    weight_in, weight_out, bias_in, bias_out, sems, bias_sem = refs
     length = pieces[0].shape[0] - EXTRA
     dim_in, hidden_size = weight_in.shape
     band = hidden_size // outer
@@ -449,13 +449,15 @@
         def _():
             copy_to(weight_out, o * band + lax.rem(at - base, band), lax.div(at - base, band)).start()
 
-        @pl.when((o == 0) & (e < 2))
-        def _():
-            copy = pltpu.make_async_copy(
-                piece.at[pl.ds(length, EXTRA)], biases.at[jnp.minimum(e, 1)], bias_sem
-            )
-            copy.start()
-            copy.wait()
+        for row, bias in enumerate((bias_in, bias_out)):
+
+            @pl.when((o == 0) & (e == row))
+            def _():
+                copy = pltpu.make_async_copy(
+                    piece.at[pl.ds(length, EXTRA)], bias, bias_sem
+                )
+                copy.start()
+                copy.wait()
 
         copies.append(copy_to(weight_in, 0, 0))
     for copy in copies:
@@ -467,11 +469,12 @@
     return pl.pallas_call(
         functools.partial(assemble_kernel, sizes),
         in_specs=[hbm] * len(pieces),
-        out_specs=[hbm] * 3,
+        out_specs=[hbm] * 4,
         out_shape=[
             jax.ShapeDtypeStruct((dim_in, hidden_size), jnp.float32),
             jax.ShapeDtypeStruct((hidden_size, width), jnp.float32),
-            jax.ShapeDtypeStruct((2, EXTRA, LANES), jnp.float32),
+            jax.ShapeDtypeStruct((EXTRA, LANES), jnp.float32),
+            jax.ShapeDtypeStruct((EXTRA, LANES), jnp.float32),
         ],
         scratch_shapes=[
             pltpu.SemaphoreType.DMA((len(pieces),)),
@@ -492,7 +495,7 @@
     return lax.ppermute(x, axis, [(p, p ^ j) for p in range(size)])
 
 
-def sum_chunks(sizes, mine, theirs, answers):
+def sum_chunks(sizes, mine, theirs):
     outer, inner, chip, _ = sizes
     chunks = [None] * outer
     for k in range(outer - 1, -1, -1):
@@ -506,11 +509,10 @@
         chunks[k] = part[0]
         for j in range(1, low):
             chunks[k] = chunks[k] + across(sizes, fast, part[j], j)
-    chunks, answers = lax.optimization_barrier((chunks, answers))
     total = chunks[0]
     for k in range(outer - 1, 0, -1):
         total = total + along(sizes, chunks[k], k)
-    return total, answers
+    return total
 
 
 def spread_chunks(sizes, total):
@@ -545,10 +547,21 @@
     picked, wanted = pick_rows(capacity, incoming, parts)
     answers = lax.all_to_all(picked, AXES, split_axis=0, concat_axis=0, tiled=True)
 
-    pieces = backward(
-        sizes, capacity, incoming, wanted, hidden_t, slope, projected, codebook_t, weight_out.T
+    weight_t = weight_out.T
+
+    def reduce_half(*operands):
+        pieces = backward(sizes, capacity, *operands)
+        return sum_chunks(sizes, list(pieces[:outer]), list(pieces[outer:]))
+
+    def nothing(*operands):
+        length = (dim_in + width) * hidden_size // LANES // devices
+        return jnp.zeros((length + EXTRA, LANES), jnp.float32)
+
+    total = lax.cond(
+        code_row[0] >= 0, reduce_half, nothing,
+        incoming, wanted, hidden_t, slope, projected, codebook_t, weight_t,
     )
-    total, answers = sum_chunks(sizes, list(pieces[:outer]), list(pieces[outer:]), answers)
+    total, answers = lax.optimization_barrier((total, answers))
     answers = answers.reshape(-1, width)
     near = spread_chunks(sizes, total)
 
@@ -560,9 +573,8 @@
     near[late], latent_grad = lax.optimization_barrier((near[late], latent_grad))
 
     chunks = near + [across(sizes, "core", x, 1) for x in near]
-    gw_in, gw_out, biases = assemble(sizes, chunks, dim_in, hidden_size, width)
-    biases = biases.reshape(-1)
-    gb_in, gb_out = biases[:hidden_size], biases[hidden_size : hidden_size + width]
+    gw_in, gw_out, gb_in, gb_out = assemble(sizes, chunks, dim_in, hidden_size, width)
+    gb_in, gb_out = gb_in.reshape(-1)[:hidden_size], gb_out.reshape(-1)[:width]
     return (latent_grad, gw_in, gb_in, gw_out, gb_out)
 
 

time: 198 us -> 180 us (0.909)
  waiting for transfers between devices: 101 us -> 87.8 us
  starting transfers between devices: 48.4 us -> 44.2 us
    all_to_all x1, waiting for transfers between devices: 8.23 us -> 0.01 us  [per_device(): lax.all_to_all(picked, AXES, split_axis=0, concat_axis=0, tiled=True)]
    ppermute x40, starting transfers between devices: 28.1 us -> 22.7 us  [across(): return lax.ppermute(x, axis, [(p, p ^ j) for p in range(size)])]
    ppermute x6, waiting for transfers between devices: 15.3 us -> 10.1 us  [along(): lax.ppermute(x, 'outer', [(o, (o + k) % outer) for o in range(outer)])]
    unnamed x19 -> x9, local copies, waits for them, and re-layouts: 2.41 us -> 0.23 us
  transfers between devices with their start and end apart: 48 -> 48, of which waited for: 18 -> 21; matrix products, arithmetic and copies ran while one was open for 5% -> 5% of each run, Pallas kernels for 4% -> 12%
where the time goes in v5:
time: 180 us; the launch traced here: 179 us
  waiting for transfers between devices  87.8 us (49%)
  starting transfers between devices  44.2 us (25%)
  Pallas kernels  36.1 us (20%)
  other arithmetic  4.93 us (3%)
  matrix products  2.38 us (1%)
  local copies, waits for them, and re-layouts  2.05 us (1%)
    all_to_all x1, waiting for transfers between devices, per_device(): lax.all_to_all(outgoing, AXES, split_axis=0, concat_axis=0, tiled=True)  43.3 us
    ppermute x40, waiting for transfers between devices, across(): return lax.ppermute(x, axis, [(p, p ^ j) for p in range(size)])  34.3 us
    ppermute x40, starting transfers between devices, across(): return lax.ppermute(x, axis, [(p, p ^ j) for p in range(size)])  22.7 us
    pallas_call x1, Pallas kernels, backward(): pl.pallas_call(functools.partial(backward_kernel, sizes, capacity), in_sp...  12.6 us
    ppermute x6, waiting for transfers between devices, along(): lax.ppermute(x, 'outer', [(o, (o + k) % outer) for o in range(outer)])  10.1 us
    ppermute x6, starting transfers between devices, along(): lax.ppermute(x, 'outer', [(o, (o + k) % outer) for o in range(outer)])  9.99 us
    pallas_call x1, Pallas kernels, forward(): pl.pallas_call(forward_kernel, grid=(rows // tile,), in_specs=[pl.BlockSp...  8.43 us
    all_to_all x1, starting transfers between devices, per_device(): lax.all_to_all(outgoing, AXES, split_axis=0, concat_axis=0, tiled=True)  7.42 us
  transfers between devices with their start and end apart: 48, of which 21 were waited for; matrix products, arithmetic and copies ran while one was open for 5% of the time, Pallas kernels for 12%

profile of v5, /device:TPU:0, one launch (start us, length us, event | category | flops | bytes accessed | tf_op | source)
XLA Modules:
  0.0 179.3 jit_solution(12401116654118772508)
XLA Ops:
  0.6 7.0 %route.1 = (f32[32,136,128]{2,1,0:T(8,128)}, s32[1,1024]{1,0:T(1,128)}) custom-call(s32[1,1024]{1,0:T(1,128)} %bitcast.44, s32[1,1024]{1,0:T(1,128)} %bitcast.45, f32[1024,256]{1,0:T(8,128)} %latents_hbm.1, f32[1024,256]{1,0:T(8,128)} %cotangent_hbm.1), custom_call_target="tpu_custom_call" | custom-call | tf_op jit(solution)/shard_map/route/pallas_call | solution.py:246
  7.6 7.4 %all-to-all-start = ((f32[32,136,128]{2,1,0:T(8,128)}), f32[32,136,128]{2,1,0:T(8,128)}, u32[]{:S(2)}, u32[]{:S(2)}) async-start(f32[32,136,128]{2,1,0:T(8,128)} %get-tuple-element.57), calls=%async_computation | async-start | bytes 4456448 | tf_op jit(solution)/shard_map/all_to_all | solution.py:542
  15.0 8.4 %forward.1 = (bf16[1024,1024]{1,0:T(8,128)(2,1)}, bf16[768,1024]{1,0:T(8,128)(2,1)}, f32[1024,1024]{1,0:T(8,128)}, f32[1024,256]{1,0:T(8,128)}, bf16[1024,512]{1,0:T(8,128)(2,1)}) custom-call(bf16[1024,768]{1,0:T(8,128)(2,1)} %codebook_ref.1, bf16[768,1024]{1,0:T(8,128)(2,1)} %weight_in_ref.1, f32[1,1024]{1,0:T(1,128)} %bitcast.46, ...), custom_call_target="tpu_custom_call" | custom-call | flops 2147483648 | bytes 14680064 | tf_op jit(solution)/shard_map/forward/pallas_call | solution.py:62
  23.5 43.3 %all-to-all-done.incoming_hbm = f32[32,136,128]{2,1,0:T(8,128)} async-done(((f32[32,136,128]{2,1,0:T(8,128)}), f32[32,136,128]{2,1,0:T(8,128)}, u32[]{:S(2)}, u32[]{:S(2)}) %all-to-all-start) | async-done | bytes 2228256 | tf_op jit(solution)/shard_map/all_to_all | solution.py:542
  66.8 5.2 %pick_rows.1 = (f32[32,64,256]{2,1,0:T(8,128)}, f32[8,2048]{1,0:T(8,128)S(1)}) custom-call(f32[32,136,128]{2,1,0:T(8,128)} %all-to-all-done.incoming_hbm, bf16[1024,512]{1,0:T(8,128)(2,1)} %get-tuple-element.59.parts_hbm), custom_call_target="tpu_custom_call" | custom-call | flops 2147483648 | bytes 4194304 | tf_op jit(solution)/shard_map/pick_rows/pallas_call | solution.py:143
  72.0 4.0 %all-to-all-start.1 = ((f32[32,64,256]{2,1,0:T(8,128)}), f32[32,64,256]{2,1,0:T(8,128)S(1)}, u32[]{:S(2)}, u32[]{:S(2)}) async-start(f32[32,64,256]{2,1,0:T(8,128)} %get-tuple-element.65), calls=%async_computation.1 | async-start | bytes 4194304 | tf_op jit(solution)/shard_map/all_to_all | solution.py:548
  78.1 58.9 %conditional.1 = (f32[264,128]{1,0:T(8,128)S(1)}) conditional(s32[]{:T(128)} %bitcast.8, () %tuple.17, (f32[32,136,128]{2,1,0:T(8,128)}, f32[8,2048]{1,0:T(8,128)S(1)}, bf16[1024,1024]{1,0:T(8,128)(2,1)}, f32[1024,1024]{1,0:T(8,128)}, f32[1024,256]{1,0:T(8,128)}, /*index=5*/bf16[768,1024]{1,0:T(8,128)(2,1)}, bf16[256,1024]{1,0:T(8,128)(2,1)S(1)}) %tuple.26), branch_computations={%region_0.0_spmd, %region_1.0_spmd} | conditional | flops 4832885760 | bytes 52867792 | solution.py:560
  78.3 12.6 %backward.1 = (f32[4,264,128]{2,1,0:T(8,128)}, f32[4,264,128]{2,1,0:T(8,128)}, f32[4,264,128]{2,1,0:T(8,128)}, f32[4,264,128]{2,1,0:T(8,128)}, f32[4,264,128]{2,...) custom-call(f32[32,136,128]{2,1,0:T(8,128)} %get-tuple-element.6.incoming_hbm, ...), custom_call_target="tpu_custom_call" | custom-call | flops 4831838208 | bytes 16777216 | tf_op jit(solution)/shard_map/cond/branch_1_fun/backward/pallas_call | solution.py:391
  94.1 1.8 %collective-permute-start.1 = (f32[2,264,128]{2,1,0:T(8,128)S(1)}, f32[2,264,128]{2,1,0:T(8,128)S(1)}, u32[]{:S(2)}, u32[]{:S(2)}) collective-permute-start(f32[2,264,128]{2,1,0:T(8,128)S(1)} %slice_add_fusion.6), channel_id=1, source_target_pairs={{0,2},{2,0},{1,3},{3,1},{4,6},{6,4},{5,7},{7,5},{8,10},{10,8},{9,1... | collective-permute-start | bytes 811016 | tf_op jit(solution)/shard_map/cond/branch_1_fun/ppermute | solution.py:495
  96.9 1.5 collective-permute-start.4
  100.5 9.2 %collective-permute-done.1 = f32[2,264,128]{2,1,0:T(8,128)S(1)} collective-permute-done((f32[2,264,128]{2,1,0:T(8,128)S(1)}, f32[2,264,128]{2,1,0:T(8,128)S(1)}, u32[]{:S(2)}, u32[]{:S(2)}) %collective-permute-start.1) | collective-permute-done | bytes 270368 | tf_op jit(solution)/shard_map/cond/branch_1_fun/ppermute | solution.py:495
  111.0 4.5 %collective-permute-done.8 = f32[2,264,128]{2,1,0:T(8,128)S(1)} collective-permute-done((f32[2,264,128]{2,1,0:T(8,128)S(1)}, f32[2,264,128]{2,1,0:T(8,128)S(1)}, u32[]{:S(2)}, u32[]{:S(2)}) %collective-permute-start.8) | collective-permute-done | bytes 270368 | tf_op jit(solution)/shard_map/cond/branch_1_fun/ppermute | solution.py:495
  115.7 1.5 collective-permute-done.12
  117.5 1.3 collective-permute-done.5
  118.7 1.9 %collective-permute-start.6 = (f32[264,128]{1,0:T(8,128)S(1)}, f32[264,128]{1,0:T(8,128)S(1)}, u32[]{:S(2)}, u32[]{:S(2)}) collective-permute-start(f32[264,128]{1,0:T(8,128)S(1)} %fusion.6), channel_id=1, source_target_pairs={{0,24},{8,0},{16,8},{24,16},{1,25},{9,1},{17,9},{25,17},{2,26},{10... | collective-permute-start | bytes 405512 | tf_op jit(solution)/shard_map/cond/branch_1_fun/ppermute | solution.py:490
  120.6 3.9 %collective-permute-done.9 = f32[264,128]{1,0:T(8,128)S(1)} collective-permute-done((f32[264,128]{1,0:T(8,128)S(1)}, f32[264,128]{1,0:T(8,128)S(1)}, u32[]{:S(2)}, u32[]{:S(2)}) %collective-permute-start.9) | collective-permute-done | bytes 135200 | tf_op jit(solution)/shard_map/cond/branch_1_fun/ppermute | solution.py:495
  124.6 2.9 %collective-permute-start.10 = (f32[264,128]{1,0:T(8,128)S(1)}, f32[264,128]{1,0:T(8,128)S(1)}, u32[]{:S(2)}, u32[]{:S(2)}) collective-permute-start(f32[264,128]{1,0:T(8,128)S(1)} %fusion.5), channel_id=1, source_target_pairs={{0,16},{8,24},{16,0},{24,8},{1,17},{9,25},{17,1},{25,9},{2,18},{10... | collective-permute-start | bytes 405512 | tf_op jit(solution)/shard_map/cond/branch_1_fun/ppermute | solution.py:490
  127.6 9.1 %collective-permute-done.10 = f32[264,128]{1,0:T(8,128)S(1)} collective-permute-done((f32[264,128]{1,0:T(8,128)S(1)}, f32[264,128]{1,0:T(8,128)S(1)}, u32[]{:S(2)}, u32[]{:S(2)}) %collective-permute-start.10) | collective-permute-done | bytes 135200 | tf_op jit(solution)/shard_map/cond/branch_1_fun/ppermute | solution.py:490
  138.9 2.0 %collective-permute-start.16 = (f32[264,128]{1,0:T(8,128)S(1)}, f32[264,128]{1,0:T(8,128)S(1)}, u32[]{:S(2)}, u32[]{:S(2)}) collective-permute-start(f32[264,128]{1,0:T(8,128)S(1)} %get-tuple-element.77.refs_0_), channel_id=1, source_target_pairs={{0,4},{4,0},{1,5},{5,1},{2,6},{6,2},{3,7},{7,3},{8,12},{12,8},{9,1... | collective-permute-start | bytes 405512 | tf_op jit(solution)/shard_map/ppermute | solution.py:495
  141.2 3.9 %collective-permute-start.15 = (f32[264,128]{1,0:T(8,128)S(1)}, f32[264,128]{1,0:T(8,128)S(1)}, u32[]{:S(2)}, u32[]{:S(2)}) collective-permute-start(f32[264,128]{1,0:T(8,128)S(1)} %get-tuple-element.77.refs_0_), channel_id=1, source_target_pairs={{0,24},{8,0},{16,8},{24,16},{1,25},{9,1},{17,9},{25,17},{2,26},{10... | collective-permute-start | bytes 405512 | tf_op jit(solution)/shard_map/ppermute | solution.py:490
  145.1 2.4 %fusion.11 = f32[1024,512]{1,0:T(8,128)S(1)} fusion(s32[1024]{0:T(1024)S(1)} %bitcast.47, bf16[2048,256]{1,0:T(8,128)(2,1)S(1)} %get-tuple-element.76, bf16[2048,256]{1,0:T(8,128)(2,1)S(1)} %get-tuple-element.75), kind=kOutput, calls=%fused_computation.28 | convolution fusion | flops 2153775104 | bytes 4198400 | tf_op jit(solution)/shard_map/dot_general | solution.py:34
  149.1 2.0 %collective-permute-start.24 = (f32[264,128]{1,0:T(8,128)S(1)}, f32[264,128]{1,0:T(8,128)S(1)}, u32[]{:S(2)}, u32[]{:S(2)}) collective-permute-start(f32[264,128]{1,0:T(8,128)S(1)} %collective-permute-done.23.refs_8_), channel_id=1, source_target_pairs={{0,4},{4,0},{1,5},{5,1},{2,6},{6,2},{3,7},{7,3},{8,12},{12,8},{9,1... | collective-permute-start | bytes 405512 | tf_op jit(solution)/shard_map/ppermute | solution.py:495
  151.3 1.6 collective-permute-start.21
  152.8 1.2 fusion.19
  158.0 1.9 %collective-permute-done.20.refs_5_ = f32[264,128]{1,0:T(8,128)S(1)} collective-permute-done((f32[264,128]{1,0:T(8,128)S(1)}, f32[264,128]{1,0:T(8,128)S(1)}, u32[]{:S(2)}, u32[]{:S(2)}) %collective-permute-start.20) | collective-permute-done | bytes 135200 | tf_op jit(solution)/shard_map/ppermute | solution.py:495
  163.3 1.6 collective-permute-done.28.refs_14_
  165.7 1.3 collective-permute-start.22
  168.4 1.6 collective-permute-start.29
  170.5 1.6 collective-permute-done.22.refs_7_
  172.6 2.0 %collective-permute-done.29.refs_15_ = f32[264,128]{1,0:T(8,128)S(1)} collective-permute-done((f32[264,128]{1,0:T(8,128)S(1)}, f32[264,128]{1,0:T(8,128)S(1)}, u32[]{:S(2)}, u32[]{:S(2)}) %collective-permute-start.29) | collective-permute-done | bytes 135200 | tf_op jit(solution)/shard_map/ppermute | solution.py:495
  174.6 1.3 collective-permute-done.45.refs_31_
  175.9 2.9 %assemble.1 = (f32[768,1024]{1,0:T(8,128)}, f32[1024,256]{1,0:T(8,128)}, f32[8,128]{1,0:T(8,128)}, f32[8,128]{1,0:T(8,128)S(1)}) custom-call(f32[264,128]{1,0:T(8,128)S(1)} %get-tuple-element.77.refs_0_, f32[264,128]{1,0:T(8,128)S(1)} %collective-permute-done.16.refs_1_, f32[264,128]{1,0:T(8,128)S(1)} %collective-permute-done.17.refs_2_, ...), custom_call_target="tpu_custom_call" | custom-call | tf_op jit(solution)/shard_map/assemble/pallas_call | solution.py:469
  (108 shorter events, 24.6 us)
Async XLA Ops:
  7.6 59.1 %all-to-all-start = ((f32[32,136,128]{2,1,0:T(8,128)}), f32[32,136,128]{2,1,0:T(8,128)}, u32[]{:S(2)}, u32[]{:S(2)}) async-start(f32[32,136,128]{2,1,0:T(8,128)} %get-tuple-element.57), calls=%async_computation | async-start | bytes 4456448 | tf_op jit(solution)/shard_map/all_to_all | solution.py:542
  72.0 65.0 %all-to-all-start.1 = ((f32[32,64,256]{2,1,0:T(8,128)}), f32[32,64,256]{2,1,0:T(8,128)S(1)}, u32[]{:S(2)}, u32[]{:S(2)}) async-start(f32[32,64,256]{2,1,0:T(8,128)} %get-tuple-element.65), calls=%async_computation.1 | async-start | bytes 4194304 | tf_op jit(solution)/shard_map/all_to_all | solution.py:548
  91.5 7.0 %collective-permute-start.7 = (f32[4,264,128]{2,1,0:T(8,128)}, f32[4,264,128]{2,1,0:T(8,128)S(1)}, u32[]{:S(2)}, u32[]{:S(2)}) collective-permute-start(f32[4,264,128]{2,1,0:T(8,128)} %get-tuple-element.29), channel_id=1, source_target_pairs={{0,1},{1,0},{2,3},{3,2},{4,5},{5,4},{6,7},{7,6},{8,9},{9,8},{10,11... | collective-permute-start | bytes 1622024 | tf_op jit(solution)/shard_map/cond/branch_1_fun/ppermute | solution.py:495
  91.8 8.4 %collective-permute-start.11 = (f32[4,264,128]{2,1,0:T(8,128)}, f32[4,264,128]{2,1,0:T(8,128)S(1)}, u32[]{:S(2)}, u32[]{:S(2)}) collective-permute-start(f32[4,264,128]{2,1,0:T(8,128)} %get-tuple-element.31), channel_id=1, source_target_pairs={{0,1},{1,0},{2,3},{3,2},{4,5},{5,4},{6,7},{7,6},{8,9},{9,8},{10,11... | collective-permute-start | bytes 1622024 | tf_op jit(solution)/shard_map/cond/branch_1_fun/ppermute | solution.py:495
  94.1 15.6 %collective-permute-start.1 = (f32[2,264,128]{2,1,0:T(8,128)S(1)}, f32[2,264,128]{2,1,0:T(8,128)S(1)}, u32[]{:S(2)}, u32[]{:S(2)}) collective-permute-start(f32[2,264,128]{2,1,0:T(8,128)S(1)} %slice_add_fusion.6), channel_id=1, source_target_pairs={{0,2},{2,0},{1,3},{3,1},{4,6},{6,4},{5,7},{7,5},{8,10},{10,8},{9,1... | collective-permute-start | bytes 811016 | tf_op jit(solution)/shard_map/cond/branch_1_fun/ppermute | solution.py:495
  96.9 13.0 %collective-permute-start.4 = (f32[2,264,128]{2,1,0:T(8,128)S(1)}, f32[2,264,128]{2,1,0:T(8,128)S(1)}, u32[]{:S(2)}, u32[]{:S(2)}) collective-permute-start(f32[2,264,128]{2,1,0:T(8,128)S(1)} %slice_add_fusion.4), channel_id=1, source_target_pairs={{0,4},{4,0},{1,5},{5,1},{2,6},{6,2},{3,7},{7,3},{8,12},{12,8},{9,1... | collective-permute-start | bytes 811016 | tf_op jit(solution)/shard_map/cond/branch_1_fun/ppermute | solution.py:495
  99.6 15.9 %collective-permute-start.8 = (f32[2,264,128]{2,1,0:T(8,128)S(1)}, f32[2,264,128]{2,1,0:T(8,128)S(1)}, u32[]{:S(2)}, u32[]{:S(2)}) collective-permute-start(f32[2,264,128]{2,1,0:T(8,128)S(1)} %slice_add_fusion.2), channel_id=1, source_target_pairs={{0,2},{2,0},{1,3},{3,1},{4,6},{6,4},{5,7},{7,5},{8,10},{10,8},{9,1... | collective-permute-start | bytes 811016 | tf_op jit(solution)/shard_map/cond/branch_1_fun/ppermute | solution.py:495
  100.2 16.9 %collective-permute-start.12 = (f32[2,264,128]{2,1,0:T(8,128)S(1)}, f32[2,264,128]{2,1,0:T(8,128)S(1)}, u32[]{:S(2)}, u32[]{:S(2)}) collective-permute-start(f32[2,264,128]{2,1,0:T(8,128)S(1)} %slice_add_fusion), channel_id=1, source_target_pairs={{0,4},{4,0},{1,5},{5,1},{2,6},{6,2},{3,7},{7,3},{8,12},{12,8},{9,1... | collective-permute-start | bytes 811016 | tf_op jit(solution)/shard_map/cond/branch_1_fun/ppermute | solution.py:495
  109.8 17.9 %collective-permute-start.2 = (f32[264,128]{1,0:T(8,128)S(1)}, f32[264,128]{1,0:T(8,128)S(1)}, u32[]{:S(2)}, u32[]{:S(2)}) collective-permute-start(f32[264,128]{1,0:T(8,128)S(1)} %slice_bitcast_fusion.6), channel_id=1, source_target_pairs={{0,4},{4,0},{1,5},{5,1},{2,6},{6,2},{3,7},{7,3},{8,12},{12,8},{9,1... | collective-permute-start | bytes 405512 | tf_op jit(solution)/shard_map/cond/branch_1_fun/ppermute | solution.py:495
  110.0 8.7 %collective-permute-start.5 = (f32[264,128]{1,0:T(8,128)S(1)}, f32[264,128]{1,0:T(8,128)S(1)}, u32[]{:S(2)}, u32[]{:S(2)}) collective-permute-start(f32[264,128]{1,0:T(8,128)S(1)} %slice_bitcast_fusion.4), channel_id=1, source_target_pairs={{0,2},{2,0},{1,3},{3,1},{4,6},{6,4},{5,7},{7,5},{8,10},{10,8},{9,1... | collective-permute-start | bytes 405512 | tf_op jit(solution)/shard_map/cond/branch_1_fun/ppermute | solution.py:495
  115.6 9.0 %collective-permute-start.9 = (f32[264,128]{1,0:T(8,128)S(1)}, f32[264,128]{1,0:T(8,128)S(1)}, u32[]{:S(2)}, u32[]{:S(2)}) collective-permute-start(f32[264,128]{1,0:T(8,128)S(1)} %slice_bitcast_fusion.2), channel_id=1, source_target_pairs={{0,4},{4,0},{1,5},{5,1},{2,6},{6,2},{3,7},{7,3},{8,12},{12,8},{9,1... | collective-permute-start | bytes 405512 | tf_op jit(solution)/shard_map/cond/branch_1_fun/ppermute | solution.py:495
  117.2 10.3 %collective-permute-start.13 = (f32[264,128]{1,0:T(8,128)S(1)}, f32[264,128]{1,0:T(8,128)S(1)}, u32[]{:S(2)}, u32[]{:S(2)}) collective-permute-start(f32[264,128]{1,0:T(8,128)S(1)} %slice_bitcast_fusion), channel_id=1, source_target_pairs={{0,2},{2,0},{1,3},{3,1},{4,6},{6,4},{5,7},{7,5},{8,10},{10,8},{9,1... | collective-permute-start | bytes 405512 | tf_op jit(solution)/shard_map/cond/branch_1_fun/ppermute | solution.py:495
  118.7 8.9 %collective-permute-start.6 = (f32[264,128]{1,0:T(8,128)S(1)}, f32[264,128]{1,0:T(8,128)S(1)}, u32[]{:S(2)}, u32[]{:S(2)}) collective-permute-start(f32[264,128]{1,0:T(8,128)S(1)} %fusion.6), channel_id=1, source_target_pairs={{0,24},{8,0},{16,8},{24,16},{1,25},{9,1},{17,9},{25,17},{2,26},{10... | collective-permute-start | bytes 405512 | tf_op jit(solution)/shard_map/cond/branch_1_fun/ppermute | solution.py:490
  124.6 12.1 %collective-permute-start.10 = (f32[264,128]{1,0:T(8,128)S(1)}, f32[264,128]{1,0:T(8,128)S(1)}, u32[]{:S(2)}, u32[]{:S(2)}) collective-permute-start(f32[264,128]{1,0:T(8,128)S(1)} %fusion.5), channel_id=1, source_target_pairs={{0,16},{8,24},{16,0},{24,8},{1,17},{9,25},{17,1},{25,9},{2,18},{10... | collective-permute-start | bytes 405512 | tf_op jit(solution)/shard_map/cond/branch_1_fun/ppermute | solution.py:490
  127.5 9.2 %collective-permute-start.14 = (f32[264,128]{1,0:T(8,128)S(1)}, f32[264,128]{1,0:T(8,128)S(1)}, u32[]{:S(2)}, u32[]{:S(2)}) collective-permute-start(f32[264,128]{1,0:T(8,128)S(1)} %fusion.4), channel_id=1, source_target_pairs={{0,8},{8,16},{16,24},{24,0},{1,9},{9,17},{17,25},{25,1},{2,10},{10... | collective-permute-start | bytes 405512 | tf_op jit(solution)/shard_map/cond/branch_1_fun/ppermute | solution.py:490
  137.1 11.4 %collective-permute-start.23 = (f32[264,128]{1,0:T(8,128)S(1)}, f32[264,128]{1,0:T(8,128)S(1)}, u32[]{:S(2)}, u32[]{:S(2)}) collective-permute-start(f32[264,128]{1,0:T(8,128)S(1)} %get-tuple-element.77.refs_0_), channel_id=1, source_target_pairs={{0,16},{8,24},{16,0},{24,8},{1,17},{9,25},{17,1},{25,9},{2,18},{10... | collective-permute-start | bytes 405512 | tf_op jit(solution)/shard_map/ppermute | solution.py:490
  138.2 10.3 %collective-permute-start.19 = (f32[264,128]{1,0:T(8,128)S(1)}, f32[264,128]{1,0:T(8,128)S(1)}, u32[]{:S(2)}, u32[]{:S(2)}) collective-permute-start(f32[264,128]{1,0:T(8,128)S(1)} %get-tuple-element.77.refs_0_), channel_id=1, source_target_pairs={{0,8},{8,16},{16,24},{24,0},{1,9},{9,17},{17,25},{25,1},{2,10},{10... | collective-permute-start | bytes 405512 | tf_op jit(solution)/shard_map/ppermute | solution.py:490
  138.2 10.9 %collective-permute-start.17 = (f32[264,128]{1,0:T(8,128)S(1)}, f32[264,128]{1,0:T(8,128)S(1)}, u32[]{:S(2)}, u32[]{:S(2)}) collective-permute-start(f32[264,128]{1,0:T(8,128)S(1)} %get-tuple-element.77.refs_0_), channel_id=1, source_target_pairs={{0,2},{2,0},{1,3},{3,1},{4,6},{6,4},{5,7},{7,5},{8,10},{10,8},{9,1... | collective-permute-start | bytes 405512 | tf_op jit(solution)/shard_map/ppermute | solution.py:495
  138.9 12.3 %collective-permute-start.16 = (f32[264,128]{1,0:T(8,128)S(1)}, f32[264,128]{1,0:T(8,128)S(1)}, u32[]{:S(2)}, u32[]{:S(2)}) collective-permute-start(f32[264,128]{1,0:T(8,128)S(1)} %get-tuple-element.77.refs_0_), channel_id=1, source_target_pairs={{0,4},{4,0},{1,5},{5,1},{2,6},{6,2},{3,7},{7,3},{8,12},{12,8},{9,1... | collective-permute-start | bytes 405512 | tf_op jit(solution)/shard_map/ppermute | solution.py:495
  141.2 10.0 %collective-permute-start.15 = (f32[264,128]{1,0:T(8,128)S(1)}, f32[264,128]{1,0:T(8,128)S(1)}, u32[]{:S(2)}, u32[]{:S(2)}) collective-permute-start(f32[264,128]{1,0:T(8,128)S(1)} %get-tuple-element.77.refs_0_), channel_id=1, source_target_pairs={{0,24},{8,0},{16,8},{24,16},{1,25},{9,1},{17,9},{25,17},{2,26},{10... | collective-permute-start | bytes 405512 | tf_op jit(solution)/shard_map/ppermute | solution.py:490
  148.5 5.6 %collective-permute-start.38 = (f32[264,128]{1,0:T(8,128)S(1)}, f32[264,128]{1,0:T(8,128)S(1)}, u32[]{:S(2)}, u32[]{:S(2)}) collective-permute-start(f32[264,128]{1,0:T(8,128)S(1)} %collective-permute-done.23.refs_8_), channel_id=1, source_target_pairs={{0,1},{1,0},{2,3},{3,2},{4,5},{5,4},{6,7},{7,6},{8,9},{9,8},{10,11... | collective-permute-start | bytes 405512 | tf_op jit(solution)/shard_map/ppermute | solution.py:495
  148.5 6.7 %collective-permute-start.25 = (f32[264,128]{1,0:T(8,128)S(1)}, f32[264,128]{1,0:T(8,128)S(1)}, u32[]{:S(2)}, u32[]{:S(2)}) collective-permute-start(f32[264,128]{1,0:T(8,128)S(1)} %collective-permute-done.23.refs_8_), channel_id=1, source_target_pairs={{0,2},{2,0},{1,3},{3,1},{4,6},{6,4},{5,7},{7,5},{8,10},{10,8},{9,1... | collective-permute-start | bytes 405512 | tf_op jit(solution)/shard_map/ppermute | solution.py:495
  149.1 6.4 %collective-permute-start.24 = (f32[264,128]{1,0:T(8,128)S(1)}, f32[264,128]{1,0:T(8,128)S(1)}, u32[]{:S(2)}, u32[]{:S(2)}) collective-permute-start(f32[264,128]{1,0:T(8,128)S(1)} %collective-permute-done.23.refs_8_), channel_id=1, source_target_pairs={{0,4},{4,0},{1,5},{5,1},{2,6},{6,2},{3,7},{7,3},{8,12},{12,8},{9,1... | collective-permute-start | bytes 405512 | tf_op jit(solution)/shard_map/ppermute | solution.py:495
  151.3 6.8 %collective-permute-start.21 = (f32[264,128]{1,0:T(8,128)S(1)}, f32[264,128]{1,0:T(8,128)S(1)}, u32[]{:S(2)}, u32[]{:S(2)}) collective-permute-start(f32[264,128]{1,0:T(8,128)S(1)} %collective-permute-done.19.refs_4_), channel_id=1, source_target_pairs={{0,4},{4,0},{1,5},{5,1},{2,6},{6,2},{3,7},{7,3},{8,12},{12,8},{9,1... | collective-permute-start | bytes 405512 | tf_op jit(solution)/shard_map/ppermute | solution.py:495
  154.1 5.9 %collective-permute-start.20 = (f32[264,128]{1,0:T(8,128)S(1)}, f32[264,128]{1,0:T(8,128)S(1)}, u32[]{:S(2)}, u32[]{:S(2)}) collective-permute-start(f32[264,128]{1,0:T(8,128)S(1)} %collective-permute-done.19.refs_4_), channel_id=1, source_target_pairs={{0,2},{2,0},{1,3},{3,1},{4,6},{6,4},{5,7},{7,5},{8,10},{10,8},{9,1... | collective-permute-start | bytes 405512 | tf_op jit(solution)/shard_map/ppermute | solution.py:495
  155.5 5.6 %collective-permute-start.31 = (f32[264,128]{1,0:T(8,128)S(1)}, f32[264,128]{1,0:T(8,128)S(1)}, u32[]{:S(2)}, u32[]{:S(2)}) collective-permute-start(f32[264,128]{1,0:T(8,128)S(1)} %collective-permute-done.16.refs_1_), channel_id=1, source_target_pairs={{0,1},{1,0},{2,3},{3,2},{4,5},{5,4},{6,7},{7,6},{8,9},{9,8},{10,11... | collective-permute-start | bytes 405512 | tf_op jit(solution)/shard_map/ppermute | solution.py:495
  155.7 6.5 %collective-permute-start.18 = (f32[264,128]{1,0:T(8,128)S(1)}, f32[264,128]{1,0:T(8,128)S(1)}, u32[]{:S(2)}, u32[]{:S(2)}) collective-permute-start(f32[264,128]{1,0:T(8,128)S(1)} %collective-permute-done.16.refs_1_), channel_id=1, source_target_pairs={{0,2},{2,0},{1,3},{3,1},{4,6},{6,4},{5,7},{7,5},{8,10},{10,8},{9,1... | collective-permute-start | bytes 405512 | tf_op jit(solution)/shard_map/ppermute | solution.py:495
  160.2 5.5 %collective-permute-start.27 = (f32[264,128]{1,0:T(8,128)S(1)}, f32[264,128]{1,0:T(8,128)S(1)}, u32[]{:S(2)}, u32[]{:S(2)}) collective-permute-start(f32[264,128]{1,0:T(8,128)S(1)} %collective-permute-done.15.refs_12_), channel_id=1, source_target_pairs={{0,2},{2,0},{1,3},{3,1},{4,6},{6,4},{5,7},{7,5},{8,10},{10,8},{9,1... | collective-permute-start | bytes 405512 | tf_op jit(solution)/shard_map/ppermute | solution.py:495
  162.2 6.2 %collective-permute-start.26 = (f32[264,128]{1,0:T(8,128)S(1)}, f32[264,128]{1,0:T(8,128)S(1)}, u32[]{:S(2)}, u32[]{:S(2)}) collective-permute-start(f32[264,128]{1,0:T(8,128)S(1)} %collective-permute-done.24.refs_9_), channel_id=1, source_target_pairs={{0,2},{2,0},{1,3},{3,1},{4,6},{6,4},{5,7},{7,5},{8,10},{10,8},{9,1... | collective-permute-start | bytes 405512 | tf_op jit(solution)/shard_map/ppermute | solution.py:495
  165.7 6.4 %collective-permute-start.22 = (f32[264,128]{1,0:T(8,128)S(1)}, f32[264,128]{1,0:T(8,128)S(1)}, u32[]{:S(2)}, u32[]{:S(2)}) collective-permute-start(f32[264,128]{1,0:T(8,128)S(1)} %collective-permute-done.20.refs_5_), channel_id=1, source_target_pairs={{0,4},{4,0},{1,5},{5,1},{2,6},{6,2},{3,7},{7,3},{8,12},{12,8},{9,1... | collective-permute-start | bytes 405512 | tf_op jit(solution)/shard_map/ppermute | solution.py:495
  167.0 5.1 %collective-permute-start.33 = (f32[264,128]{1,0:T(8,128)S(1)}, f32[264,128]{1,0:T(8,128)S(1)}, u32[]{:S(2)}, u32[]{:S(2)}) collective-permute-start(f32[264,128]{1,0:T(8,128)S(1)} %collective-permute-done.18.refs_3_), channel_id=1, source_target_pairs={{0,1},{1,0},{2,3},{3,2},{4,5},{5,4},{6,7},{7,6},{8,9},{9,8},{10,11... | collective-permute-start | bytes 405512 | tf_op jit(solution)/shard_map/ppermute | solution.py:495
  168.4 6.2 %collective-permute-start.29 = (f32[264,128]{1,0:T(8,128)S(1)}, f32[264,128]{1,0:T(8,128)S(1)}, u32[]{:S(2)}, u32[]{:S(2)}) collective-permute-start(f32[264,128]{1,0:T(8,128)S(1)} %collective-permute-done.27.refs_13_), channel_id=1, source_target_pairs={{0,4},{4,0},{1,5},{5,1},{2,6},{6,2},{3,7},{7,3},{8,12},{12,8},{9,1... | collective-permute-start | bytes 405512 | tf_op jit(solution)/shard_map/ppermute | solution.py:495
  (24 other events, 153.9 us)

commit v6 on v5

--- a/solution.py
+++ b/solution.py
@@ -1,4 +1,5 @@
 import functools
+import math
 
 import jax
 import jax.numpy as jnp
@@ -415,23 +416,28 @@
 
 def assemble_kernel(sizes, *refs):
     outer, inner, chip, core = sizes
-    devices = outer * inner * chip * core
-    pieces, refs = refs[:devices], refs[devices:]
+    planes = inner * chip
+    operands, refs = refs[: 2 * core * planes], refs[2 * core * planes :]
     weight_in, weight_out, bias_in, bias_out, sems, bias_sem = refs
-    length = pieces[0].shape[0] - EXTRA
+    length = operands[0].shape[0] - EXTRA
     dim_in, hidden_size = weight_in.shape
     band = hidden_size // outer
     base = band // LANES * dim_in
     first = lax.axis_index("outer")
     plane = lax.axis_index("inner") * chip + lax.axis_index("chip")
     me = lax.axis_index("core")
+    pieces = []
+    for n, operand in enumerate(operands):
+        c, n = divmod(n, 2 * planes)
+        far, j = divmod(n, planes)
+        if far:
+            pieces += [(operand.at[k - 1], c, k, j) for k in range(1, outer)]
+        else:
+            pieces.append((operand, c, 0, j))
     copies = []
-    for n, piece in enumerate(pieces):
-        c, n = divmod(n, devices // core)
-        k, j = divmod(n, inner * chip)
-        n += c * (devices // core)
+    for n, (piece, c, k, j) in enumerate(pieces):
         o = lax.rem(first + outer - k, outer)
-        e = lax.bitwise_xor(plane, place(sizes, k, j)) * core + lax.bitwise_xor(me, c)
+        e = lax.bitwise_xor(plane, j) * core + lax.bitwise_xor(me, c)
         at = e * length
         source = piece.at[pl.ds(0, length)]
 
@@ -477,7 +483,7 @@
             jax.ShapeDtypeStruct((EXTRA, LANES), jnp.float32),
         ],
         scratch_shapes=[
-            pltpu.SemaphoreType.DMA((len(pieces),)),
+            pltpu.SemaphoreType.DMA((math.prod(sizes),)),
             pltpu.SemaphoreType.DMA,
         ],
         compiler_params=pltpu.CompilerParams(vmem_limit_bytes=4 * 2**20),
@@ -517,14 +523,17 @@
 
 def spread_chunks(sizes, total):
     outer, inner, chip, _ = sizes
-    near = []
-    for k in range(outer):
-        slow, fast = ("inner", "chip") if k % 2 else ("chip", "inner")
-        x = along(sizes, total, k) if k else total
-        row = [across(sizes, fast, x, j) if j else x for j in range(sizes[AXES.index(fast)])]
-        for j in range(sizes[AXES.index(slow)]):
-            near += [across(sizes, slow, x, j) if j else x for x in row]
-    return near
+    planes = inner * chip
+
+    def plane(x, j):
+        if j == 0:
+            return x
+        return lax.ppermute(x, ("inner", "chip"), [(p, p ^ j) for p in range(planes)])
+
+    line = [along(sizes, total, k) for k in range(1, outer)]
+    near = [plane(total, j) for j in range(planes)]
+    line = jnp.stack(line)
+    return near + [plane(line, j) for j in range(planes)]
 
 
 def per_device(
@@ -539,6 +548,7 @@
 
     outgoing, slots = route(devices, capacity, code_owner, code_row, latents, cotangent)
     outgoing, bias_in = lax.optimization_barrier((outgoing, bias_in))
+    taken, bias_in = lax.optimization_barrier((code_row[0] >= 0, bias_in))
     incoming = lax.all_to_all(outgoing, AXES, split_axis=0, concat_axis=0, tiled=True)
 
     hidden_t, codebook_t, slope, projected, parts = forward(
@@ -558,7 +568,7 @@
         return jnp.zeros((length + EXTRA, LANES), jnp.float32)
 
     total = lax.cond(
-        code_row[0] >= 0, reduce_half, nothing,
+        taken, reduce_half, nothing,
         incoming, wanted, hidden_t, slope, projected, codebook_t, weight_t,
     )
     total, answers = lax.optimization_barrier((total, answers))
@@ -569,8 +579,7 @@
     from_slot = slots.reshape(-1, 1) == slot_ids[None, :]
     chosen = pick(from_slot.astype(jnp.bfloat16), answers)
     latent_grad = cotangent - 0.25 * (chosen - latents)
-    late = len(near) - inner * chip
-    near[late], latent_grad = lax.optimization_barrier((near[late], latent_grad))
+    near[-1], latent_grad = lax.optimization_barrier((near[-1], latent_grad))
 
     chunks = near + [across(sizes, "core", x, 1) for x in near]
     gw_in, gw_out, gb_in, gb_out = assemble(sizes, chunks, dim_in, hidden_size, width)

time: 180 us -> 186 us (1.033)
  waiting for transfers between devices: 87.8 us -> 102 us
  starting transfers between devices: 44.2 us -> 35.9 us
    ppermute x0 -> x6, waiting for transfers between devices: none -> 17.4 us  [plane(): lax.ppermute(x, ('inner', 'chip'), [(p, p ^ j) for p in range(planes)])]
    ppermute x40 -> x20, starting transfers between devices: 22.7 us -> 8.38 us  [across(): return lax.ppermute(x, axis, [(p, p ^ j) for p in range(size)])]
    ppermute x40 -> x20, waiting for transfers between devices: 34.3 us -> 23.9 us  [across(): return lax.ppermute(x, axis, [(p, p ^ j) for p in range(size)])]
    ppermute x6, waiting for transfers between devices: 10.1 us -> 19.6 us  [along(): lax.ppermute(x, 'outer', [(o, (o + k) % outer) for o in range(outer)])]
    ppermute x0 -> x6, starting transfers between devices: none -> 6.1 us  [plane(): lax.ppermute(x, ('inner', 'chip'), [(p, p ^ j) for p in range(planes)])]
  transfers between devices with their start and end apart: 48 -> 34, of which waited for: 21 -> 15; matrix products, arithmetic and copies ran while one was open for 5% -> 5% of each run, Pallas kernels for 12% -> 11%
where the time goes in v6:
time: 186 us
  waiting for transfers between devices  102 us (55%)
  Pallas kernels  36.1 us (19%)
  starting transfers between devices  35.9 us (19%)
  other arithmetic  4.96 us (3%)
  matrix products  2.38 us (1%)
  local copies, waits for them, and re-layouts  2.05 us (1%)
    all_to_all x1, waiting for transfers between devices, per_device(): lax.all_to_all(outgoing, AXES, split_axis=0, concat_axis=0, tiled=True)  41.4 us
    ppermute x20, waiting for transfers between devices, across(): return lax.ppermute(x, axis, [(p, p ^ j) for p in range(size)])  23.9 us
    ppermute x6, waiting for transfers between devices, along(): lax.ppermute(x, 'outer', [(o, (o + k) % outer) for o in range(outer)])  19.6 us
    ppermute x6, waiting for transfers between devices, plane(): lax.ppermute(x, ('inner', 'chip'), [(p, p ^ j) for p in range(planes)])  17.4 us
    pallas_call x1, Pallas kernels, backward(): pl.pallas_call(functools.partial(backward_kernel, sizes, capacity), in_sp...  12.6 us
    ppermute x6, starting transfers between devices, along(): lax.ppermute(x, 'outer', [(o, (o + k) % outer) for o in range(outer)])  10 us
    pallas_call x1, Pallas kernels, forward(): pl.pallas_call(forward_kernel, grid=(rows // tile,), in_specs=[pl.BlockSp...  8.43 us
    ppermute x20, starting transfers between devices, across(): return lax.ppermute(x, axis, [(p, p ^ j) for p in range(size)])  8.38 us
  transfers between devices with their start and end apart: 34, of which 15 were waited for; matrix products, arithmetic and copies ran while one was open for 5% of the time, Pallas kernels for 11%

profile of v6, /device:TPU:0, one launch (start us, length us, event | category | flops | bytes accessed | tf_op | source)
XLA Modules:
  0.0 185.7 jit_solution(6671130827536752199)
XLA Ops:
  0.6 7.0 %route.1 = (f32[32,136,128]{2,1,0:T(8,128)}, s32[1,1024]{1,0:T(1,128)}) custom-call(s32[1,1024]{1,0:T(1,128)} %bitcast.50, s32[1,1024]{1,0:T(1,128)} %bitcast.51, f32[1024,256]{1,0:T(8,128)} %latents_hbm.1, f32[1024,256]{1,0:T(8,128)} %cotangent_hbm.1), custom_call_target="tpu_custom_call" | custom-call | tf_op jit(solution)/shard_map/route/pallas_call | solution.py:247
  7.6 7.4 %all-to-all-start = ((f32[32,136,128]{2,1,0:T(8,128)}), f32[32,136,128]{2,1,0:T(8,128)}, u32[]{:S(2)}, u32[]{:S(2)}) async-start(f32[32,136,128]{2,1,0:T(8,128)} %get-tuple-element.61), calls=%async_computation | async-start | bytes 4456448 | tf_op jit(solution)/shard_map/all_to_all | solution.py:552
  15.0 1.2 slice.87
  16.9 8.4 %forward.1 = (bf16[1024,1024]{1,0:T(8,128)(2,1)}, bf16[768,1024]{1,0:T(8,128)(2,1)}, f32[1024,1024]{1,0:T(8,128)}, f32[1024,256]{1,0:T(8,128)}, bf16[1024,512]{1,0:T(8,128)(2,1)}) custom-call(bf16[1024,768]{1,0:T(8,128)(2,1)} %codebook_ref.1, bf16[768,1024]{1,0:T(8,128)(2,1)} %weight_in_ref.1, f32[1,1024]{1,0:T(1,128)} %bitcast.52, ...), custom_call_target="tpu_custom_call" | custom-call | flops 2147483648 | bytes 14680064 | tf_op jit(solution)/shard_map/forward/pallas_call | solution.py:63
  25.3 41.4 %all-to-all-done.incoming_hbm = f32[32,136,128]{2,1,0:T(8,128)} async-done(((f32[32,136,128]{2,1,0:T(8,128)}), f32[32,136,128]{2,1,0:T(8,128)}, u32[]{:S(2)}, u32[]{:S(2)}) %all-to-all-start) | async-done | bytes 2228256 | tf_op jit(solution)/shard_map/all_to_all | solution.py:552
  66.8 5.2 %pick_rows.1 = (f32[32,64,256]{2,1,0:T(8,128)}, f32[8,2048]{1,0:T(8,128)S(1)}) custom-call(f32[32,136,128]{2,1,0:T(8,128)} %all-to-all-done.incoming_hbm, bf16[1024,512]{1,0:T(8,128)(2,1)} %get-tuple-element.63.parts_hbm), custom_call_target="tpu_custom_call" | custom-call | flops 2147483648 | bytes 4194304 | tf_op jit(solution)/shard_map/pick_rows/pallas_call | solution.py:144
  72.0 4.0 %all-to-all-start.1 = ((f32[32,64,256]{2,1,0:T(8,128)}), f32[32,64,256]{2,1,0:T(8,128)S(1)}, u32[]{:S(2)}, u32[]{:S(2)}) async-start(f32[32,64,256]{2,1,0:T(8,128)} %get-tuple-element.69), calls=%async_computation.1 | async-start | bytes 4194304 | tf_op jit(solution)/shard_map/all_to_all | solution.py:558
  76.2 60.7 %conditional.1 = (f32[264,128]{1,0:T(8,128)S(1)}) conditional(s32[]{:T(128)} %convert_element_type.10, () %tuple.20, (f32[32,136,128]{2,1,0:T(8,128)}, f32[8,2048]{1,0:T(8,128)S(1)}, bf16[1024,1024]{1,0:T(8,128)(2,1)}, f32[1024,1024]{1,0:T(8,128)}, f32[1024,256]{1,0:T(8,128)}, /*index=5*/bf16[768,1024]{1,0:T(8,128)(2,1)}, ...), branch_computations={%region_0.0_spmd, %region_1.0_spmd} | conditional | flops 4832885760 | bytes 52867792 | solution.py:570
  76.4 12.6 %backward.1 = (f32[4,264,128]{2,1,0:T(8,128)}, f32[4,264,128]{2,1,0:T(8,128)}, f32[4,264,128]{2,1,0:T(8,128)}, f32[4,264,128]{2,1,0:T(8,128)}, f32[4,264,128]{2,...) custom-call(f32[32,136,128]{2,1,0:T(8,128)} %get-tuple-element.6.incoming_hbm, ...), custom_call_target="tpu_custom_call" | custom-call | flops 4831838208 | bytes 16777216 | tf_op jit(solution)/shard_map/cond/branch_1_fun/backward/pallas_call | solution.py:392
  92.3 1.8 collective-permute-start.1
  95.1 1.5 collective-permute-start.4
  98.7 9.3 %collective-permute-done.1 = f32[2,264,128]{2,1,0:T(8,128)S(1)} collective-permute-done((f32[2,264,128]{2,1,0:T(8,128)S(1)}, f32[2,264,128]{2,1,0:T(8,128)S(1)}, u32[]{:S(2)}, u32[]{:S(2)}) %collective-permute-start.1) | collective-permute-done | bytes 270368 | tf_op jit(solution)/shard_map/cond/branch_1_fun/ppermute | solution.py:501
  109.7 4.0 %collective-permute-done.8 = f32[2,264,128]{2,1,0:T(8,128)S(1)} collective-permute-done((f32[2,264,128]{2,1,0:T(8,128)S(1)}, f32[2,264,128]{2,1,0:T(8,128)S(1)}, u32[]{:S(2)}, u32[]{:S(2)}) %collective-permute-start.8) | collective-permute-done | bytes 270368 | tf_op jit(solution)/shard_map/cond/branch_1_fun/ppermute | solution.py:501
  114.1 2.1 %collective-permute-done.12 = f32[2,264,128]{2,1,0:T(8,128)S(1)} collective-permute-done((f32[2,264,128]{2,1,0:T(8,128)S(1)}, f32[2,264,128]{2,1,0:T(8,128)S(1)}, u32[]{:S(2)}, u32[]{:S(2)}) %collective-permute-start.12) | collective-permute-done | bytes 270368 | tf_op jit(solution)/shard_map/cond/branch_1_fun/ppermute | solution.py:501
  116.4 3.0 %collective-permute-start.6 = (f32[264,128]{1,0:T(8,128)S(1)}, f32[264,128]{1,0:T(8,128)S(1)}, u32[]{:S(2)}, u32[]{:S(2)}) collective-permute-start(f32[264,128]{1,0:T(8,128)S(1)} %fusion.6), channel_id=1, source_target_pairs={{0,24},{8,0},{16,8},{24,16},{1,25},{9,1},{17,9},{25,17},{2,26},{10... | collective-permute-start | bytes 405512 | tf_op jit(solution)/shard_map/cond/branch_1_fun/ppermute | solution.py:496
  119.3 4.1 %collective-permute-done.9 = f32[264,128]{1,0:T(8,128)S(1)} collective-permute-done((f32[264,128]{1,0:T(8,128)S(1)}, f32[264,128]{1,0:T(8,128)S(1)}, u32[]{:S(2)}, u32[]{:S(2)}) %collective-permute-start.9) | collective-permute-done | bytes 135200 | tf_op jit(solution)/shard_map/cond/branch_1_fun/ppermute | solution.py:501
  123.4 2.2 %collective-permute-start.10 = (f32[264,128]{1,0:T(8,128)S(1)}, f32[264,128]{1,0:T(8,128)S(1)}, u32[]{:S(2)}, u32[]{:S(2)}) collective-permute-start(f32[264,128]{1,0:T(8,128)S(1)} %fusion.5), channel_id=1, source_target_pairs={{0,16},{8,24},{16,0},{24,8},{1,17},{9,25},{17,1},{25,9},{2,18},{10... | collective-permute-start | bytes 405512 | tf_op jit(solution)/shard_map/cond/branch_1_fun/ppermute | solution.py:496
  125.6 1.7 collective-permute-start.14
  127.3 9.4 %collective-permute-done.10 = f32[264,128]{1,0:T(8,128)S(1)} collective-permute-done((f32[264,128]{1,0:T(8,128)S(1)}, f32[264,128]{1,0:T(8,128)S(1)}, u32[]{:S(2)}, u32[]{:S(2)}) %collective-permute-start.10) | collective-permute-done | bytes 135200 | tf_op jit(solution)/shard_map/cond/branch_1_fun/ppermute | solution.py:496
  137.1 2.1 %collective-permute-start.21 = (f32[264,128]{1,0:T(8,128)S(1)}, f32[264,128]{1,0:T(8,128)S(1)}, u32[]{:S(2)}, u32[]{:S(2)}) collective-permute-start(f32[264,128]{1,0:T(8,128)S(1)} %get-tuple-element.81.refs_0_), channel_id=1, source_target_pairs={{0,6},{2,4},{4,2},{6,0},{1,7},{3,5},{5,3},{7,1},{8,14},{10,12},{12... | collective-permute-start | bytes 405512 | tf_op jit(solution)/shard_map/ppermute | solution.py:531
  139.2 1.1 collective-permute-start.16
  140.3 2.0 %collective-permute-start.15 = (f32[264,128]{1,0:T(8,128)S(1)}, f32[264,128]{1,0:T(8,128)S(1)}, u32[]{:S(2)}, u32[]{:S(2)}) collective-permute-start(f32[264,128]{1,0:T(8,128)S(1)} %get-tuple-element.81.refs_0_), channel_id=1, source_target_pairs={{0,8},{8,16},{16,24},{24,0},{1,9},{9,17},{17,25},{25,1},{2,10},{10... | collective-permute-start | bytes 405512 | tf_op jit(solution)/shard_map/ppermute | solution.py:496
  142.7 3.2 %collective-permute-done.17 = f32[264,128]{1,0:T(8,128)S(1)} collective-permute-done((f32[264,128]{1,0:T(8,128)S(1)}, f32[264,128]{1,0:T(8,128)S(1)}, u32[]{:S(2)}, u32[]{:S(2)}) %collective-permute-start.17) | collective-permute-done | bytes 135200 | tf_op jit(solution)/shard_map/ppermute | solution.py:496
  145.9 7.1 %collective-permute-done.16 = f32[264,128]{1,0:T(8,128)S(1)} collective-permute-done((f32[264,128]{1,0:T(8,128)S(1)}, f32[264,128]{1,0:T(8,128)S(1)}, u32[]{:S(2)}, u32[]{:S(2)}) %collective-permute-start.16) | collective-permute-done | bytes 135200 | tf_op jit(solution)/shard_map/ppermute | solution.py:496
  154.0 2.5 %collective-permute-start.18 = (f32[3,264,128]{2,1,0:T(8,128)S(1)}, f32[3,264,128]{2,1,0:T(8,128)S(1)}, u32[]{:S(2)}, u32[]{:S(2)}) collective-permute-start(f32[3,264,128]{2,1,0:T(8,128)S(1)} %pad_maximum_fusion.refs_4_), channel_id=1, source_target_pairs={{0,6},{2,4},{4,2},{6,0},{1,7},{3,5},{5,3},{7,1},{8,14},{10,12},{12... | collective-permute-start | bytes 1216520 | tf_op jit(solution)/shard_map/ppermute | solution.py:531
  156.5 2.4 %fusion.11 = f32[1024,512]{1,0:T(8,128)S(1)} fusion(s32[1024]{0:T(1024)S(1)} %bitcast.53, bf16[2048,256]{1,0:T(8,128)(2,1)S(1)} %get-tuple-element.80, bf16[2048,256]{1,0:T(8,128)(2,1)S(1)} %get-tuple-element.79), kind=kOutput, calls=%fused_computation.28 | convolution fusion | flops 2153775104 | bytes 4198400 | tf_op jit(solution)/shard_map/dot_general | solution.py:35
  159.1 14.9 %collective-permute-done.18.refs_7_ = f32[3,264,128]{2,1,0:T(8,128)S(1)} collective-permute-done((f32[3,264,128]{2,1,0:T(8,128)S(1)}, f32[3,264,128]{2,1,0:T(8,128)S(1)}, u32[]{:S(2)}, u32[]{:S(2)}) %collective-permute-start.18) | collective-permute-done | bytes 405536 | tf_op jit(solution)/shard_map/ppermute | solution.py:531
  174.2 1.2 fusion.19
  176.5 2.4 %collective-permute-done.19.refs_1_ = f32[264,128]{1,0:T(8,128)S(1)} collective-permute-done((f32[264,128]{1,0:T(8,128)S(1)}, f32[264,128]{1,0:T(8,128)S(1)}, u32[]{:S(2)}, u32[]{:S(2)}) %collective-permute-start.19) | collective-permute-done | bytes 135200 | tf_op jit(solution)/shard_map/ppermute | solution.py:531
  179.5 1.4 collective-permute-done.26.refs_10_
  181.0 1.2 collective-permute-done.25.refs_9_
  182.3 2.9 %assemble.1 = (f32[768,1024]{1,0:T(8,128)}, f32[1024,256]{1,0:T(8,128)}, f32[8,128]{1,0:T(8,128)}, f32[8,128]{1,0:T(8,128)S(1)}) custom-call(f32[264,128]{1,0:T(8,128)S(1)} %get-tuple-element.81.refs_0_, f32[264,128]{1,0:T(8,128)S(1)} %collective-permute-done.19.refs_1_, f32[264,128]{1,0:T(8,128)S(1)} %collective-permute-done.20.refs_2_, ...), custom_call_target="tpu_custom_call" | custom-call | tf_op jit(solution)/shard_map/assemble/pallas_call | solution.py:475
  (81 shorter events, 12.9 us)
Async XLA Ops:
  7.6 59.1 %all-to-all-start = ((f32[32,136,128]{2,1,0:T(8,128)}), f32[32,136,128]{2,1,0:T(8,128)}, u32[]{:S(2)}, u32[]{:S(2)}) async-start(f32[32,136,128]{2,1,0:T(8,128)} %get-tuple-element.61), calls=%async_computation | async-start | bytes 4456448 | tf_op jit(solution)/shard_map/all_to_all | solution.py:552
  72.0 65.0 %all-to-all-start.1 = ((f32[32,64,256]{2,1,0:T(8,128)}), f32[32,64,256]{2,1,0:T(8,128)S(1)}, u32[]{:S(2)}, u32[]{:S(2)}) async-start(f32[32,64,256]{2,1,0:T(8,128)} %get-tuple-element.69), calls=%async_computation.1 | async-start | bytes 4194304 | tf_op jit(solution)/shard_map/all_to_all | solution.py:558
  89.1 2.2 %collective-permute-start = (f32[4,264,128]{2,1,0:T(8,128)}, f32[4,264,128]{2,1,0:T(8,128)S(1)}, u32[]{:S(2)}, u32[]{:S(2)}) collective-permute-start(f32[4,264,128]{2,1,0:T(8,128)} %get-tuple-element.25), channel_id=1, source_target_pairs={{0,1},{1,0},{2,3},{3,2},{4,5},{5,4},{6,7},{7,6},{8,9},{9,8},{10,11... | collective-permute-start | bytes 1622024 | tf_op jit(solution)/shard_map/cond/branch_1_fun/ppermute | solution.py:501
  89.4 4.7 %collective-permute-start.3 = (f32[4,264,128]{2,1,0:T(8,128)}, f32[4,264,128]{2,1,0:T(8,128)S(1)}, u32[]{:S(2)}, u32[]{:S(2)}) collective-permute-start(f32[4,264,128]{2,1,0:T(8,128)} %get-tuple-element.27), channel_id=1, source_target_pairs={{0,1},{1,0},{2,3},{3,2},{4,5},{5,4},{6,7},{7,6},{8,9},{9,8},{10,11... | collective-permute-start | bytes 1622024 | tf_op jit(solution)/shard_map/cond/branch_1_fun/ppermute | solution.py:501
  89.7 7.0 %collective-permute-start.7 = (f32[4,264,128]{2,1,0:T(8,128)}, f32[4,264,128]{2,1,0:T(8,128)S(1)}, u32[]{:S(2)}, u32[]{:S(2)}) collective-permute-start(f32[4,264,128]{2,1,0:T(8,128)} %get-tuple-element.29), channel_id=1, source_target_pairs={{0,1},{1,0},{2,3},{3,2},{4,5},{5,4},{6,7},{7,6},{8,9},{9,8},{10,11... | collective-permute-start | bytes 1622024 | tf_op jit(solution)/shard_map/cond/branch_1_fun/ppermute | solution.py:501
  89.9 8.4 %collective-permute-start.11 = (f32[4,264,128]{2,1,0:T(8,128)}, f32[4,264,128]{2,1,0:T(8,128)S(1)}, u32[]{:S(2)}, u32[]{:S(2)}) collective-permute-start(f32[4,264,128]{2,1,0:T(8,128)} %get-tuple-element.31), channel_id=1, source_target_pairs={{0,1},{1,0},{2,3},{3,2},{4,5},{5,4},{6,7},{7,6},{8,9},{9,8},{10,11... | collective-permute-start | bytes 1622024 | tf_op jit(solution)/shard_map/cond/branch_1_fun/ppermute | solution.py:501
  92.3 15.7 %collective-permute-start.1 = (f32[2,264,128]{2,1,0:T(8,128)S(1)}, f32[2,264,128]{2,1,0:T(8,128)S(1)}, u32[]{:S(2)}, u32[]{:S(2)}) collective-permute-start(f32[2,264,128]{2,1,0:T(8,128)S(1)} %slice_add_fusion.6), channel_id=1, source_target_pairs={{0,2},{2,0},{1,3},{3,1},{4,6},{6,4},{5,7},{7,5},{8,10},{10,8},{9,1... | collective-permute-start | bytes 811016 | tf_op jit(solution)/shard_map/cond/branch_1_fun/ppermute | solution.py:501
  95.1 13.7 %collective-permute-start.4 = (f32[2,264,128]{2,1,0:T(8,128)S(1)}, f32[2,264,128]{2,1,0:T(8,128)S(1)}, u32[]{:S(2)}, u32[]{:S(2)}) collective-permute-start(f32[2,264,128]{2,1,0:T(8,128)S(1)} %slice_add_fusion.4), channel_id=1, source_target_pairs={{0,4},{4,0},{1,5},{5,1},{2,6},{6,2},{3,7},{7,3},{8,12},{12,8},{9,1... | collective-permute-start | bytes 811016 | tf_op jit(solution)/shard_map/cond/branch_1_fun/ppermute | solution.py:501
  97.7 16.1 %collective-permute-start.8 = (f32[2,264,128]{2,1,0:T(8,128)S(1)}, f32[2,264,128]{2,1,0:T(8,128)S(1)}, u32[]{:S(2)}, u32[]{:S(2)}) collective-permute-start(f32[2,264,128]{2,1,0:T(8,128)S(1)} %slice_add_fusion.2), channel_id=1, source_target_pairs={{0,2},{2,0},{1,3},{3,1},{4,6},{6,4},{5,7},{7,5},{8,10},{10,8},{9,1... | collective-permute-start | bytes 811016 | tf_op jit(solution)/shard_map/cond/branch_1_fun/ppermute | solution.py:501
  98.4 17.8 %collective-permute-start.12 = (f32[2,264,128]{2,1,0:T(8,128)S(1)}, f32[2,264,128]{2,1,0:T(8,128)S(1)}, u32[]{:S(2)}, u32[]{:S(2)}) collective-permute-start(f32[2,264,128]{2,1,0:T(8,128)S(1)} %slice_add_fusion), channel_id=1, source_target_pairs={{0,4},{4,0},{1,5},{5,1},{2,6},{6,2},{3,7},{7,3},{8,12},{12,8},{9,1... | collective-permute-start | bytes 811016 | tf_op jit(solution)/shard_map/cond/branch_1_fun/ppermute | solution.py:501
  108.0 19.3 %collective-permute-start.2 = (f32[264,128]{1,0:T(8,128)S(1)}, f32[264,128]{1,0:T(8,128)S(1)}, u32[]{:S(2)}, u32[]{:S(2)}) collective-permute-start(f32[264,128]{1,0:T(8,128)S(1)} %slice_bitcast_fusion.6), channel_id=1, source_target_pairs={{0,4},{4,0},{1,5},{5,1},{2,6},{6,2},{3,7},{7,3},{8,12},{12,8},{9,1... | collective-permute-start | bytes 405512 | tf_op jit(solution)/shard_map/cond/branch_1_fun/ppermute | solution.py:501
  108.9 7.4 %collective-permute-start.5 = (f32[264,128]{1,0:T(8,128)S(1)}, f32[264,128]{1,0:T(8,128)S(1)}, u32[]{:S(2)}, u32[]{:S(2)}) collective-permute-start(f32[264,128]{1,0:T(8,128)S(1)} %slice_bitcast_fusion.4), channel_id=1, source_target_pairs={{0,2},{2,0},{1,3},{3,1},{4,6},{6,4},{5,7},{7,5},{8,10},{10,8},{9,1... | collective-permute-start | bytes 405512 | tf_op jit(solution)/shard_map/cond/branch_1_fun/ppermute | solution.py:501
  113.9 9.6 %collective-permute-start.9 = (f32[264,128]{1,0:T(8,128)S(1)}, f32[264,128]{1,0:T(8,128)S(1)}, u32[]{:S(2)}, u32[]{:S(2)}) collective-permute-start(f32[264,128]{1,0:T(8,128)S(1)} %slice_bitcast_fusion.2), channel_id=1, source_target_pairs={{0,4},{4,0},{1,5},{5,1},{2,6},{6,2},{3,7},{7,3},{8,12},{12,8},{9,1... | collective-permute-start | bytes 405512 | tf_op jit(solution)/shard_map/cond/branch_1_fun/ppermute | solution.py:501
  116.2 9.4 %collective-permute-start.13 = (f32[264,128]{1,0:T(8,128)S(1)}, f32[264,128]{1,0:T(8,128)S(1)}, u32[]{:S(2)}, u32[]{:S(2)}) collective-permute-start(f32[264,128]{1,0:T(8,128)S(1)} %slice_bitcast_fusion), channel_id=1, source_target_pairs={{0,2},{2,0},{1,3},{3,1},{4,6},{6,4},{5,7},{7,5},{8,10},{10,8},{9,1... | collective-permute-start | bytes 405512 | tf_op jit(solution)/shard_map/cond/branch_1_fun/ppermute | solution.py:501
  116.4 11.0 %collective-permute-start.6 = (f32[264,128]{1,0:T(8,128)S(1)}, f32[264,128]{1,0:T(8,128)S(1)}, u32[]{:S(2)}, u32[]{:S(2)}) collective-permute-start(f32[264,128]{1,0:T(8,128)S(1)} %fusion.6), channel_id=1, source_target_pairs={{0,24},{8,0},{16,8},{24,16},{1,25},{9,1},{17,9},{25,17},{2,26},{10... | collective-permute-start | bytes 405512 | tf_op jit(solution)/shard_map/cond/branch_1_fun/ppermute | solution.py:496
  123.4 13.3 %collective-permute-start.10 = (f32[264,128]{1,0:T(8,128)S(1)}, f32[264,128]{1,0:T(8,128)S(1)}, u32[]{:S(2)}, u32[]{:S(2)}) collective-permute-start(f32[264,128]{1,0:T(8,128)S(1)} %fusion.5), channel_id=1, source_target_pairs={{0,16},{8,24},{16,0},{24,8},{1,17},{9,25},{17,1},{25,9},{2,18},{10... | collective-permute-start | bytes 405512 | tf_op jit(solution)/shard_map/cond/branch_1_fun/ppermute | solution.py:496
  125.6 11.0 %collective-permute-start.14 = (f32[264,128]{1,0:T(8,128)S(1)}, f32[264,128]{1,0:T(8,128)S(1)}, u32[]{:S(2)}, u32[]{:S(2)}) collective-permute-start(f32[264,128]{1,0:T(8,128)S(1)} %fusion.4), channel_id=1, source_target_pairs={{0,8},{8,16},{16,24},{24,0},{1,9},{9,17},{17,25},{25,1},{2,10},{10... | collective-permute-start | bytes 405512 | tf_op jit(solution)/shard_map/cond/branch_1_fun/ppermute | solution.py:496
  137.0 21.9 %collective-permute-start.24 = (f32[264,128]{1,0:T(8,128)S(1)}, f32[264,128]{1,0:T(8,128)S(1)}, u32[]{:S(2)}, u32[]{:S(2)}) collective-permute-start(f32[264,128]{1,0:T(8,128)S(1)} %get-tuple-element.81.refs_0_), channel_id=1, source_target_pairs={{0,1},{1,0},{2,3},{3,2},{4,5},{5,4},{6,7},{7,6},{8,9},{9,8},{10,11... | collective-permute-start | bytes 405512 | tf_op jit(solution)/shard_map/ppermute | solution.py:501
  137.1 38.4 %collective-permute-start.21 = (f32[264,128]{1,0:T(8,128)S(1)}, f32[264,128]{1,0:T(8,128)S(1)}, u32[]{:S(2)}, u32[]{:S(2)}) collective-permute-start(f32[264,128]{1,0:T(8,128)S(1)} %get-tuple-element.81.refs_0_), channel_id=1, source_target_pairs={{0,6},{2,4},{4,2},{6,0},{1,7},{3,5},{5,3},{7,1},{8,14},{10,12},{12... | collective-permute-start | bytes 405512 | tf_op jit(solution)/shard_map/ppermute | solution.py:531
  139.2 6.7 %collective-permute-start.17 = (f32[264,128]{1,0:T(8,128)S(1)}, f32[264,128]{1,0:T(8,128)S(1)}, u32[]{:S(2)}, u32[]{:S(2)}) collective-permute-start(f32[264,128]{1,0:T(8,128)S(1)} %get-tuple-element.81.refs_0_), channel_id=1, source_target_pairs={{0,24},{8,0},{16,8},{24,16},{1,25},{9,1},{17,9},{25,17},{2,26},{10... | collective-permute-start | bytes 405512 | tf_op jit(solution)/shard_map/ppermute | solution.py:496
  139.2 13.7 %collective-permute-start.16 = (f32[264,128]{1,0:T(8,128)S(1)}, f32[264,128]{1,0:T(8,128)S(1)}, u32[]{:S(2)}, u32[]{:S(2)}) collective-permute-start(f32[264,128]{1,0:T(8,128)S(1)} %get-tuple-element.81.refs_0_), channel_id=1, source_target_pairs={{0,16},{8,24},{16,0},{24,8},{1,17},{9,25},{17,1},{25,9},{2,18},{10... | collective-permute-start | bytes 405512 | tf_op jit(solution)/shard_map/ppermute | solution.py:496
  140.3 12.6 %collective-permute-start.15 = (f32[264,128]{1,0:T(8,128)S(1)}, f32[264,128]{1,0:T(8,128)S(1)}, u32[]{:S(2)}, u32[]{:S(2)}) collective-permute-start(f32[264,128]{1,0:T(8,128)S(1)} %get-tuple-element.81.refs_0_), channel_id=1, source_target_pairs={{0,8},{8,16},{16,24},{24,0},{1,9},{9,17},{17,25},{25,1},{2,10},{10... | collective-permute-start | bytes 405512 | tf_op jit(solution)/shard_map/ppermute | solution.py:496
  153.0 23.0 %collective-permute-start.23 = (f32[3,264,128]{2,1,0:T(8,128)S(1)}, f32[3,264,128]{2,1,0:T(8,128)S(1)}, u32[]{:S(2)}, u32[]{:S(2)}) collective-permute-start(f32[3,264,128]{2,1,0:T(8,128)S(1)} %pad_maximum_fusion.refs_4_), channel_id=1, source_target_pairs={{0,4},{2,6},{4,0},{6,2},{1,5},{3,7},{5,1},{7,3},{8,12},{10,14},{12... | collective-permute-start | bytes 1216520 | tf_op jit(solution)/shard_map/ppermute | solution.py:531
  153.0 23.0 %collective-permute-start.22 = (f32[3,264,128]{2,1,0:T(8,128)S(1)}, f32[3,264,128]{2,1,0:T(8,128)S(1)}, u32[]{:S(2)}, u32[]{:S(2)}) collective-permute-start(f32[3,264,128]{2,1,0:T(8,128)S(1)} %pad_maximum_fusion.refs_4_), channel_id=1, source_target_pairs={{0,2},{2,0},{4,6},{6,4},{1,3},{3,1},{5,7},{7,5},{8,10},{10,8},{12,... | collective-permute-start | bytes 1216520 | tf_op jit(solution)/shard_map/ppermute | solution.py:531
  154.0 20.0 %collective-permute-start.18 = (f32[3,264,128]{2,1,0:T(8,128)S(1)}, f32[3,264,128]{2,1,0:T(8,128)S(1)}, u32[]{:S(2)}, u32[]{:S(2)}) collective-permute-start(f32[3,264,128]{2,1,0:T(8,128)S(1)} %pad_maximum_fusion.refs_4_), channel_id=1, source_target_pairs={{0,6},{2,4},{4,2},{6,0},{1,7},{3,5},{5,3},{7,1},{8,14},{10,12},{12... | collective-permute-start | bytes 1216520 | tf_op jit(solution)/shard_map/ppermute | solution.py:531
  158.9 16.6 %collective-permute-start.20 = (f32[264,128]{1,0:T(8,128)S(1)}, f32[264,128]{1,0:T(8,128)S(1)}, u32[]{:S(2)}, u32[]{:S(2)}) collective-permute-start(f32[264,128]{1,0:T(8,128)S(1)} %get-tuple-element.81.refs_0_), channel_id=1, source_target_pairs={{0,4},{2,6},{4,0},{6,2},{1,5},{3,7},{5,1},{7,3},{8,12},{10,14},{12... | collective-permute-start | bytes 405512 | tf_op jit(solution)/shard_map/ppermute | solution.py:531
  173.9 5.0 %collective-permute-start.19 = (f32[264,128]{1,0:T(8,128)S(1)}, f32[264,128]{1,0:T(8,128)S(1)}, u32[]{:S(2)}, u32[]{:S(2)}) collective-permute-start(f32[264,128]{1,0:T(8,128)S(1)} %get-tuple-element.81.refs_0_), channel_id=1, source_target_pairs={{0,2},{2,0},{4,6},{6,4},{1,3},{3,1},{5,7},{7,5},{8,10},{10,8},{12,... | collective-permute-start | bytes 405512 | tf_op jit(solution)/shard_map/ppermute | solution.py:531
  175.5 6.8 %collective-permute-start.28 = (f32[3,264,128]{2,1,0:T(8,128)S(1)}, f32[3,264,128]{2,1,0:T(8,128)S(1)}, u32[]{:S(2)}, u32[]{:S(2)}) collective-permute-start(f32[3,264,128]{2,1,0:T(8,128)S(1)} %pad_maximum_fusion.refs_4_), channel_id=1, source_target_pairs={{0,1},{1,0},{2,3},{3,2},{4,5},{5,4},{6,7},{7,6},{8,9},{9,8},{10,11... | collective-permute-start | bytes 1216520 | tf_op jit(solution)/shard_map/ppermute | solution.py:501
  175.5 3.4 %collective-permute-start.27 = (f32[264,128]{1,0:T(8,128)S(1)}, f32[264,128]{1,0:T(8,128)S(1)}, u32[]{:S(2)}, u32[]{:S(2)}) collective-permute-start(f32[264,128]{1,0:T(8,128)S(1)} %collective-permute-done.21.refs_3_), channel_id=1, source_target_pairs={{0,1},{1,0},{2,3},{3,2},{4,5},{5,4},{6,7},{7,6},{8,9},{9,8},{10,11... | collective-permute-start | bytes 405512 | tf_op jit(solution)/shard_map/ppermute | solution.py:501
  176.0 6.3 %collective-permute-start.30 = (f32[3,264,128]{2,1,0:T(8,128)S(1)}, f32[3,264,128]{2,1,0:T(8,128)S(1)}, u32[]{:S(2)}, u32[]{:S(2)}) collective-permute-start(f32[3,264,128]{2,1,0:T(8,128)S(1)} %collective-permute-done.23.refs_6_), channel_id=1, source_target_pairs={{0,1},{1,0},{2,3},{3,2},{4,5},{5,4},{6,7},{7,6},{8,9},{9,8},{10,11... | collective-permute-start | bytes 1216520 | tf_op jit(solution)/shard_map/ppermute | solution.py:501
  176.1 6.2 %collective-permute-start.29 = (f32[3,264,128]{2,1,0:T(8,128)S(1)}, f32[3,264,128]{2,1,0:T(8,128)S(1)}, u32[]{:S(2)}, u32[]{:S(2)}) collective-permute-start(f32[3,264,128]{2,1,0:T(8,128)S(1)} %collective-permute-done.22.refs_5_), channel_id=1, source_target_pairs={{0,1},{1,0},{2,3},{3,2},{4,5},{5,4},{6,7},{7,6},{8,9},{9,8},{10,11... | collective-permute-start | bytes 1216520 | tf_op jit(solution)/shard_map/ppermute | solution.py:501
  179.0 3.3 %collective-permute-start.31 = (f32[3,264,128]{2,1,0:T(8,128)S(1)}, f32[3,264,128]{2,1,0:T(8,128)S(1)}, u32[]{:S(2)}, u32[]{:S(2)}) collective-permute-start(f32[3,264,128]{2,1,0:T(8,128)S(1)} %collective-permute-done.18.refs_7_), channel_id=1, source_target_pairs={{0,1},{1,0},{2,3},{3,2},{4,5},{5,4},{6,7},{7,6},{8,9},{9,8},{10,11... | collective-permute-start | bytes 1216520 | tf_op jit(solution)/shard_map/ppermute | solution.py:501
  (10 other events, 124.2 us)

commit v7 on v5

--- a/solution.py
+++ b/solution.py
@@ -539,6 +539,7 @@
 
     outgoing, slots = route(devices, capacity, code_owner, code_row, latents, cotangent)
     outgoing, bias_in = lax.optimization_barrier((outgoing, bias_in))
+    taken, bias_in = lax.optimization_barrier((code_row[0] >= 0, bias_in))
     incoming = lax.all_to_all(outgoing, AXES, split_axis=0, concat_axis=0, tiled=True)
 
     hidden_t, codebook_t, slope, projected, parts = forward(
@@ -558,7 +559,7 @@
         return jnp.zeros((length + EXTRA, LANES), jnp.float32)
 
     total = lax.cond(
-        code_row[0] >= 0, reduce_half, nothing,
+        taken, reduce_half, nothing,
         incoming, wanted, hidden_t, slope, projected, codebook_t, weight_t,
     )
     total, answers = lax.optimization_barrier((total, answers))

time: 180 us -> 181 us (level)
  starting transfers between devices: 44.2 us -> 46.7 us
  waiting for transfers between devices: 87.8 us -> 85.7 us
    all_to_all x1, waiting for transfers between devices: 43.3 us -> 41.4 us  [per_device(): lax.all_to_all(outgoing, AXES, split_axis=0, concat_axis=0, tiled=True)]
  transfers between devices with their start and end apart: 48 -> 48, of which waited for: 21 -> 19; matrix products, arithmetic and copies ran while one was open for 5% -> 5% of each run, Pallas kernels for 12% -> 12%
where the time goes in v7:
time: 181 us
  waiting for transfers between devices  85.7 us (47%)
  starting transfers between devices  46.7 us (26%)
  Pallas kernels  36.9 us (20%)
  other arithmetic  4.94 us (3%)
  matrix products  2.38 us (1%)
  local copies, waits for them, and re-layouts  2.06 us (1%)
    all_to_all x1, waiting for transfers between devices, per_device(): lax.all_to_all(outgoing, AXES, split_axis=0, concat_axis=0, tiled=True)  41.4 us
    ppermute x40, waiting for transfers between devices, across(): return lax.ppermute(x, axis, [(p, p ^ j) for p in range(size)])  34.4 us
    ppermute x40, starting transfers between devices, across(): return lax.ppermute(x, axis, [(p, p ^ j) for p in range(size)])  24 us
    pallas_call x1, Pallas kernels, backward(): pl.pallas_call(functools.partial(backward_kernel, sizes, capacity), in_sp...  12.6 us
    ppermute x6, starting transfers between devices, along(): lax.ppermute(x, 'outer', [(o, (o + k) % outer) for o in range(outer)])  11.4 us
    ppermute x6, waiting for transfers between devices, along(): lax.ppermute(x, 'outer', [(o, (o + k) % outer) for o in range(outer)])  9.91 us
    pallas_call x1, Pallas kernels, forward(): pl.pallas_call(forward_kernel, grid=(rows // tile,), in_specs=[pl.BlockSp...  8.43 us
    all_to_all x1, starting transfers between devices, per_device(): lax.all_to_all(outgoing, AXES, split_axis=0, concat_axis=0, tiled=True)  7.3 us
  transfers between devices with their start and end apart: 48, of which 19 were waited for; matrix products, arithmetic and copies ran while one was open for 5% of the time, Pallas kernels for 12%

profile of v7, /device:TPU:0, one launch (start us, length us, event | category | flops | bytes accessed | tf_op | source)
XLA Modules:
  0.0 180.7 jit_solution(9751650797897154143)
XLA Ops:
  0.6 7.0 %route.1 = (f32[32,136,128]{2,1,0:T(8,128)}, s32[1,1024]{1,0:T(1,128)}) custom-call(s32[1,1024]{1,0:T(1,128)} %bitcast.44, s32[1,1024]{1,0:T(1,128)} %bitcast.45, f32[1024,256]{1,0:T(8,128)} %latents_hbm.1, f32[1024,256]{1,0:T(8,128)} %cotangent_hbm.1), custom_call_target="tpu_custom_call" | custom-call | tf_op jit(solution)/shard_map/route/pallas_call | solution.py:246
  7.6 7.3 %all-to-all-start = ((f32[32,136,128]{2,1,0:T(8,128)}), f32[32,136,128]{2,1,0:T(8,128)S(1)}, u32[]{:S(2)}, u32[]{:S(2)}) async-start(f32[32,136,128]{2,1,0:T(8,128)} %get-tuple-element.61), calls=%async_computation | async-start | bytes 4456448 | tf_op jit(solution)/shard_map/all_to_all | solution.py:543
  16.8 8.4 %forward.1 = (bf16[1024,1024]{1,0:T(8,128)(2,1)}, bf16[768,1024]{1,0:T(8,128)(2,1)}, f32[1024,1024]{1,0:T(8,128)}, f32[1024,256]{1,0:T(8,128)}, bf16[1024,512]{1,0:T(8,128)(2,1)}) custom-call(bf16[1024,768]{1,0:T(8,128)(2,1)} %codebook_ref.1, bf16[768,1024]{1,0:T(8,128)(2,1)} %weight_in_ref.1, f32[1,1024]{1,0:T(1,128)} %bitcast.46, ...), custom_call_target="tpu_custom_call" | custom-call | flops 2147483648 | bytes 14680064 | tf_op jit(solution)/shard_map/forward/pallas_call | solution.py:62
  25.2 41.4 %all-to-all-done.incoming_hbm = f32[32,136,128]{2,1,0:T(8,128)S(1)} async-done(((f32[32,136,128]{2,1,0:T(8,128)}), f32[32,136,128]{2,1,0:T(8,128)S(1)}, u32[]{:S(2)}, u32[]{:S(2)}) %all-to-all-start) | async-done | bytes 2228256 | tf_op jit(solution)/shard_map/all_to_all | solution.py:543
  66.6 6.0 %pick_rows.1 = (f32[32,64,256]{2,1,0:T(8,128)}, f32[8,2048]{1,0:T(8,128)S(1)}) custom-call(f32[32,136,128]{2,1,0:T(8,128)S(1)} %all-to-all-done.incoming_hbm, bf16[1024,512]{1,0:T(8,128)(2,1)} %get-tuple-element.63.parts_hbm), custom_call_target="tpu_custom_call" | custom-call | flops 2147483648 | bytes 4194304 | tf_op jit(solution)/shard_map/pick_rows/pallas_call | solution.py:143
  72.7 4.0 %all-to-all-start.1 = ((f32[32,64,256]{2,1,0:T(8,128)}), f32[32,64,256]{2,1,0:T(8,128)S(1)}, u32[]{:S(2)}, u32[]{:S(2)}) async-start(f32[32,64,256]{2,1,0:T(8,128)} %get-tuple-element.69), calls=%async_computation.1 | async-start | bytes 4194304 | tf_op jit(solution)/shard_map/all_to_all | solution.py:549
  76.9 60.7 %conditional.1 = (f32[264,128]{1,0:T(8,128)S(1)}) conditional(s32[]{:T(128)} %convert_element_type.10, () %tuple.20, (f32[32,136,128]{2,1,0:T(8,128)}, f32[8,2048]{1,0:T(8,128)S(1)}, bf16[1024,1024]{1,0:T(8,128)(2,1)}, f32[1024,1024]{1,0:T(8,128)}, f32[1024,256]{1,0:T(8,128)}, /*index=5*/bf16[768,1024]{1,0:T(8,128)(2,1)}, ...), branch_computations={%region_0.0_spmd, %region_1.0_spmd} | conditional | flops 4832885760 | bytes 52867792 | solution.py:561
  77.1 12.6 %backward.1 = (f32[4,264,128]{2,1,0:T(8,128)}, f32[4,264,128]{2,1,0:T(8,128)}, f32[4,264,128]{2,1,0:T(8,128)}, f32[4,264,128]{2,1,0:T(8,128)}, f32[4,264,128]{2,...) custom-call(f32[32,136,128]{2,1,0:T(8,128)} %get-tuple-element.6.incoming_hbm, ...), custom_call_target="tpu_custom_call" | custom-call | flops 4831838208 | bytes 16777216 | tf_op jit(solution)/shard_map/cond/branch_1_fun/backward/pallas_call | solution.py:391
  93.0 1.8 %collective-permute-start.1 = (f32[2,264,128]{2,1,0:T(8,128)S(1)}, f32[2,264,128]{2,1,0:T(8,128)S(1)}, u32[]{:S(2)}, u32[]{:S(2)}) collective-permute-start(f32[2,264,128]{2,1,0:T(8,128)S(1)} %slice_add_fusion.6), channel_id=1, source_target_pairs={{0,2},{2,0},{1,3},{3,1},{4,6},{6,4},{5,7},{7,5},{8,10},{10,8},{9,1... | collective-permute-start | bytes 811016 | tf_op jit(solution)/shard_map/cond/branch_1_fun/ppermute | solution.py:495
  95.8 1.5 collective-permute-start.4
  99.4 9.3 %collective-permute-done.1 = f32[2,264,128]{2,1,0:T(8,128)S(1)} collective-permute-done((f32[2,264,128]{2,1,0:T(8,128)S(1)}, f32[2,264,128]{2,1,0:T(8,128)S(1)}, u32[]{:S(2)}, u32[]{:S(2)}) %collective-permute-start.1) | collective-permute-done | bytes 270368 | tf_op jit(solution)/shard_map/cond/branch_1_fun/ppermute | solution.py:495
  110.4 4.0 %collective-permute-done.8 = f32[2,264,128]{2,1,0:T(8,128)S(1)} collective-permute-done((f32[2,264,128]{2,1,0:T(8,128)S(1)}, f32[2,264,128]{2,1,0:T(8,128)S(1)}, u32[]{:S(2)}, u32[]{:S(2)}) %collective-permute-start.8) | collective-permute-done | bytes 270368 | tf_op jit(solution)/shard_map/cond/branch_1_fun/ppermute | solution.py:495
  114.8 2.1 %collective-permute-done.12 = f32[2,264,128]{2,1,0:T(8,128)S(1)} collective-permute-done((f32[2,264,128]{2,1,0:T(8,128)S(1)}, f32[2,264,128]{2,1,0:T(8,128)S(1)}, u32[]{:S(2)}, u32[]{:S(2)}) %collective-permute-start.12) | collective-permute-done | bytes 270368 | tf_op jit(solution)/shard_map/cond/branch_1_fun/ppermute | solution.py:495
  117.0 3.0 %collective-permute-start.6 = (f32[264,128]{1,0:T(8,128)S(1)}, f32[264,128]{1,0:T(8,128)S(1)}, u32[]{:S(2)}, u32[]{:S(2)}) collective-permute-start(f32[264,128]{1,0:T(8,128)S(1)} %fusion.6), channel_id=1, source_target_pairs={{0,24},{8,0},{16,8},{24,16},{1,25},{9,1},{17,9},{25,17},{2,26},{10... | collective-permute-start | bytes 405512 | tf_op jit(solution)/shard_map/cond/branch_1_fun/ppermute | solution.py:490
  120.0 4.1 %collective-permute-done.9 = f32[264,128]{1,0:T(8,128)S(1)} collective-permute-done((f32[264,128]{1,0:T(8,128)S(1)}, f32[264,128]{1,0:T(8,128)S(1)}, u32[]{:S(2)}, u32[]{:S(2)}) %collective-permute-start.9) | collective-permute-done | bytes 135200 | tf_op jit(solution)/shard_map/cond/branch_1_fun/ppermute | solution.py:495
  124.1 2.2 %collective-permute-start.10 = (f32[264,128]{1,0:T(8,128)S(1)}, f32[264,128]{1,0:T(8,128)S(1)}, u32[]{:S(2)}, u32[]{:S(2)}) collective-permute-start(f32[264,128]{1,0:T(8,128)S(1)} %fusion.5), channel_id=1, source_target_pairs={{0,16},{8,24},{16,0},{24,8},{1,17},{9,25},{17,1},{25,9},{2,18},{10... | collective-permute-start | bytes 405512 | tf_op jit(solution)/shard_map/cond/branch_1_fun/ppermute | solution.py:490
  126.3 1.7 collective-permute-start.14
  128.0 9.4 %collective-permute-done.10 = f32[264,128]{1,0:T(8,128)S(1)} collective-permute-done((f32[264,128]{1,0:T(8,128)S(1)}, f32[264,128]{1,0:T(8,128)S(1)}, u32[]{:S(2)}, u32[]{:S(2)}) %collective-permute-start.10) | collective-permute-done | bytes 135200 | tf_op jit(solution)/shard_map/cond/branch_1_fun/ppermute | solution.py:490
  139.6 2.0 %collective-permute-start.16 = (f32[264,128]{1,0:T(8,128)S(1)}, f32[264,128]{1,0:T(8,128)S(1)}, u32[]{:S(2)}, u32[]{:S(2)}) collective-permute-start(f32[264,128]{1,0:T(8,128)S(1)} %get-tuple-element.81.refs_0_), channel_id=1, source_target_pairs={{0,4},{4,0},{1,5},{5,1},{2,6},{6,2},{3,7},{7,3},{8,12},{12,8},{9,1... | collective-permute-start | bytes 405512 | tf_op jit(solution)/shard_map/ppermute | solution.py:495
  141.9 3.9 %collective-permute-start.15 = (f32[264,128]{1,0:T(8,128)S(1)}, f32[264,128]{1,0:T(8,128)S(1)}, u32[]{:S(2)}, u32[]{:S(2)}) collective-permute-start(f32[264,128]{1,0:T(8,128)S(1)} %get-tuple-element.81.refs_0_), channel_id=1, source_target_pairs={{0,24},{8,0},{16,8},{24,16},{1,25},{9,1},{17,9},{25,17},{2,26},{10... | collective-permute-start | bytes 405512 | tf_op jit(solution)/shard_map/ppermute | solution.py:490
  145.8 2.4 %fusion.11 = f32[1024,512]{1,0:T(8,128)S(1)} fusion(s32[1024]{0:T(1024)S(1)} %bitcast.47, bf16[2048,256]{1,0:T(8,128)(2,1)S(1)} %get-tuple-element.80, bf16[2048,256]{1,0:T(8,128)(2,1)S(1)} %get-tuple-element.79), kind=kOutput, calls=%fused_computation.28 | convolution fusion | flops 2153775104 | bytes 4198400 | tf_op jit(solution)/shard_map/dot_general | solution.py:34
  149.8 2.0 %collective-permute-start.24 = (f32[264,128]{1,0:T(8,128)S(1)}, f32[264,128]{1,0:T(8,128)S(1)}, u32[]{:S(2)}, u32[]{:S(2)}) collective-permute-start(f32[264,128]{1,0:T(8,128)S(1)} %collective-permute-done.23.refs_8_), channel_id=1, source_target_pairs={{0,4},{4,0},{1,5},{5,1},{2,6},{6,2},{3,7},{7,3},{8,12},{12,8},{9,1... | collective-permute-start | bytes 405512 | tf_op jit(solution)/shard_map/ppermute | solution.py:495
  153.7 2.1 %collective-permute-start.20 = (f32[264,128]{1,0:T(8,128)S(1)}, f32[264,128]{1,0:T(8,128)S(1)}, u32[]{:S(2)}, u32[]{:S(2)}) collective-permute-start(f32[264,128]{1,0:T(8,128)S(1)} %collective-permute-done.19.refs_4_), channel_id=1, source_target_pairs={{0,2},{2,0},{1,3},{3,1},{4,6},{6,4},{5,7},{7,5},{8,10},{10,8},{9,1... | collective-permute-start | bytes 405512 | tf_op jit(solution)/shard_map/ppermute | solution.py:495
  157.2 1.5 collective-permute-done.21.refs_6_
  159.2 1.7 collective-permute-start.28
  162.2 1.7 collective-permute-start.26
  164.7 2.3 %collective-permute-done.27.refs_13_ = f32[264,128]{1,0:T(8,128)S(1)} collective-permute-done((f32[264,128]{1,0:T(8,128)S(1)}, f32[264,128]{1,0:T(8,128)S(1)}, u32[]{:S(2)}, u32[]{:S(2)}) %collective-permute-start.27) | collective-permute-done | bytes 135200 | tf_op jit(solution)/shard_map/ppermute | solution.py:495
  167.6 1.5 collective-permute-done.26.refs_11_
  169.1 1.6 collective-permute-start.29
  171.2 2.2 %collective-permute-done.22.refs_7_ = f32[264,128]{1,0:T(8,128)S(1)} collective-permute-done((f32[264,128]{1,0:T(8,128)S(1)}, f32[264,128]{1,0:T(8,128)S(1)}, u32[]{:S(2)}, u32[]{:S(2)}) %collective-permute-start.22) | collective-permute-done | bytes 135200 | tf_op jit(solution)/shard_map/ppermute | solution.py:495
  173.9 2.0 %collective-permute-done.29.refs_15_ = f32[264,128]{1,0:T(8,128)S(1)} collective-permute-done((f32[264,128]{1,0:T(8,128)S(1)}, f32[264,128]{1,0:T(8,128)S(1)}, u32[]{:S(2)}, u32[]{:S(2)}) %collective-permute-start.29) | collective-permute-done | bytes 135200 | tf_op jit(solution)/shard_map/ppermute | solution.py:495
  177.3 2.9 %assemble.1 = (f32[768,1024]{1,0:T(8,128)}, f32[1024,256]{1,0:T(8,128)}, f32[8,128]{1,0:T(8,128)}, f32[8,128]{1,0:T(8,128)S(1)}) custom-call(f32[264,128]{1,0:T(8,128)S(1)} %get-tuple-element.81.refs_0_, f32[264,128]{1,0:T(8,128)S(1)} %collective-permute-done.16.refs_1_, f32[264,128]{1,0:T(8,128)S(1)} %collective-permute-done.17.refs_2_, ...), custom_call_target="tpu_custom_call" | custom-call | tf_op jit(solution)/shard_map/assemble/pallas_call | solution.py:469
  (110 shorter events, 23.2 us)
Async XLA Ops:
  7.6 59.0 %all-to-all-start = ((f32[32,136,128]{2,1,0:T(8,128)}), f32[32,136,128]{2,1,0:T(8,128)S(1)}, u32[]{:S(2)}, u32[]{:S(2)}) async-start(f32[32,136,128]{2,1,0:T(8,128)} %get-tuple-element.61), calls=%async_computation | async-start | bytes 4456448 | tf_op jit(solution)/shard_map/all_to_all | solution.py:543
  72.7 65.0 %all-to-all-start.1 = ((f32[32,64,256]{2,1,0:T(8,128)}), f32[32,64,256]{2,1,0:T(8,128)S(1)}, u32[]{:S(2)}, u32[]{:S(2)}) async-start(f32[32,64,256]{2,1,0:T(8,128)} %get-tuple-element.69), calls=%async_computation.1 | async-start | bytes 4194304 | tf_op jit(solution)/shard_map/all_to_all | solution.py:549
  90.3 7.0 %collective-permute-start.7 = (f32[4,264,128]{2,1,0:T(8,128)}, f32[4,264,128]{2,1,0:T(8,128)S(1)}, u32[]{:S(2)}, u32[]{:S(2)}) collective-permute-start(f32[4,264,128]{2,1,0:T(8,128)} %get-tuple-element.29), channel_id=1, source_target_pairs={{0,1},{1,0},{2,3},{3,2},{4,5},{5,4},{6,7},{7,6},{8,9},{9,8},{10,11... | collective-permute-start | bytes 1622024 | tf_op jit(solution)/shard_map/cond/branch_1_fun/ppermute | solution.py:495
  90.6 8.4 %collective-permute-start.11 = (f32[4,264,128]{2,1,0:T(8,128)}, f32[4,264,128]{2,1,0:T(8,128)S(1)}, u32[]{:S(2)}, u32[]{:S(2)}) collective-permute-start(f32[4,264,128]{2,1,0:T(8,128)} %get-tuple-element.31), channel_id=1, source_target_pairs={{0,1},{1,0},{2,3},{3,2},{4,5},{5,4},{6,7},{7,6},{8,9},{9,8},{10,11... | collective-permute-start | bytes 1622024 | tf_op jit(solution)/shard_map/cond/branch_1_fun/ppermute | solution.py:495
  93.0 15.7 %collective-permute-start.1 = (f32[2,264,128]{2,1,0:T(8,128)S(1)}, f32[2,264,128]{2,1,0:T(8,128)S(1)}, u32[]{:S(2)}, u32[]{:S(2)}) collective-permute-start(f32[2,264,128]{2,1,0:T(8,128)S(1)} %slice_add_fusion.6), channel_id=1, source_target_pairs={{0,2},{2,0},{1,3},{3,1},{4,6},{6,4},{5,7},{7,5},{8,10},{10,8},{9,1... | collective-permute-start | bytes 811016 | tf_op jit(solution)/shard_map/cond/branch_1_fun/ppermute | solution.py:495
  95.8 13.7 %collective-permute-start.4 = (f32[2,264,128]{2,1,0:T(8,128)S(1)}, f32[2,264,128]{2,1,0:T(8,128)S(1)}, u32[]{:S(2)}, u32[]{:S(2)}) collective-permute-start(f32[2,264,128]{2,1,0:T(8,128)S(1)} %slice_add_fusion.4), channel_id=1, source_target_pairs={{0,4},{4,0},{1,5},{5,1},{2,6},{6,2},{3,7},{7,3},{8,12},{12,8},{9,1... | collective-permute-start | bytes 811016 | tf_op jit(solution)/shard_map/cond/branch_1_fun/ppermute | solution.py:495
  98.4 16.1 %collective-permute-start.8 = (f32[2,264,128]{2,1,0:T(8,128)S(1)}, f32[2,264,128]{2,1,0:T(8,128)S(1)}, u32[]{:S(2)}, u32[]{:S(2)}) collective-permute-start(f32[2,264,128]{2,1,0:T(8,128)S(1)} %slice_add_fusion.2), channel_id=1, source_target_pairs={{0,2},{2,0},{1,3},{3,1},{4,6},{6,4},{5,7},{7,5},{8,10},{10,8},{9,1... | collective-permute-start | bytes 811016 | tf_op jit(solution)/shard_map/cond/branch_1_fun/ppermute | solution.py:495
  99.1 17.8 %collective-permute-start.12 = (f32[2,264,128]{2,1,0:T(8,128)S(1)}, f32[2,264,128]{2,1,0:T(8,128)S(1)}, u32[]{:S(2)}, u32[]{:S(2)}) collective-permute-start(f32[2,264,128]{2,1,0:T(8,128)S(1)} %slice_add_fusion), channel_id=1, source_target_pairs={{0,4},{4,0},{1,5},{5,1},{2,6},{6,2},{3,7},{7,3},{8,12},{12,8},{9,1... | collective-permute-start | bytes 811016 | tf_op jit(solution)/shard_map/cond/branch_1_fun/ppermute | solution.py:495
  108.7 19.3 %collective-permute-start.2 = (f32[264,128]{1,0:T(8,128)S(1)}, f32[264,128]{1,0:T(8,128)S(1)}, u32[]{:S(2)}, u32[]{:S(2)}) collective-permute-start(f32[264,128]{1,0:T(8,128)S(1)} %slice_bitcast_fusion.6), channel_id=1, source_target_pairs={{0,4},{4,0},{1,5},{5,1},{2,6},{6,2},{3,7},{7,3},{8,12},{12,8},{9,1... | collective-permute-start | bytes 405512 | tf_op jit(solution)/shard_map/cond/branch_1_fun/ppermute | solution.py:495
  109.6 7.4 %collective-permute-start.5 = (f32[264,128]{1,0:T(8,128)S(1)}, f32[264,128]{1,0:T(8,128)S(1)}, u32[]{:S(2)}, u32[]{:S(2)}) collective-permute-start(f32[264,128]{1,0:T(8,128)S(1)} %slice_bitcast_fusion.4), channel_id=1, source_target_pairs={{0,2},{2,0},{1,3},{3,1},{4,6},{6,4},{5,7},{7,5},{8,10},{10,8},{9,1... | collective-permute-start | bytes 405512 | tf_op jit(solution)/shard_map/cond/branch_1_fun/ppermute | solution.py:495
  114.5 9.6 %collective-permute-start.9 = (f32[264,128]{1,0:T(8,128)S(1)}, f32[264,128]{1,0:T(8,128)S(1)}, u32[]{:S(2)}, u32[]{:S(2)}) collective-permute-start(f32[264,128]{1,0:T(8,128)S(1)} %slice_bitcast_fusion.2), channel_id=1, source_target_pairs={{0,4},{4,0},{1,5},{5,1},{2,6},{6,2},{3,7},{7,3},{8,12},{12,8},{9,1... | collective-permute-start | bytes 405512 | tf_op jit(solution)/shard_map/cond/branch_1_fun/ppermute | solution.py:495
  116.9 9.4 %collective-permute-start.13 = (f32[264,128]{1,0:T(8,128)S(1)}, f32[264,128]{1,0:T(8,128)S(1)}, u32[]{:S(2)}, u32[]{:S(2)}) collective-permute-start(f32[264,128]{1,0:T(8,128)S(1)} %slice_bitcast_fusion), channel_id=1, source_target_pairs={{0,2},{2,0},{1,3},{3,1},{4,6},{6,4},{5,7},{7,5},{8,10},{10,8},{9,1... | collective-permute-start | bytes 405512 | tf_op jit(solution)/shard_map/cond/branch_1_fun/ppermute | solution.py:495
  117.0 11.0 %collective-permute-start.6 = (f32[264,128]{1,0:T(8,128)S(1)}, f32[264,128]{1,0:T(8,128)S(1)}, u32[]{:S(2)}, u32[]{:S(2)}) collective-permute-start(f32[264,128]{1,0:T(8,128)S(1)} %fusion.6), channel_id=1, source_target_pairs={{0,24},{8,0},{16,8},{24,16},{1,25},{9,1},{17,9},{25,17},{2,26},{10... | collective-permute-start | bytes 405512 | tf_op jit(solution)/shard_map/cond/branch_1_fun/ppermute | solution.py:490
  124.1 13.3 %collective-permute-start.10 = (f32[264,128]{1,0:T(8,128)S(1)}, f32[264,128]{1,0:T(8,128)S(1)}, u32[]{:S(2)}, u32[]{:S(2)}) collective-permute-start(f32[264,128]{1,0:T(8,128)S(1)} %fusion.5), channel_id=1, source_target_pairs={{0,16},{8,24},{16,0},{24,8},{1,17},{9,25},{17,1},{25,9},{2,18},{10... | collective-permute-start | bytes 405512 | tf_op jit(solution)/shard_map/cond/branch_1_fun/ppermute | solution.py:490
  126.3 11.1 %collective-permute-start.14 = (f32[264,128]{1,0:T(8,128)S(1)}, f32[264,128]{1,0:T(8,128)S(1)}, u32[]{:S(2)}, u32[]{:S(2)}) collective-permute-start(f32[264,128]{1,0:T(8,128)S(1)} %fusion.4), channel_id=1, source_target_pairs={{0,8},{8,16},{16,24},{24,0},{1,9},{9,17},{17,25},{25,1},{2,10},{10... | collective-permute-start | bytes 405512 | tf_op jit(solution)/shard_map/cond/branch_1_fun/ppermute | solution.py:490
  137.8 11.0 %collective-permute-start.23 = (f32[264,128]{1,0:T(8,128)S(1)}, f32[264,128]{1,0:T(8,128)S(1)}, u32[]{:S(2)}, u32[]{:S(2)}) collective-permute-start(f32[264,128]{1,0:T(8,128)S(1)} %get-tuple-element.81.refs_0_), channel_id=1, source_target_pairs={{0,16},{8,24},{16,0},{24,8},{1,17},{9,25},{17,1},{25,9},{2,18},{10... | collective-permute-start | bytes 405512 | tf_op jit(solution)/shard_map/ppermute | solution.py:490
  138.5 10.3 %collective-permute-start.19 = (f32[264,128]{1,0:T(8,128)S(1)}, f32[264,128]{1,0:T(8,128)S(1)}, u32[]{:S(2)}, u32[]{:S(2)}) collective-permute-start(f32[264,128]{1,0:T(8,128)S(1)} %get-tuple-element.81.refs_0_), channel_id=1, source_target_pairs={{0,8},{8,16},{16,24},{24,0},{1,9},{9,17},{17,25},{25,1},{2,10},{10... | collective-permute-start | bytes 405512 | tf_op jit(solution)/shard_map/ppermute | solution.py:490
  138.5 11.4 %collective-permute-start.17 = (f32[264,128]{1,0:T(8,128)S(1)}, f32[264,128]{1,0:T(8,128)S(1)}, u32[]{:S(2)}, u32[]{:S(2)}) collective-permute-start(f32[264,128]{1,0:T(8,128)S(1)} %get-tuple-element.81.refs_0_), channel_id=1, source_target_pairs={{0,2},{2,0},{1,3},{3,1},{4,6},{6,4},{5,7},{7,5},{8,10},{10,8},{9,1... | collective-permute-start | bytes 405512 | tf_op jit(solution)/shard_map/ppermute | solution.py:495
  139.6 12.3 %collective-permute-start.16 = (f32[264,128]{1,0:T(8,128)S(1)}, f32[264,128]{1,0:T(8,128)S(1)}, u32[]{:S(2)}, u32[]{:S(2)}) collective-permute-start(f32[264,128]{1,0:T(8,128)S(1)} %get-tuple-element.81.refs_0_), channel_id=1, source_target_pairs={{0,4},{4,0},{1,5},{5,1},{2,6},{6,2},{3,7},{7,3},{8,12},{12,8},{9,1... | collective-permute-start | bytes 405512 | tf_op jit(solution)/shard_map/ppermute | solution.py:495
  141.9 9.9 %collective-permute-start.15 = (f32[264,128]{1,0:T(8,128)S(1)}, f32[264,128]{1,0:T(8,128)S(1)}, u32[]{:S(2)}, u32[]{:S(2)}) collective-permute-start(f32[264,128]{1,0:T(8,128)S(1)} %get-tuple-element.81.refs_0_), channel_id=1, source_target_pairs={{0,24},{8,0},{16,8},{24,16},{1,25},{9,1},{17,9},{25,17},{2,26},{10... | collective-permute-start | bytes 405512 | tf_op jit(solution)/shard_map/ppermute | solution.py:490
  148.7 7.1 %collective-permute-start.25 = (f32[264,128]{1,0:T(8,128)S(1)}, f32[264,128]{1,0:T(8,128)S(1)}, u32[]{:S(2)}, u32[]{:S(2)}) collective-permute-start(f32[264,128]{1,0:T(8,128)S(1)} %collective-permute-done.23.refs_8_), channel_id=1, source_target_pairs={{0,2},{2,0},{1,3},{3,1},{4,6},{6,4},{5,7},{7,5},{8,10},{10,8},{9,1... | collective-permute-start | bytes 405512 | tf_op jit(solution)/shard_map/ppermute | solution.py:495
  149.8 6.4 %collective-permute-start.24 = (f32[264,128]{1,0:T(8,128)S(1)}, f32[264,128]{1,0:T(8,128)S(1)}, u32[]{:S(2)}, u32[]{:S(2)}) collective-permute-start(f32[264,128]{1,0:T(8,128)S(1)} %collective-permute-done.23.refs_8_), channel_id=1, source_target_pairs={{0,4},{4,0},{1,5},{5,1},{2,6},{6,2},{3,7},{7,3},{8,12},{12,8},{9,1... | collective-permute-start | bytes 405512 | tf_op jit(solution)/shard_map/ppermute | solution.py:495
  151.9 6.9 %collective-permute-start.21 = (f32[264,128]{1,0:T(8,128)S(1)}, f32[264,128]{1,0:T(8,128)S(1)}, u32[]{:S(2)}, u32[]{:S(2)}) collective-permute-start(f32[264,128]{1,0:T(8,128)S(1)} %collective-permute-done.19.refs_4_), channel_id=1, source_target_pairs={{0,4},{4,0},{1,5},{5,1},{2,6},{6,2},{3,7},{7,3},{8,12},{12,8},{9,1... | collective-permute-start | bytes 405512 | tf_op jit(solution)/shard_map/ppermute | solution.py:495
  153.7 5.5 %collective-permute-start.20 = (f32[264,128]{1,0:T(8,128)S(1)}, f32[264,128]{1,0:T(8,128)S(1)}, u32[]{:S(2)}, u32[]{:S(2)}) collective-permute-start(f32[264,128]{1,0:T(8,128)S(1)} %collective-permute-done.19.refs_4_), channel_id=1, source_target_pairs={{0,2},{2,0},{1,3},{3,1},{4,6},{6,4},{5,7},{7,5},{8,10},{10,8},{9,1... | collective-permute-start | bytes 405512 | tf_op jit(solution)/shard_map/ppermute | solution.py:495
  156.3 5.9 %collective-permute-start.18 = (f32[264,128]{1,0:T(8,128)S(1)}, f32[264,128]{1,0:T(8,128)S(1)}, u32[]{:S(2)}, u32[]{:S(2)}) collective-permute-start(f32[264,128]{1,0:T(8,128)S(1)} %collective-permute-done.16.refs_1_), channel_id=1, source_target_pairs={{0,2},{2,0},{1,3},{3,1},{4,6},{6,4},{5,7},{7,5},{8,10},{10,8},{9,1... | collective-permute-start | bytes 405512 | tf_op jit(solution)/shard_map/ppermute | solution.py:495
  159.2 5.5 %collective-permute-start.28 = (f32[264,128]{1,0:T(8,128)S(1)}, f32[264,128]{1,0:T(8,128)S(1)}, u32[]{:S(2)}, u32[]{:S(2)}) collective-permute-start(f32[264,128]{1,0:T(8,128)S(1)} %collective-permute-done.15.refs_12_), channel_id=1, source_target_pairs={{0,4},{4,0},{1,5},{5,1},{2,6},{6,2},{3,7},{7,3},{8,12},{12,8},{9,1... | collective-permute-start | bytes 405512 | tf_op jit(solution)/shard_map/ppermute | solution.py:495
  160.9 6.2 %collective-permute-start.27 = (f32[264,128]{1,0:T(8,128)S(1)}, f32[264,128]{1,0:T(8,128)S(1)}, u32[]{:S(2)}, u32[]{:S(2)}) collective-permute-start(f32[264,128]{1,0:T(8,128)S(1)} %collective-permute-done.15.refs_12_), channel_id=1, source_target_pairs={{0,2},{2,0},{1,3},{3,1},{4,6},{6,4},{5,7},{7,5},{8,10},{10,8},{9,1... | collective-permute-start | bytes 405512 | tf_op jit(solution)/shard_map/ppermute | solution.py:495
  162.2 6.8 %collective-permute-start.26 = (f32[264,128]{1,0:T(8,128)S(1)}, f32[264,128]{1,0:T(8,128)S(1)}, u32[]{:S(2)}, u32[]{:S(2)}) collective-permute-start(f32[264,128]{1,0:T(8,128)S(1)} %collective-permute-done.24.refs_9_), channel_id=1, source_target_pairs={{0,2},{2,0},{1,3},{3,1},{4,6},{6,4},{5,7},{7,5},{8,10},{10,8},{9,1... | collective-permute-start | bytes 405512 | tf_op jit(solution)/shard_map/ppermute | solution.py:495
  164.7 5.9 %collective-permute-start.36 = (f32[264,128]{1,0:T(8,128)S(1)}, f32[264,128]{1,0:T(8,128)S(1)}, u32[]{:S(2)}, u32[]{:S(2)}) collective-permute-start(f32[264,128]{1,0:T(8,128)S(1)} %collective-permute-done.21.refs_6_), channel_id=1, source_target_pairs={{0,1},{1,0},{2,3},{3,2},{4,5},{5,4},{6,7},{7,6},{8,9},{9,8},{10,11... | collective-permute-start | bytes 405512 | tf_op jit(solution)/shard_map/ppermute | solution.py:495
  167.1 6.4 %collective-permute-start.22 = (f32[264,128]{1,0:T(8,128)S(1)}, f32[264,128]{1,0:T(8,128)S(1)}, u32[]{:S(2)}, u32[]{:S(2)}) collective-permute-start(f32[264,128]{1,0:T(8,128)S(1)} %collective-permute-done.20.refs_5_), channel_id=1, source_target_pairs={{0,4},{4,0},{1,5},{5,1},{2,6},{6,2},{3,7},{7,3},{8,12},{12,8},{9,1... | collective-permute-start | bytes 405512 | tf_op jit(solution)/shard_map/ppermute | solution.py:495
  167.2 6.3 %collective-permute-start.33 = (f32[264,128]{1,0:T(8,128)S(1)}, f32[264,128]{1,0:T(8,128)S(1)}, u32[]{:S(2)}, u32[]{:S(2)}) collective-permute-start(f32[264,128]{1,0:T(8,128)S(1)} %collective-permute-done.18.refs_3_), channel_id=1, source_target_pairs={{0,1},{1,0},{2,3},{3,2},{4,5},{5,4},{6,7},{7,6},{8,9},{9,8},{10,11... | collective-permute-start | bytes 405512 | tf_op jit(solution)/shard_map/ppermute | solution.py:495
  169.1 6.9 %collective-permute-start.29 = (f32[264,128]{1,0:T(8,128)S(1)}, f32[264,128]{1,0:T(8,128)S(1)}, u32[]{:S(2)}, u32[]{:S(2)}) collective-permute-start(f32[264,128]{1,0:T(8,128)S(1)} %collective-permute-done.27.refs_13_), channel_id=1, source_target_pairs={{0,4},{4,0},{1,5},{5,1},{2,6},{6,2},{3,7},{7,3},{8,12},{12,8},{9,1... | collective-permute-start | bytes 405512 | tf_op jit(solution)/shard_map/ppermute | solution.py:495
  (25 other events, 159.0 us)

commit v8 on v5

--- a/solution.py
+++ b/solution.py
@@ -518,9 +518,10 @@
 def spread_chunks(sizes, total):
     outer, inner, chip, _ = sizes
     near = []
-    for k in range(outer):
+    line = [along(sizes, total, k) if k else total for k in range(outer)]
+    line[:2] = lax.optimization_barrier(tuple(line[:2]))
+    for k, x in enumerate(line):
         slow, fast = ("inner", "chip") if k % 2 else ("chip", "inner")
-        x = along(sizes, total, k) if k else total
         row = [across(sizes, fast, x, j) if j else x for j in range(sizes[AXES.index(fast)])]
         for j in range(sizes[AXES.index(slow)]):
             near += [across(sizes, slow, x, j) if j else x for x in row]

time: 180 us -> 184 us (1.022)
  waiting for transfers between devices: 87.8 us -> 90.9 us
    ppermute x6, waiting for transfers between devices: 10.1 us -> 14.2 us  [along(): lax.ppermute(x, 'outer', [(o, (o + k) % outer) for o in range(outer)])]
  transfers between devices with their start and end apart: 48 -> 48, of which waited for: 21 -> 22; matrix products, arithmetic and copies ran while one was open for 5% -> 5% of each run, Pallas kernels for 12% -> 11%
where the time goes in v8:
time: 184 us
  waiting for transfers between devices  90.9 us (49%)
  starting transfers between devices  44.8 us (24%)
  Pallas kernels  36.9 us (20%)
  other arithmetic  4.93 us (3%)
  matrix products  2.38 us (1%)
  local copies, waits for them, and re-layouts  2.06 us (1%)
    all_to_all x1, waiting for transfers between devices, per_device(): lax.all_to_all(outgoing, AXES, split_axis=0, concat_axis=0, tiled=True)  43.3 us
    ppermute x40, waiting for transfers between devices, across(): return lax.ppermute(x, axis, [(p, p ^ j) for p in range(size)])  33.4 us
    ppermute x40, starting transfers between devices, across(): return lax.ppermute(x, axis, [(p, p ^ j) for p in range(size)])  23 us
    ppermute x6, waiting for transfers between devices, along(): lax.ppermute(x, 'outer', [(o, (o + k) % outer) for o in range(outer)])  14.2 us
    pallas_call x1, Pallas kernels, backward(): pl.pallas_call(functools.partial(backward_kernel, sizes, capacity), in_sp...  12.6 us
    ppermute x6, starting transfers between devices, along(): lax.ppermute(x, 'outer', [(o, (o + k) % outer) for o in range(outer)])  10.5 us
    pallas_call x1, Pallas kernels, forward(): pl.pallas_call(forward_kernel, grid=(rows // tile,), in_specs=[pl.BlockSp...  8.43 us
    all_to_all x1, starting transfers between devices, per_device(): lax.all_to_all(outgoing, AXES, split_axis=0, concat_axis=0, tiled=True)  7.3 us
  transfers between devices with their start and end apart: 48, of which 22 were waited for; matrix products, arithmetic and copies ran while one was open for 5% of the time, Pallas kernels for 11%

profile of v8, /device:TPU:0, one launch (start us, length us, event | category | flops | bytes accessed | tf_op | source)
XLA Modules:
  0.0 183.9 jit_solution(12594302473468118723)
XLA Ops:
  0.6 7.0 %route.1 = (f32[32,136,128]{2,1,0:T(8,128)}, s32[1,1024]{1,0:T(1,128)}) custom-call(s32[1,1024]{1,0:T(1,128)} %bitcast.44, s32[1,1024]{1,0:T(1,128)} %bitcast.45, f32[1024,256]{1,0:T(8,128)} %latents_hbm.1, f32[1024,256]{1,0:T(8,128)} %cotangent_hbm.1), custom_call_target="tpu_custom_call" | custom-call | tf_op jit(solution)/shard_map/route/pallas_call | solution.py:246
  7.6 7.3 %all-to-all-start = ((f32[32,136,128]{2,1,0:T(8,128)}), f32[32,136,128]{2,1,0:T(8,128)S(1)}, u32[]{:S(2)}, u32[]{:S(2)}) async-start(f32[32,136,128]{2,1,0:T(8,128)} %get-tuple-element.59), calls=%async_computation | async-start | bytes 4456448 | tf_op jit(solution)/shard_map/all_to_all | solution.py:543
  14.9 8.4 %forward.1 = (bf16[1024,1024]{1,0:T(8,128)(2,1)}, bf16[768,1024]{1,0:T(8,128)(2,1)}, f32[1024,1024]{1,0:T(8,128)}, f32[1024,256]{1,0:T(8,128)}, bf16[1024,512]{1,0:T(8,128)(2,1)}) custom-call(bf16[1024,768]{1,0:T(8,128)(2,1)} %codebook_ref.1, bf16[768,1024]{1,0:T(8,128)(2,1)} %weight_in_ref.1, f32[1,1024]{1,0:T(1,128)} %bitcast.46, ...), custom_call_target="tpu_custom_call" | custom-call | flops 2147483648 | bytes 14680064 | tf_op jit(solution)/shard_map/forward/pallas_call | solution.py:62
  23.4 43.3 %all-to-all-done.incoming_hbm = f32[32,136,128]{2,1,0:T(8,128)S(1)} async-done(((f32[32,136,128]{2,1,0:T(8,128)}), f32[32,136,128]{2,1,0:T(8,128)S(1)}, u32[]{:S(2)}, u32[]{:S(2)}) %all-to-all-start) | async-done | bytes 2228256 | tf_op jit(solution)/shard_map/all_to_all | solution.py:543
  66.6 6.0 %pick_rows.1 = (f32[32,64,256]{2,1,0:T(8,128)}, f32[8,2048]{1,0:T(8,128)S(1)}) custom-call(f32[32,136,128]{2,1,0:T(8,128)S(1)} %all-to-all-done.incoming_hbm, bf16[1024,512]{1,0:T(8,128)(2,1)} %get-tuple-element.61.parts_hbm), custom_call_target="tpu_custom_call" | custom-call | flops 2147483648 | bytes 4194304 | tf_op jit(solution)/shard_map/pick_rows/pallas_call | solution.py:143
  72.7 4.0 %all-to-all-start.1 = ((f32[32,64,256]{2,1,0:T(8,128)}), f32[32,64,256]{2,1,0:T(8,128)S(1)}, u32[]{:S(2)}, u32[]{:S(2)}) async-start(f32[32,64,256]{2,1,0:T(8,128)} %get-tuple-element.67), calls=%async_computation.1 | async-start | bytes 4194304 | tf_op jit(solution)/shard_map/all_to_all | solution.py:549
  78.8 58.9 %conditional.1 = (f32[264,128]{1,0:T(8,128)S(1)}) conditional(s32[]{:T(128)} %bitcast.8, () %tuple.18, (f32[32,136,128]{2,1,0:T(8,128)}, f32[8,2048]{1,0:T(8,128)S(1)}, bf16[1024,1024]{1,0:T(8,128)(2,1)}, f32[1024,1024]{1,0:T(8,128)}, f32[1024,256]{1,0:T(8,128)}, /*index=5*/bf16[768,1024]{1,0:T(8,128)(2,1)}, bf16[256,1024]{1,0:T(8,128)(2,1)S(1)}) %tuple.29), branch_computations={%region_0.0_spmd, %region_1.0_spmd} | conditional | flops 4832885760 | bytes 52867792 | solution.py:561
  79.0 12.6 %backward.1 = (f32[4,264,128]{2,1,0:T(8,128)}, f32[4,264,128]{2,1,0:T(8,128)}, f32[4,264,128]{2,1,0:T(8,128)}, f32[4,264,128]{2,1,0:T(8,128)}, f32[4,264,128]{2,...) custom-call(f32[32,136,128]{2,1,0:T(8,128)} %get-tuple-element.6.incoming_hbm, ...), custom_call_target="tpu_custom_call" | custom-call | flops 4831838208 | bytes 16777216 | tf_op jit(solution)/shard_map/cond/branch_1_fun/backward/pallas_call | solution.py:391
  94.8 1.8 collective-permute-start.1
  97.6 1.5 collective-permute-start.4
  101.2 9.2 %collective-permute-done.1 = f32[2,264,128]{2,1,0:T(8,128)S(1)} collective-permute-done((f32[2,264,128]{2,1,0:T(8,128)S(1)}, f32[2,264,128]{2,1,0:T(8,128)S(1)}, u32[]{:S(2)}, u32[]{:S(2)}) %collective-permute-start.1) | collective-permute-done | bytes 270368 | tf_op jit(solution)/shard_map/cond/branch_1_fun/ppermute | solution.py:495
  111.7 4.5 %collective-permute-done.8 = f32[2,264,128]{2,1,0:T(8,128)S(1)} collective-permute-done((f32[2,264,128]{2,1,0:T(8,128)S(1)}, f32[2,264,128]{2,1,0:T(8,128)S(1)}, u32[]{:S(2)}, u32[]{:S(2)}) %collective-permute-start.8) | collective-permute-done | bytes 270368 | tf_op jit(solution)/shard_map/cond/branch_1_fun/ppermute | solution.py:495
  116.4 1.5 collective-permute-done.12
  118.2 1.2 collective-permute-done.5
  119.4 1.9 %collective-permute-start.6 = (f32[264,128]{1,0:T(8,128)S(1)}, f32[264,128]{1,0:T(8,128)S(1)}, u32[]{:S(2)}, u32[]{:S(2)}) collective-permute-start(f32[264,128]{1,0:T(8,128)S(1)} %fusion.6), channel_id=1, source_target_pairs={{0,24},{8,0},{16,8},{24,16},{1,25},{9,1},{17,9},{25,17},{2,26},{10... | collective-permute-start | bytes 405512 | tf_op jit(solution)/shard_map/cond/branch_1_fun/ppermute | solution.py:490
  121.3 3.9 %collective-permute-done.9 = f32[264,128]{1,0:T(8,128)S(1)} collective-permute-done((f32[264,128]{1,0:T(8,128)S(1)}, f32[264,128]{1,0:T(8,128)S(1)}, u32[]{:S(2)}, u32[]{:S(2)}) %collective-permute-start.9) | collective-permute-done | bytes 135200 | tf_op jit(solution)/shard_map/cond/branch_1_fun/ppermute | solution.py:495
  125.3 2.9 %collective-permute-start.10 = (f32[264,128]{1,0:T(8,128)S(1)}, f32[264,128]{1,0:T(8,128)S(1)}, u32[]{:S(2)}, u32[]{:S(2)}) collective-permute-start(f32[264,128]{1,0:T(8,128)S(1)} %fusion.5), channel_id=1, source_target_pairs={{0,16},{8,24},{16,0},{24,8},{1,17},{9,25},{17,1},{25,9},{2,18},{10... | collective-permute-start | bytes 405512 | tf_op jit(solution)/shard_map/cond/branch_1_fun/ppermute | solution.py:490
  128.3 9.1 %collective-permute-done.10 = f32[264,128]{1,0:T(8,128)S(1)} collective-permute-done((f32[264,128]{1,0:T(8,128)S(1)}, f32[264,128]{1,0:T(8,128)S(1)}, u32[]{:S(2)}, u32[]{:S(2)}) %collective-permute-start.10) | collective-permute-done | bytes 135200 | tf_op jit(solution)/shard_map/cond/branch_1_fun/ppermute | solution.py:490
  137.7 1.7 collective-permute-start.23
  139.4 3.8 %collective-permute-start.15 = (f32[264,128]{1,0:T(8,128)S(1)}, f32[264,128]{1,0:T(8,128)S(1)}, u32[]{:S(2)}, u32[]{:S(2)}) collective-permute-start(f32[264,128]{1,0:T(8,128)S(1)} %get-tuple-element.81.refs_0_), channel_id=1, source_target_pairs={{0,24},{8,0},{16,8},{24,16},{1,25},{9,1},{17,9},{25,17},{2,26},{10... | collective-permute-start | bytes 405512 | tf_op jit(solution)/shard_map/ppermute | solution.py:490
  143.6 5.1 %collective-permute-done.23.refs_8_ = f32[264,128]{1,0:T(8,128)S(1)} collective-permute-done((f32[264,128]{1,0:T(8,128)S(1)}, f32[264,128]{1,0:T(8,128)S(1)}, u32[]{:S(2)}, u32[]{:S(2)}) %collective-permute-start.23) | collective-permute-done | bytes 135200 | tf_op jit(solution)/shard_map/ppermute | solution.py:490
  148.9 2.5 %collective-permute-start.24 = (f32[264,128]{1,0:T(8,128)S(1)}, f32[264,128]{1,0:T(8,128)S(1)}, u32[]{:S(2)}, u32[]{:S(2)}) collective-permute-start(f32[264,128]{1,0:T(8,128)S(1)} %collective-permute-done.23.refs_8_), channel_id=1, source_target_pairs={{0,4},{4,0},{1,5},{5,1},{2,6},{6,2},{3,7},{7,3},{8,12},{12,8},{9,1... | collective-permute-start | bytes 405512 | tf_op jit(solution)/shard_map/ppermute | solution.py:495
  151.4 2.4 %fusion.11 = f32[1024,512]{1,0:T(8,128)S(1)} fusion(s32[1024]{0:T(1024)S(1)} %bitcast.47, bf16[2048,256]{1,0:T(8,128)(2,1)S(1)} %get-tuple-element.80, bf16[2048,256]{1,0:T(8,128)(2,1)S(1)} %get-tuple-element.79), kind=kOutput, calls=%fused_computation.28 | convolution fusion | flops 2153775104 | bytes 4198400 | tf_op jit(solution)/shard_map/dot_general | solution.py:34
  155.4 1.7 collective-permute-start.21
  157.1 1.2 fusion.19
  163.7 2.2 %collective-permute-start.26 = (f32[264,128]{1,0:T(8,128)S(1)}, f32[264,128]{1,0:T(8,128)S(1)}, u32[]{:S(2)}, u32[]{:S(2)}) collective-permute-start(f32[264,128]{1,0:T(8,128)S(1)} %collective-permute-done.24.refs_9_), channel_id=1, source_target_pairs={{0,2},{2,0},{1,3},{3,1},{4,6},{6,4},{5,7},{7,5},{8,10},{10,8},{9,1... | collective-permute-start | bytes 405512 | tf_op jit(solution)/shard_map/ppermute | solution.py:495
  168.1 2.0 %collective-permute-done.26.refs_11_ = f32[264,128]{1,0:T(8,128)S(1)} collective-permute-done((f32[264,128]{1,0:T(8,128)S(1)}, f32[264,128]{1,0:T(8,128)S(1)}, u32[]{:S(2)}, u32[]{:S(2)}) %collective-permute-start.26) | collective-permute-done | bytes 135200 | tf_op jit(solution)/shard_map/ppermute | solution.py:495
  171.1 1.8 collective-permute-done.19.refs_3_
  172.9 1.9 %collective-permute-start.29 = (f32[264,128]{1,0:T(8,128)S(1)}, f32[264,128]{1,0:T(8,128)S(1)}, u32[]{:S(2)}, u32[]{:S(2)}) collective-permute-start(f32[264,128]{1,0:T(8,128)S(1)} %collective-permute-done.27.refs_13_), channel_id=1, source_target_pairs={{0,4},{4,0},{1,5},{5,1},{2,6},{6,2},{3,7},{7,3},{8,12},{12,8},{9,1... | collective-permute-start | bytes 405512 | tf_op jit(solution)/shard_map/ppermute | solution.py:495
  177.1 2.0 %collective-permute-done.29.refs_15_ = f32[264,128]{1,0:T(8,128)S(1)} collective-permute-done((f32[264,128]{1,0:T(8,128)S(1)}, f32[264,128]{1,0:T(8,128)S(1)}, u32[]{:S(2)}, u32[]{:S(2)}) %collective-permute-start.29) | collective-permute-done | bytes 135200 | tf_op jit(solution)/shard_map/ppermute | solution.py:495
  179.1 1.3 collective-permute-done.45.refs_31_
  180.4 2.9 %assemble.1 = (f32[768,1024]{1,0:T(8,128)}, f32[1024,256]{1,0:T(8,128)}, f32[8,128]{1,0:T(8,128)}, f32[8,128]{1,0:T(8,128)S(1)}) custom-call(f32[264,128]{1,0:T(8,128)S(1)} %get-tuple-element.81.refs_0_, f32[264,128]{1,0:T(8,128)S(1)} %collective-permute-done.17.refs_1_, f32[264,128]{1,0:T(8,128)S(1)} %collective-permute-done.18.refs_2_, ...), custom_call_target="tpu_custom_call" | custom-call | tf_op jit(solution)/shard_map/assemble/pallas_call | solution.py:469
  (110 shorter events, 23.1 us)
Async XLA Ops:
  7.6 59.0 %all-to-all-start = ((f32[32,136,128]{2,1,0:T(8,128)}), f32[32,136,128]{2,1,0:T(8,128)S(1)}, u32[]{:S(2)}, u32[]{:S(2)}) async-start(f32[32,136,128]{2,1,0:T(8,128)} %get-tuple-element.59), calls=%async_computation | async-start | bytes 4456448 | tf_op jit(solution)/shard_map/all_to_all | solution.py:543
  72.7 65.0 %all-to-all-start.1 = ((f32[32,64,256]{2,1,0:T(8,128)}), f32[32,64,256]{2,1,0:T(8,128)S(1)}, u32[]{:S(2)}, u32[]{:S(2)}) async-start(f32[32,64,256]{2,1,0:T(8,128)} %get-tuple-element.67), calls=%async_computation.1 | async-start | bytes 4194304 | tf_op jit(solution)/shard_map/all_to_all | solution.py:549
  92.2 7.0 %collective-permute-start.7 = (f32[4,264,128]{2,1,0:T(8,128)}, f32[4,264,128]{2,1,0:T(8,128)S(1)}, u32[]{:S(2)}, u32[]{:S(2)}) collective-permute-start(f32[4,264,128]{2,1,0:T(8,128)} %get-tuple-element.29), channel_id=1, source_target_pairs={{0,1},{1,0},{2,3},{3,2},{4,5},{5,4},{6,7},{7,6},{8,9},{9,8},{10,11... | collective-permute-start | bytes 1622024 | tf_op jit(solution)/shard_map/cond/branch_1_fun/ppermute | solution.py:495
  92.4 8.4 %collective-permute-start.11 = (f32[4,264,128]{2,1,0:T(8,128)}, f32[4,264,128]{2,1,0:T(8,128)S(1)}, u32[]{:S(2)}, u32[]{:S(2)}) collective-permute-start(f32[4,264,128]{2,1,0:T(8,128)} %get-tuple-element.31), channel_id=1, source_target_pairs={{0,1},{1,0},{2,3},{3,2},{4,5},{5,4},{6,7},{7,6},{8,9},{9,8},{10,11... | collective-permute-start | bytes 1622024 | tf_op jit(solution)/shard_map/cond/branch_1_fun/ppermute | solution.py:495
  94.8 15.6 %collective-permute-start.1 = (f32[2,264,128]{2,1,0:T(8,128)S(1)}, f32[2,264,128]{2,1,0:T(8,128)S(1)}, u32[]{:S(2)}, u32[]{:S(2)}) collective-permute-start(f32[2,264,128]{2,1,0:T(8,128)S(1)} %slice_add_fusion.6), channel_id=1, source_target_pairs={{0,2},{2,0},{1,3},{3,1},{4,6},{6,4},{5,7},{7,5},{8,10},{10,8},{9,1... | collective-permute-start | bytes 811016 | tf_op jit(solution)/shard_map/cond/branch_1_fun/ppermute | solution.py:495
  97.6 13.0 %collective-permute-start.4 = (f32[2,264,128]{2,1,0:T(8,128)S(1)}, f32[2,264,128]{2,1,0:T(8,128)S(1)}, u32[]{:S(2)}, u32[]{:S(2)}) collective-permute-start(f32[2,264,128]{2,1,0:T(8,128)S(1)} %slice_add_fusion.4), channel_id=1, source_target_pairs={{0,4},{4,0},{1,5},{5,1},{2,6},{6,2},{3,7},{7,3},{8,12},{12,8},{9,1... | collective-permute-start | bytes 811016 | tf_op jit(solution)/shard_map/cond/branch_1_fun/ppermute | solution.py:495
  100.2 15.9 %collective-permute-start.8 = (f32[2,264,128]{2,1,0:T(8,128)S(1)}, f32[2,264,128]{2,1,0:T(8,128)S(1)}, u32[]{:S(2)}, u32[]{:S(2)}) collective-permute-start(f32[2,264,128]{2,1,0:T(8,128)S(1)} %slice_add_fusion.2), channel_id=1, source_target_pairs={{0,2},{2,0},{1,3},{3,1},{4,6},{6,4},{5,7},{7,5},{8,10},{10,8},{9,1... | collective-permute-start | bytes 811016 | tf_op jit(solution)/shard_map/cond/branch_1_fun/ppermute | solution.py:495
  100.9 16.9 %collective-permute-start.12 = (f32[2,264,128]{2,1,0:T(8,128)S(1)}, f32[2,264,128]{2,1,0:T(8,128)S(1)}, u32[]{:S(2)}, u32[]{:S(2)}) collective-permute-start(f32[2,264,128]{2,1,0:T(8,128)S(1)} %slice_add_fusion), channel_id=1, source_target_pairs={{0,4},{4,0},{1,5},{5,1},{2,6},{6,2},{3,7},{7,3},{8,12},{12,8},{9,1... | collective-permute-start | bytes 811016 | tf_op jit(solution)/shard_map/cond/branch_1_fun/ppermute | solution.py:495
  110.5 17.9 %collective-permute-start.2 = (f32[264,128]{1,0:T(8,128)S(1)}, f32[264,128]{1,0:T(8,128)S(1)}, u32[]{:S(2)}, u32[]{:S(2)}) collective-permute-start(f32[264,128]{1,0:T(8,128)S(1)} %slice_bitcast_fusion.6), channel_id=1, source_target_pairs={{0,4},{4,0},{1,5},{5,1},{2,6},{6,2},{3,7},{7,3},{8,12},{12,8},{9,1... | collective-permute-start | bytes 405512 | tf_op jit(solution)/shard_map/cond/branch_1_fun/ppermute | solution.py:495
  110.7 8.7 %collective-permute-start.5 = (f32[264,128]{1,0:T(8,128)S(1)}, f32[264,128]{1,0:T(8,128)S(1)}, u32[]{:S(2)}, u32[]{:S(2)}) collective-permute-start(f32[264,128]{1,0:T(8,128)S(1)} %slice_bitcast_fusion.4), channel_id=1, source_target_pairs={{0,2},{2,0},{1,3},{3,1},{4,6},{6,4},{5,7},{7,5},{8,10},{10,8},{9,1... | collective-permute-start | bytes 405512 | tf_op jit(solution)/shard_map/cond/branch_1_fun/ppermute | solution.py:495
  116.3 9.0 %collective-permute-start.9 = (f32[264,128]{1,0:T(8,128)S(1)}, f32[264,128]{1,0:T(8,128)S(1)}, u32[]{:S(2)}, u32[]{:S(2)}) collective-permute-start(f32[264,128]{1,0:T(8,128)S(1)} %slice_bitcast_fusion.2), channel_id=1, source_target_pairs={{0,4},{4,0},{1,5},{5,1},{2,6},{6,2},{3,7},{7,3},{8,12},{12,8},{9,1... | collective-permute-start | bytes 405512 | tf_op jit(solution)/shard_map/cond/branch_1_fun/ppermute | solution.py:495
  117.9 10.3 %collective-permute-start.13 = (f32[264,128]{1,0:T(8,128)S(1)}, f32[264,128]{1,0:T(8,128)S(1)}, u32[]{:S(2)}, u32[]{:S(2)}) collective-permute-start(f32[264,128]{1,0:T(8,128)S(1)} %slice_bitcast_fusion), channel_id=1, source_target_pairs={{0,2},{2,0},{1,3},{3,1},{4,6},{6,4},{5,7},{7,5},{8,10},{10,8},{9,1... | collective-permute-start | bytes 405512 | tf_op jit(solution)/shard_map/cond/branch_1_fun/ppermute | solution.py:495
  119.4 8.9 %collective-permute-start.6 = (f32[264,128]{1,0:T(8,128)S(1)}, f32[264,128]{1,0:T(8,128)S(1)}, u32[]{:S(2)}, u32[]{:S(2)}) collective-permute-start(f32[264,128]{1,0:T(8,128)S(1)} %fusion.6), channel_id=1, source_target_pairs={{0,24},{8,0},{16,8},{24,16},{1,25},{9,1},{17,9},{25,17},{2,26},{10... | collective-permute-start | bytes 405512 | tf_op jit(solution)/shard_map/cond/branch_1_fun/ppermute | solution.py:490
  125.3 12.1 %collective-permute-start.10 = (f32[264,128]{1,0:T(8,128)S(1)}, f32[264,128]{1,0:T(8,128)S(1)}, u32[]{:S(2)}, u32[]{:S(2)}) collective-permute-start(f32[264,128]{1,0:T(8,128)S(1)} %fusion.5), channel_id=1, source_target_pairs={{0,16},{8,24},{16,0},{24,8},{1,17},{9,25},{17,1},{25,9},{2,18},{10... | collective-permute-start | bytes 405512 | tf_op jit(solution)/shard_map/cond/branch_1_fun/ppermute | solution.py:490
  128.2 9.2 %collective-permute-start.14 = (f32[264,128]{1,0:T(8,128)S(1)}, f32[264,128]{1,0:T(8,128)S(1)}, u32[]{:S(2)}, u32[]{:S(2)}) collective-permute-start(f32[264,128]{1,0:T(8,128)S(1)} %fusion.4), channel_id=1, source_target_pairs={{0,8},{8,16},{16,24},{24,0},{1,9},{9,17},{17,25},{25,1},{2,10},{10... | collective-permute-start | bytes 405512 | tf_op jit(solution)/shard_map/cond/branch_1_fun/ppermute | solution.py:490
  137.7 11.0 %collective-permute-start.23 = (f32[264,128]{1,0:T(8,128)S(1)}, f32[264,128]{1,0:T(8,128)S(1)}, u32[]{:S(2)}, u32[]{:S(2)}) collective-permute-start(f32[264,128]{1,0:T(8,128)S(1)} %get-tuple-element.81.refs_0_), channel_id=1, source_target_pairs={{0,16},{8,24},{16,0},{24,8},{1,17},{9,25},{17,1},{25,9},{2,18},{10... | collective-permute-start | bytes 405512 | tf_op jit(solution)/shard_map/ppermute | solution.py:490
  139.4 14.4 %collective-permute-start.16 = (f32[264,128]{1,0:T(8,128)S(1)}, f32[264,128]{1,0:T(8,128)S(1)}, u32[]{:S(2)}, u32[]{:S(2)}) collective-permute-start(f32[264,128]{1,0:T(8,128)S(1)} %get-tuple-element.81.refs_0_), channel_id=1, source_target_pairs={{0,8},{8,16},{16,24},{24,0},{1,9},{9,17},{17,25},{25,1},{2,10},{10... | collective-permute-start | bytes 405512 | tf_op jit(solution)/shard_map/ppermute | solution.py:490
  139.4 14.5 %collective-permute-start.15 = (f32[264,128]{1,0:T(8,128)S(1)}, f32[264,128]{1,0:T(8,128)S(1)}, u32[]{:S(2)}, u32[]{:S(2)}) collective-permute-start(f32[264,128]{1,0:T(8,128)S(1)} %get-tuple-element.81.refs_0_), channel_id=1, source_target_pairs={{0,24},{8,0},{16,8},{24,16},{1,25},{9,1},{17,9},{25,17},{2,26},{10... | collective-permute-start | bytes 405512 | tf_op jit(solution)/shard_map/ppermute | solution.py:490
  148.7 5.7 %collective-permute-start.38 = (f32[264,128]{1,0:T(8,128)S(1)}, f32[264,128]{1,0:T(8,128)S(1)}, u32[]{:S(2)}, u32[]{:S(2)}) collective-permute-start(f32[264,128]{1,0:T(8,128)S(1)} %collective-permute-done.23.refs_8_), channel_id=1, source_target_pairs={{0,1},{1,0},{2,3},{3,2},{4,5},{5,4},{6,7},{7,6},{8,9},{9,8},{10,11... | collective-permute-start | bytes 405512 | tf_op jit(solution)/shard_map/ppermute | solution.py:495
  148.7 6.6 %collective-permute-start.25 = (f32[264,128]{1,0:T(8,128)S(1)}, f32[264,128]{1,0:T(8,128)S(1)}, u32[]{:S(2)}, u32[]{:S(2)}) collective-permute-start(f32[264,128]{1,0:T(8,128)S(1)} %collective-permute-done.23.refs_8_), channel_id=1, source_target_pairs={{0,2},{2,0},{1,3},{3,1},{4,6},{6,4},{5,7},{7,5},{8,10},{10,8},{9,1... | collective-permute-start | bytes 405512 | tf_op jit(solution)/shard_map/ppermute | solution.py:495
  148.9 6.5 %collective-permute-start.24 = (f32[264,128]{1,0:T(8,128)S(1)}, f32[264,128]{1,0:T(8,128)S(1)}, u32[]{:S(2)}, u32[]{:S(2)}) collective-permute-start(f32[264,128]{1,0:T(8,128)S(1)} %collective-permute-done.23.refs_8_), channel_id=1, source_target_pairs={{0,4},{4,0},{1,5},{5,1},{2,6},{6,2},{3,7},{7,3},{8,12},{12,8},{9,1... | collective-permute-start | bytes 405512 | tf_op jit(solution)/shard_map/ppermute | solution.py:495
  153.9 6.0 %collective-permute-start.18 = (f32[264,128]{1,0:T(8,128)S(1)}, f32[264,128]{1,0:T(8,128)S(1)}, u32[]{:S(2)}, u32[]{:S(2)}) collective-permute-start(f32[264,128]{1,0:T(8,128)S(1)} %get-tuple-element.81.refs_0_), channel_id=1, source_target_pairs={{0,2},{2,0},{1,3},{3,1},{4,6},{6,4},{5,7},{7,5},{8,10},{10,8},{9,1... | collective-permute-start | bytes 405512 | tf_op jit(solution)/shard_map/ppermute | solution.py:495
  154.4 6.4 %collective-permute-start.17 = (f32[264,128]{1,0:T(8,128)S(1)}, f32[264,128]{1,0:T(8,128)S(1)}, u32[]{:S(2)}, u32[]{:S(2)}) collective-permute-start(f32[264,128]{1,0:T(8,128)S(1)} %get-tuple-element.81.refs_0_), channel_id=1, source_target_pairs={{0,4},{4,0},{1,5},{5,1},{2,6},{6,2},{3,7},{7,3},{8,12},{12,8},{9,1... | collective-permute-start | bytes 405512 | tf_op jit(solution)/shard_map/ppermute | solution.py:495
  155.3 6.4 %collective-permute-start.34 = (f32[264,128]{1,0:T(8,128)S(1)}, f32[264,128]{1,0:T(8,128)S(1)}, u32[]{:S(2)}, u32[]{:S(2)}) collective-permute-start(f32[264,128]{1,0:T(8,128)S(1)} %collective-permute-done.16.refs_4_), channel_id=1, source_target_pairs={{0,1},{1,0},{2,3},{3,2},{4,5},{5,4},{6,7},{7,6},{8,9},{9,8},{10,11... | collective-permute-start | bytes 405512 | tf_op jit(solution)/shard_map/ppermute | solution.py:495
  155.4 7.5 %collective-permute-start.21 = (f32[264,128]{1,0:T(8,128)S(1)}, f32[264,128]{1,0:T(8,128)S(1)}, u32[]{:S(2)}, u32[]{:S(2)}) collective-permute-start(f32[264,128]{1,0:T(8,128)S(1)} %collective-permute-done.16.refs_4_), channel_id=1, source_target_pairs={{0,4},{4,0},{1,5},{5,1},{2,6},{6,2},{3,7},{7,3},{8,12},{12,8},{9,1... | collective-permute-start | bytes 405512 | tf_op jit(solution)/shard_map/ppermute | solution.py:495
  158.4 5.3 %collective-permute-start.20 = (f32[264,128]{1,0:T(8,128)S(1)}, f32[264,128]{1,0:T(8,128)S(1)}, u32[]{:S(2)}, u32[]{:S(2)}) collective-permute-start(f32[264,128]{1,0:T(8,128)S(1)} %collective-permute-done.16.refs_4_), channel_id=1, source_target_pairs={{0,2},{2,0},{1,3},{3,1},{4,6},{6,4},{5,7},{7,5},{8,10},{10,8},{9,1... | collective-permute-start | bytes 405512 | tf_op jit(solution)/shard_map/ppermute | solution.py:495
  163.7 6.5 %collective-permute-start.26 = (f32[264,128]{1,0:T(8,128)S(1)}, f32[264,128]{1,0:T(8,128)S(1)}, u32[]{:S(2)}, u32[]{:S(2)}) collective-permute-start(f32[264,128]{1,0:T(8,128)S(1)} %collective-permute-done.24.refs_9_), channel_id=1, source_target_pairs={{0,2},{2,0},{1,3},{3,1},{4,6},{6,4},{5,7},{7,5},{8,10},{10,8},{9,1... | collective-permute-start | bytes 405512 | tf_op jit(solution)/shard_map/ppermute | solution.py:495
  166.7 6.2 %collective-permute-start.19 = (f32[264,128]{1,0:T(8,128)S(1)}, f32[264,128]{1,0:T(8,128)S(1)}, u32[]{:S(2)}, u32[]{:S(2)}) collective-permute-start(f32[264,128]{1,0:T(8,128)S(1)} %collective-permute-done.17.refs_1_), channel_id=1, source_target_pairs={{0,2},{2,0},{1,3},{3,1},{4,6},{6,4},{5,7},{7,5},{8,10},{10,8},{9,1... | collective-permute-start | bytes 405512 | tf_op jit(solution)/shard_map/ppermute | solution.py:495
  168.0 6.9 %collective-permute-start.36 = (f32[264,128]{1,0:T(8,128)S(1)}, f32[264,128]{1,0:T(8,128)S(1)}, u32[]{:S(2)}, u32[]{:S(2)}) collective-permute-start(f32[264,128]{1,0:T(8,128)S(1)} %collective-permute-done.21.refs_6_), channel_id=1, source_target_pairs={{0,1},{1,0},{2,3},{3,2},{4,5},{5,4},{6,7},{7,6},{8,9},{9,8},{10,11... | collective-permute-start | bytes 405512 | tf_op jit(solution)/shard_map/ppermute | solution.py:495
  170.2 6.4 %collective-permute-start.22 = (f32[264,128]{1,0:T(8,128)S(1)}, f32[264,128]{1,0:T(8,128)S(1)}, u32[]{:S(2)}, u32[]{:S(2)}) collective-permute-start(f32[264,128]{1,0:T(8,128)S(1)} %collective-permute-done.20.refs_5_), channel_id=1, source_target_pairs={{0,4},{4,0},{1,5},{5,1},{2,6},{6,2},{3,7},{7,3},{8,12},{12,8},{9,1... | collective-permute-start | bytes 405512 | tf_op jit(solution)/shard_map/ppermute | solution.py:495
  171.1 5.5 %collective-permute-start.44 = (f32[264,128]{1,0:T(8,128)S(1)}, f32[264,128]{1,0:T(8,128)S(1)}, u32[]{:S(2)}, u32[]{:S(2)}) collective-permute-start(f32[264,128]{1,0:T(8,128)S(1)} %collective-permute-done.28.refs_14_), channel_id=1, source_target_pairs={{0,1},{1,0},{2,3},{3,2},{4,5},{5,4},{6,7},{7,6},{8,9},{9,8},{10,11... | collective-permute-start | bytes 405512 | tf_op jit(solution)/shard_map/ppermute | solution.py:495
  172.9 6.1 %collective-permute-start.29 = (f32[264,128]{1,0:T(8,128)S(1)}, f32[264,128]{1,0:T(8,128)S(1)}, u32[]{:S(2)}, u32[]{:S(2)}) collective-permute-start(f32[264,128]{1,0:T(8,128)S(1)} %collective-permute-done.27.refs_13_), channel_id=1, source_target_pairs={{0,4},{4,0},{1,5},{5,1},{2,6},{6,2},{3,7},{7,3},{8,12},{12,8},{9,1... | collective-permute-start | bytes 405512 | tf_op jit(solution)/shard_map/ppermute | solution.py:495
  (25 other events, 159.1 us)
